TPU v7x, 256 devices: a whole 4x4x8 slice. The times are simulated.
256 devices in a mesh: fluid: 128 (over z, x, y_lo, core), group: 2 (over y_hi).
Axes of the slice: x: 4, y: 4 (y_hi: 2, y_lo: 2; y = y_hi * 2 + y_lo), z: 8, core: 2. Of those that a mesh axis runs over, the one named last changes fastest.
Arguments:
- populations: float32 [19, 256, 128, 128], P(None, 'fluid', 'group'), may hold values from 0.01 to 0.25
- relax_rates: float32 [19], replicated, may hold values from 0.5 to 1.9
- slab: int32 [131072, 1], P(('fluid', 'group')), may hold values from 0 to 127; in each aligned block of 512 rows (0 to 511, 512 to 1023, ...) at most 8 rows name the same one
- stencil_base: int32 [131072], P(('fluid', 'group')), may hold values from 0 to 8063, as said below
- frac: float32 [3, 131072], P(None, ('fluid', 'group')), may hold values from 0.45 to 0.55
- atom_vel: float32 [3, 131072], P(None, ('fluid', 'group')), may hold values from -2 to 2
- friction: float32 [131072], P(('fluid', 'group')), may hold values from 2 to 20
- features: bfloat16 [128, 131072], P(None, ('fluid', 'group')), may hold values from -6 to 6
- neighbors: int32 [131072, 16], P(('fluid', 'group')), may hold values from 0 to 1535
- bonds: float32 [3, 131072, 16], P(None, ('fluid', 'group')), may hold values from -3 to 3
- w_self: bfloat16 [128, 128], replicated, may hold values from -0.5 to 0.5
- w_nbr: bfloat16 [128, 128], replicated, may hold values from -0.5 to 0.5
- w_rbf: float32 [128, 16], replicated, may hold values from -1.5 to 1.5
- w_out: float32 [128], replicated, may hold values from -0.5 to 0.5
Outputs:
- new_pops: float32 [19, 256, 128, 128], P(None, 'fluid', 'group')
- atom_force: float32 [3, 131072], P(None, ('fluid', 'group'))
- new_features: bfloat16 [128, 131072], P(None, ('fluid', 'group'))
Inputs may be any that keep to these rules, and one draw needn't show every extreme that they name: In the rows of one device no slab is named by more than 8 atoms; in some such blocks one slab is named by exactly 8. `stencil_base`: each value is (z0 * 64 + x0) * 128 + y0 with z0 at most 0, x0 at most 62 and y0 below 128.
All inputs are finite; a program needn't handle non-finite values.
Results may differ from a plain program's by a relative error of at most 0.0023.
Values may be sent and summed in bfloat16 or wider, within the bound.
No kernel may reach another device: no remote copies, remote signals or barrier semaphores. Data moves between devices by JAX's collectives and lax.ppermute only.
A program may use at most 64 MiB of HBM per device.

v0:
```python
import jax
import jax.numpy as jnp
import numpy as np
from jax import lax
from jax.sharding import PartitionSpec as P

RADIAL_REACH = 4.0


def extended(value, sides, width):
    for axis, dim in sides:
        size, length = (lax.axis_size(axis), value.shape[dim])
        up = [(i, (i + 1) % size) for i in range(size)]
        down = [(j, i) for i, j in up]
        last = lax.slice_in_dim(value, length - width, length, axis=dim)
        leading = lax.slice_in_dim(value, 0, width, axis=dim)
        before = lax.ppermute(last, axis, up)
        after = lax.ppermute(leading, axis, down)
        value = jnp.concatenate([before, value, after], axis=dim)
    return value


def speed_list():
    return [
        [0, 0, 0],
        [1, 0, 0],
        [-1, 0, 0],
        [0, 1, 0],
        [0, -1, 0],
        [0, 0, 1],
        [0, 0, -1],
        [1, 1, 0],
        [-1, -1, 0],
        [1, -1, 0],
        [-1, 1, 0],
        [1, 0, 1],
        [-1, 0, -1],
        [1, 0, -1],
        [-1, 0, 1],
        [0, 1, 1],
        [0, -1, -1],
        [0, 1, -1],
        [0, -1, 1],
    ]


def lattice_weights():
    return [1.0 / 3.0] + [1.0 / 18.0] * 6 + [1.0 / 36.0] * 12


def moment_table():
    tables = []
    for speed in speed_list():
        along_x = float(speed[0])
        along_y = float(speed[1])
        along_z = float(speed[2])
        tables.append(
            [
                1.0,
                along_x,
                along_y,
                along_z,
                along_x * along_y,
                along_x * along_z,
                along_y * along_z,
                along_x * along_x,
                along_y * along_y,
                along_z * along_z,
                along_x * along_y * along_y,
                along_x * along_z * along_z,
                along_x * along_x * along_y,
                along_x * along_x * along_z,
                along_y * along_y * along_z,
                along_y * along_z * along_z,
                along_x * along_x * along_y * along_y,
                along_x * along_x * along_z * along_z,
                along_y * along_y * along_z * along_z,
            ]
        )
    return [[tables[column][moment] for column in range(19)] for moment in range(19)]


def invert_rows(matrix):
    order = len(matrix)
    joined = [
        list(matrix[place]) + [1.0 if other == place else 0.0 for other in range(order)]
        for place in range(order)
    ]
    for column in range(order):
        pivot_place = max(range(column, order), key=lambda place: abs(joined[place][column]))
        joined[column], joined[pivot_place] = (joined[pivot_place], joined[column])
        pivot = joined[column][column]
        joined[column] = [entry / pivot for entry in joined[column]]
        for place in range(order):
            if place != column:
                factor = joined[place][column]
                if factor != 0.0:
                    joined[place] = [
                        entry - factor * upper
                        for entry, upper in zip(joined[place], joined[column])
                    ]
    return [joined[place][order:] for place in range(order)]


def moment_inverse():
    return invert_rows(moment_table())


def fluid_moments(pops):
    lattice = jnp.asarray(np.array(speed_list()).T, jnp.float32)
    density = jnp.sum(pops, axis=0)
    velocity = jnp.dot(lattice, pops, precision=lax.Precision.HIGHEST) / density
    return (density, velocity)


def collide(pops, density, velocity, force, rates):
    lattice = jnp.asarray(np.array(speed_list()), jnp.float32)
    weights = jnp.asarray(np.array(lattice_weights()), jnp.float32)[:, None]
    along = jnp.dot(lattice, velocity, precision=lax.Precision.HIGHEST)
    speed_sq = jnp.sum(velocity * velocity, axis=0)
    equilibrium = weights * density * (1.0 + 3.0 * along + 4.5 * along * along - 1.5 * speed_sq)
    moments = jnp.dot(
        jnp.asarray(moment_table(), jnp.float32),
        pops - equilibrium,
        precision=lax.Precision.HIGHEST,
    )
    inverse = jnp.asarray(moment_inverse(), jnp.float32)
    relaxed = jnp.dot(inverse, rates[:, None] * moments, precision=lax.Precision.HIGHEST)
    forcing = jnp.dot(inverse[:, 1:4], force, precision=lax.Precision.HIGHEST)
    return pops - relaxed + forcing


def stencil(plane, column, row, frac, width, depth):
    nodes = []
    weights = []
    for lift_z in (0, 1):
        for lift_x in (0, 1):
            for lift_y in (0, 1):
                node = ((plane + lift_z) * width + column + lift_x) * depth + (row + lift_y) % depth
                factor_x = frac[0] if lift_x else 1.0 - frac[0]
                factor_y = frac[1] if lift_y else 1.0 - frac[1]
                factor_z = frac[2] if lift_z else 1.0 - frac[2]
                nodes.append(node.astype(jnp.int32))
                weights.append(factor_x * factor_y * factor_z)
    return (jnp.stack(nodes), jnp.stack(weights))


def interpolate(velocity, nodes, weights):
    return jnp.sum(weights[None] * velocity[:, nodes], axis=1)


def spread(drag, nodes, weights, cells):
    terms = (-weights[None] * drag[:, None, :]).reshape(3, -1)
    return jnp.zeros((3, cells), jnp.float32).at[:, nodes.reshape(-1)].add(terms)


def potential(window, own, nbrs, bonds, w_self, w_nbr, w_rbf, w_out):
    own_proj = jnp.dot(w_self, own, preferred_element_type=jnp.float32)
    projected = jnp.dot(w_nbr, window, preferred_element_type=jnp.float32).astype(jnp.bfloat16)
    picked = projected[:, nbrs.reshape(-1)].reshape(own.shape[0], nbrs.shape[0], nbrs.shape[1])
    length = jnp.sqrt(jnp.sum(bonds * bonds, axis=0) + 1e-06)
    basis = w_rbf.shape[1]
    spacing = RADIAL_REACH / (basis - 1)
    centers = jnp.arange(basis).astype(jnp.float32) * spacing
    scaled = (length[None] - centers[:, None, None]) / spacing
    radial = jnp.exp(-scaled * scaled)
    edge = jnp.einsum("fr,rak->fak", w_rbf, radial, precision=lax.Precision.HIGHEST)
    hidden = jax.nn.silu(own_proj[:, :, None] + picked.astype(jnp.float32) + edge)
    scalar = jnp.einsum("f,fak->ak", w_out, hidden, precision=lax.Precision.HIGHEST)
    force = jnp.einsum("ak,cak->ca", scalar, bonds, precision=lax.Precision.HIGHEST)
    updated = (own.astype(jnp.float32) + jnp.mean(hidden, axis=2)).astype(jnp.bfloat16)
    return (force, updated)


def body(
    populations,
    relax_rates,
    slab,
    stencil_base,
    frac,
    atom_vel,
    friction,
    features,
    neighbors,
    bonds,
    w_self,
    w_nbr,
    w_rbf,
    w_out,
):
    speeds = speed_list()
    planes = populations.shape[1]
    width = populations.shape[2]
    depth = populations.shape[3]
    cells = planes * width * depth
    flat = populations.reshape(19, cells)
    density, velocity = fluid_moments(flat)
    atoms = slab.shape[0]
    slabs = lax.axis_size("fluid")
    capacity = max(2, 2 * atoms // slabs)
    target = slab[:, 0]
    chosen = (target[:, None] == jnp.arange(slabs, dtype=jnp.int32)[None, :]).astype(jnp.int32)
    places = jnp.sum((jnp.cumsum(chosen, axis=0) - 1) * chosen, axis=1)
    payload = jnp.concatenate([frac, atom_vel, friction[None, :]], axis=0)
    outgoing = jnp.zeros((slabs, 7, capacity), jnp.float32).at[target, :, places].set(payload.T)
    out_base = jnp.zeros((slabs, capacity), jnp.int32).at[target, places].set(stencil_base)
    incoming, in_base = (
        lax.all_to_all(outgoing, "fluid", split_axis=0, concat_axis=0, tiled=True),
        lax.all_to_all(out_base, "fluid", split_axis=0, concat_axis=0, tiled=True),
    )
    slots = slabs * capacity
    received = incoming.transpose(1, 0, 2).reshape(7, slots)
    bases = in_base.reshape(slots)
    nodes, weights = stencil(
        bases // (depth * width), bases // depth % width, bases % depth, received[0:3], width, depth
    )
    drag = received[6] * (interpolate(velocity, nodes, weights) - received[3:6])
    force_field = spread(drag, nodes, weights, cells)
    returned = lax.all_to_all(
        drag.reshape(3, slabs, capacity).transpose(1, 0, 2),
        "fluid",
        split_axis=0,
        concat_axis=0,
        tiled=True,
    )
    atom_drag = returned[target, :, places].T
    post = collide(flat, density, velocity, force_field, relax_rates).reshape(
        19, planes, width, depth
    )
    padded = extended(post, (("fluid", 1), ("group", 2)), 1)
    moved = []
    for number in range(19):
        shift_x = speeds[number][0]
        shift_y = speeds[number][1]
        shift_z = speeds[number][2]
        window = padded[
            number, 1 - shift_z : 1 - shift_z + planes, 1 - shift_x : 1 - shift_x + width
        ]
        moved.append(jnp.roll(window, shift_y, axis=2))
    new_pops = jnp.stack(moved)
    window_feats = extended(features, (("fluid", 1),), atoms)
    conservative, updated = potential(
        window_feats, features, neighbors, bonds, w_self, w_nbr, w_rbf, w_out
    )
    return (new_pops, conservative + atom_drag, updated)


def solution(mesh):
    in_specs = (
        P(None, "fluid", "group", None),
        P(),
        P(("fluid", "group"), None),
        P(("fluid", "group")),
        P(None, ("fluid", "group")),
        P(None, ("fluid", "group")),
        P(("fluid", "group")),
        P(None, ("fluid", "group")),
        P(("fluid", "group"), None),
        P(None, ("fluid", "group"), None),
        P(),
        P(),
        P(),
        P(),
    )
    out_specs = (
        P(None, "fluid", "group", None),
        P(None, ("fluid", "group")),
        P(None, ("fluid", "group")),
    )
    return jax.shard_map(body, mesh=mesh, in_specs=in_specs, out_specs=out_specs, check_vma=False)
```

profile of v0, /device:TPU:16, one launch (start us, length us, event | category | flops | bytes accessed | tf_op | source)
XLA Modules:
  0.0 321.9 jit_solution(8139677804803743998)
XLA Ops:
  0.7 8.3 %collective-permute-start.5 = (bf16[128,512]{1,0:T(8,128)(2,1)}, bf16[128,512]{1,0:T(8,128)(2,1)}, u32[]{:S(2)}, u32[]{:S(2)}) collective-permute-start(bf16[128,512]{1,0:T(8,128)(2,1)} %param.26), channel_id=1, source_target_pairs={{2,0},{4,2},{6,4},{8,6},{10,8},{12,10},{14,12},{16,14},{18,16},{20... | collective-permute-start | bytes 393224 | tf_op jit(solution)/shard_map/ppermute | solution.py:18
  11.1 22.0 %scatter_fusion = s32[128,8]{0,1:T(8,128)S(1)} fusion(s32[128,8]{0,1:T(8,128)S(1)} %broadcast_in_dim.9, s32[512]{0:T(512)S(1)} %bitcast.190, s32[512]{0:T(512)S(1)} %copy-done.24), kind=kCustom, calls=%fused_computation.3 | custom fusion | bytes 10240 | tf_op jit(solution)/shard_map/scatter | solution.py:206
  33.8 10.1 %all-to-all-start = ((s32[128,1,8]{2,1,0:T(1,128)}), s32[128,1,8]{2,1,0:T(1,128)S(1)}, u32[]{:S(2)}, u32[]{:S(2)}) async-start(s32[128,1,8]{2,1,0:T(1,128)} %copy.40), calls=%async_computation | async-start | bytes 131072 | tf_op jit(solution)/shard_map/all_to_all | solution.py:209
  48.2 1.4 fusion.74
  49.6 2.1 convolution_multiply_fusion
  51.8 1.5 convolution_subtract_fusion
  53.4 1.4 copy.56
  54.8 5.0 %copy.42 = f32[3,16384]{0,1:T(8,128)} copy(f32[3,16384]{1,0:T(4,128)S(1)} %get-tuple-element.85) | data formatting | bytes 393216 | tf_op jit(solution)/shard_map/div | solution.py:112
  60.8 54.2 %scatter_fusion.1 = f32[128,7,8]{1,2,0:T(8,128)} fusion(f32[128,7,8]{1,2,0:T(8,128)} %broadcast_in_dim.10, s32[512]{0:T(512)S(1)} %bitcast.191, f32[512,7]{1,0:T(8,128)S(1)} %copy.41), kind=kCustom, calls=%fused_computation.4 | custom fusion | bytes 47104 | tf_op jit(solution)/shard_map/scatter | solution.py:205
  115.1 12.5 %all-to-all-start.1 = ((f32[128,7,8]{1,2,0:T(8,128)}), f32[128,7,8]{1,2,0:T(8,128)S(1)}, u32[]{:S(2)}, u32[]{:S(2)}) async-start(f32[128,7,8]{1,2,0:T(8,128)} %scatter_fusion.1), calls=%async_computation.1 | async-start | bytes 1048576 | tf_op jit(solution)/shard_map/all_to_all | solution.py:208
  130.1 31.2 %gather_fusion = f32[8192,3]{1,0:T(8,128)} fusion(f32[3,16384]{0,1:T(8,128)} %copy.42, s32[8192]{0:T(1024)S(1)} %broadcast_clamp_fusion.1), kind=kCustom, calls=%fused_computation | custom fusion | bytes 229376 | tf_op jit(solution)/shard_map/gather | solution.py:149
  164.6 2.9 multiply_reduce_fusion
  168.2 1.5 copy.48
  169.7 12.3 %all-to-all-start.2 = ((f32[128,3,8]{2,1,0:T(4,128)}), f32[128,3,8]{2,1,0:T(4,128)S(1)}, u32[]{:S(2)}, u32[]{:S(2)}) async-start(f32[128,3,8]{2,1,0:T(4,128)} %copy.48), calls=%async_computation.2 | async-start | bytes 524288 | tf_op jit(solution)/shard_map/all_to_all | solution.py:219
  182.1 2.6 bitcast_multiply_fusion
  184.7 44.2 %scatter_custom_fusion.2 = f32[3,16384]{0,1:T(8,128)} fusion(s32[8192]{0:T(1024)} %bitcast.230, f32[3,8192]{0,1:T(8,128)} %bitcast_multiply_fusion, f32[]{:T(128)} %constant.113.clone.1), kind=kCustom, calls=%fused_computation.11 | custom fusion | flops 24576 | bytes 4391424 | tf_op jit(solution)/shard_map/scatter-add | solution.py:154
  228.9 9.3 %convolution_add_fusion = f32[19,16384]{1,0:T(8,128)S(1)} fusion(f32[19,16384]{1,0:T(8,128)S(1)} %convolution_subtract_fusion, f32[19,3]{1,0:T(8,128)S(1)} %copy-done.18, f32[3,16384]{0,1:T(8,128)} %scatter_custom_fusion.2), kind=kOutput, calls=%fused_computation.6 | convolution fusion | flops 11517952 | bytes 2687204 | tf_op jit(solution)/shard_map/dot_general | solution.py:129
  239.8 1.1 fusion.72
  242.4 5.9 %collective-permute-start.1 = (f32[19,1,64,128]{3,2,1,0:T(8,128)}, f32[19,1,64,128]{3,2,1,0:T(8,128)}, u32[]{:S(2)}, u32[]{:S(2)}) collective-permute-start(f32[19,1,64,128]{3,2,1,0:T(8,128)} %get-tuple-element.61), channel_id=1, source_target_pairs={{2,0},{4,2},{6,4},{8,6},{10,8},{12,10},{14,12},{16,14},{18,16},{20... | collective-permute-start | bytes 1867784 | tf_op jit(solution)/shard_map/ppermute | solution.py:18
  249.1 2.6 gather_fusion.2
  251.8 1.3 fusion.3
  253.1 24.2 %gather_fusion.1 = bf16[8192,128]{1,0:T(8,128)(2,1)S(1)} fusion(bf16[128,1536]{0,1:T(8,128)(2,1)S(1)} %fusion.3, s32[8192]{0:T(1024)S(1)} %broadcast_clamp_fusion), kind=kCustom, calls=%fused_computation.1 | custom fusion | bytes 4227072 | tf_op jit(solution)/shard_map/gather | solution.py:160
  278.3 9.0 %fusion.73 = (f32[128,512]{0,1:T(8,128)}, f32[128,512,16]{0,1,2:T(8,128)S(1)}) fusion(f32[128,16]{0,1:T(8,128)S(1)} %copy-done.29, f32[16]{0:T(128)S(1)} %convert_multiply_fusion, f32[512,16]{0,1:T(8,128)S(1)} %copy-done.15, f32[128,512,16]{0,2,1:T(8,128)S(1)} %bitcast.206, f32[128,512]{0,1:T(8,128)S(1)} %copy-done.12), kind=kOutput, calls=%fused_computation.207 | convolution fusion | flops 209125376 | bytes 8953920 | tf_op jit(solution)/shard_map/fr,rak->fak/dot_general | solution.py:167
  287.3 3.6 %fusion.42 = f32[1,512,16]{1,0,2:T(1,128)S(1)} fusion(f32[128,512,16]{0,1,2:T(8,128)S(1)} %get-tuple-element.87, f32[128]{0:T(128)S(1)} %copy-done.27), kind=kOutput, calls=%fused_computation.175 | convolution fusion | flops 12582912 | bytes 4227584 | tf_op jit(solution)/shard_map/f,fak->ak/dot_general | solution.py:169
  291.1 3.8 %fusion.76 = f32[512,1,3]{2,1,0:T(1,128)S(1)} fusion(f32[512,16,1]{1,2,0:T(1,128)S(1)} %bitcast.223, f32[3,512,16]{2,0,1:T(4,128)S(1)} %copy-done.6), kind=kOutput, calls=%fused_computation.210 | convolution fusion | flops 294912 | bytes 137216 | tf_op jit(solution)/shard_map/ak,cak->ca/dot_general | solution.py:170
  295.0 1.2 constant_dynamic-update-slice_fusion.12
  296.8 1.7 constant_dynamic-update-slice_fusion.13
  298.6 1.2 copy-done.5
  302.0 3.0 collective-permute-start.3
  306.2 1.3 collective-permute-done.3
  309.6 1.5 slice_bitcast_fusion
  311.1 1.5 slice_bitcast_fusion.1
  (172 shorter events, 34.3 us)
Async XLA Ops:
  0.6 251.2 %copy-start = (bf16[128,128]{1,0:T(8,128)(2,1)S(1)}, bf16[128,128]{1,0:T(8,128)(2,1)}, u32[]{:S(2)}) copy-start(bf16[128,128]{1,0:T(8,128)(2,1)} %param.30) | copy-start | bytes 98308
  0.6 10.4 %copy-start.17 = (s32[512,1]{0,1:T(1,128)S(1)}, s32[512,1]{0,1:T(1,128)}, u32[]{:S(2)}) copy-start(s32[512,1]{0,1:T(1,128)} %param.21) | copy-start | bytes 6148
  0.7 10.4 %copy-start.24 = (s32[512]{0:T(512)S(1)}, s32[512]{0:T(512)}, u32[]{:S(2)}) copy-start(s32[512]{0:T(512)} %param.22) | copy-start | bytes 6148
  0.7 251.1 %collective-permute-start.5 = (bf16[128,512]{1,0:T(8,128)(2,1)}, bf16[128,512]{1,0:T(8,128)(2,1)}, u32[]{:S(2)}, u32[]{:S(2)}) collective-permute-start(bf16[128,512]{1,0:T(8,128)(2,1)} %param.26), channel_id=1, source_target_pairs={{2,0},{4,2},{6,4},{8,6},{10,8},{12,10},{14,12},{16,14},{18,16},{20... | collective-permute-start | bytes 393224 | tf_op jit(solution)/shard_map/ppermute | solution.py:18
  9.0 242.8 %collective-permute-start.4 = (bf16[128,512]{1,0:T(8,128)(2,1)}, bf16[128,512]{1,0:T(8,128)(2,1)}, u32[]{:S(2)}, u32[]{:S(2)}) collective-permute-start(bf16[128,512]{1,0:T(8,128)(2,1)} %param.26), channel_id=1, source_target_pairs={{0,2},{2,4},{4,6},{6,8},{8,10},{10,12},{12,14},{14,16},{16,18},{18... | collective-permute-start | bytes 393224 | tf_op jit(solution)/shard_map/ppermute | solution.py:17
  11.1 32.9 %copy-start.8 = (f32[3,512,16]{1,2,0:T(8,128)S(1)}, f32[3,512,16]{1,2,0:T(8,128)}, u32[]{:S(2)}) copy-start(f32[3,512,16]{1,2,0:T(8,128)} %param.28) | copy-start | bytes 294916
  11.1 33.5 %copy-start.14 = (s32[512,16]{0,1:T(8,128)S(1)}, s32[512,16]{0,1:T(8,128)}, u32[]{:S(2)}) copy-start(s32[512,16]{0,1:T(8,128)} %param.27) | copy-start | bytes 98308
  11.1 33.9 %copy-start.7 = (bf16[128,512]{1,0:T(8,128)(2,1)S(1)}, bf16[128,512]{1,0:T(8,128)(2,1)}, u32[]{:S(2)}) copy-start(bf16[128,512]{1,0:T(8,128)(2,1)} %param.26) | copy-start | bytes 393220
  11.1 33.9 %copy-start.16 = (bf16[128,128]{1,0:T(8,128)(2,1)S(1)}, bf16[128,128]{1,0:T(8,128)(2,1)}, u32[]{:S(2)}) copy-start(bf16[128,128]{1,0:T(8,128)(2,1)} %param.29) | copy-start | bytes 98308
  33.1 12.8 %copy-start.4 = (f32[19,2,64,128]{3,2,1,0:T(8,128)S(1)}, f32[19,2,64,128]{3,2,1,0:T(8,128)}, u32[]{:S(2)}) copy-start(f32[19,2,64,128]{3,2,1,0:T(8,128)} %param.19) | copy-start | bytes 3735556
  33.8 81.2 %all-to-all-start = ((s32[128,1,8]{2,1,0:T(1,128)}), s32[128,1,8]{2,1,0:T(1,128)S(1)}, u32[]{:S(2)}, u32[]{:S(2)}) async-start(s32[128,1,8]{2,1,0:T(1,128)} %copy.40), calls=%async_computation | async-start | bytes 131072 | tf_op jit(solution)/shard_map/all_to_all | solution.py:209
  47.1 2.5 copy-start.19
  47.1 2.5 copy-start.26
  47.1 2.5 copy-start.28
  49.6 2.1 copy-start.21
  51.7 1.5 copy-start.22
  51.7 1.5 copy-start.23
  51.7 1.5 copy-start.25
  115.1 46.2 %all-to-all-start.1 = ((f32[128,7,8]{1,2,0:T(8,128)}), f32[128,7,8]{1,2,0:T(8,128)S(1)}, u32[]{:S(2)}, u32[]{:S(2)}) async-start(f32[128,7,8]{1,2,0:T(8,128)} %scatter_fusion.1), calls=%async_computation.1 | async-start | bytes 1048576 | tf_op jit(solution)/shard_map/all_to_all | solution.py:208
  167.9 14.2 %copy-start.13 = (f32[1,8,8,128]{3,1,2,0:T(8,128)S(1)}, f32[1,8,8,128]{3,1,2,0:T(8,128)}, u32[]{:S(2)}) copy-start(f32[1,8,8,128]{3,1,2,0:T(8,128)} %copy.69) | copy-start | bytes 98308
  169.7 78.6 %all-to-all-start.2 = ((f32[128,3,8]{2,1,0:T(4,128)}), f32[128,3,8]{2,1,0:T(4,128)S(1)}, u32[]{:S(2)}, u32[]{:S(2)}) async-start(f32[128,3,8]{2,1,0:T(4,128)} %copy.48), calls=%async_computation.2 | async-start | bytes 524288 | tf_op jit(solution)/shard_map/all_to_all | solution.py:219
  184.7 44.2 %copy-start.18 = (f32[19,3]{1,0:T(8,128)S(1)}, f32[19,3]{1,0:T(8,128)}, u32[]{:S(2)}) copy-start(f32[19,3]{1,0:T(8,128)} %constant.141) | copy-start | bytes 688
  242.4 54.4 %collective-permute-start.1 = (f32[19,1,64,128]{3,2,1,0:T(8,128)}, f32[19,1,64,128]{3,2,1,0:T(8,128)}, u32[]{:S(2)}, u32[]{:S(2)}) collective-permute-start(f32[19,1,64,128]{3,2,1,0:T(8,128)} %get-tuple-element.61), channel_id=1, source_target_pairs={{2,0},{4,2},{6,4},{8,6},{10,8},{12,10},{14,12},{16,14},{18,16},{20... | collective-permute-start | bytes 1867784 | tf_op jit(solution)/shard_map/ppermute | solution.py:18
  248.3 46.7 %collective-permute-start = (f32[19,1,64,128]{3,2,1,0:T(8,128)}, f32[19,1,64,128]{3,2,1,0:T(8,128)}, u32[]{:S(2)}, u32[]{:S(2)}) collective-permute-start(f32[19,1,64,128]{3,2,1,0:T(8,128)} %get-tuple-element.62), channel_id=1, source_target_pairs={{0,2},{2,4},{4,6},{6,8},{8,10},{10,12},{12,14},{14,16},{16,18},{18... | collective-permute-start | bytes 1867784 | tf_op jit(solution)/shard_map/ppermute | solution.py:17
  278.3 9.0 %copy-start.27 = (f32[128]{0:T(128)S(1)}, f32[128]{0:T(128)}, u32[]{:S(2)}) copy-start(f32[128]{0:T(128)} %param.32) | copy-start | bytes 1540
  287.3 3.8 %copy-start.6 = (f32[3,512,16]{2,0,1:T(4,128)S(1)}, f32[3,512,16]{2,0,1:T(4,128)}, u32[]{:S(2)}) copy-start(f32[3,512,16]{2,0,1:T(4,128)} %copy.56) | copy-start | bytes 294916
  296.8 3.7 %copy-start.9 = (f32[19,3,64,128]{3,2,1,0:T(8,128)}, f32[19,3,64,128]{3,2,1,0:T(8,128)S(1)}, u32[]{:S(2)}) copy-start(f32[19,3,64,128]{3,2,1,0:T(8,128)S(1)} %get-tuple-element.59) | copy-start | bytes 5603332
  296.8 3.7 %copy-start.11 = (f32[128,512]{0,1:T(8,128)S(1)}, f32[128,512]{0,1:T(8,128)}, u32[]{:S(2)}) copy-start(f32[128,512]{0,1:T(8,128)} %get-tuple-element.86) | copy-start | bytes 786436
  299.8 5.6 %collective-permute-start.2 = (f32[19,4,1,128]{3,2,1,0:T(1,128)S(1)}, f32[19,4,1,128]{3,2,1,0:T(1,128)S(1)}, u32[]{:S(2)}, u32[]{:S(2)}) collective-permute-start(f32[19,4,1,128]{3,2,1,0:T(1,128)S(1)} %get-tuple-element.48), channel_id=1, source_target_pairs={{0,1},{1,0},{2,3},{3,2},{4,5},{5,4},{6,7},{7,6},{8,9},{9,8},{10,11... | collective-permute-start | bytes 116744 | tf_op jit(solution)/shard_map/ppermute | solution.py:17
  302.0 5.5 %collective-permute-start.3 = (f32[19,4,1,128]{3,2,1,0:T(1,128)S(1)}, f32[19,4,1,128]{3,2,1,0:T(1,128)S(1)}, u32[]{:S(2)}, u32[]{:S(2)}) collective-permute-start(f32[19,4,1,128]{3,2,1,0:T(1,128)S(1)} %get-tuple-element.47), channel_id=1, source_target_pairs={{1,0},{0,1},{3,2},{2,3},{5,4},{4,5},{7,6},{6,7},{9,8},{8,9},{11,10... | collective-permute-start | bytes 116744 | tf_op jit(solution)/shard_map/ppermute | solution.py:18
  306.1 2.1 copy-start.10
  317.3 4.1 %copy-start.1 = (bf16[128,128]{1,0:T(8,128)(2,1)S(1)}, bf16[128,128]{1,0:T(8,128)(2,1)}, u32[]{:S(2)}) copy-start(bf16[128,128]{1,0:T(8,128)(2,1)} %param.30) | copy-start | bytes 98308
  (8 other events, 8.7 us)
where the time goes:
time: 328 us; the launch traced here: 322 us
  local copies, waits for them, and re-layouts  166 us (51%)
  other arithmetic  65.5 us (20%)
  starting transfers between devices  52.8 us (16%)
  matrix products  33.9 us (10%)
    scatter x1, local copies, waits for them, and re-layouts, body(): jnp.zeros((slabs, 7, capacity), jnp.float32).at[target, :, places]  54.2 us
    scatter-add x1, other arithmetic, spread(): jnp.zeros((3, cells), jnp.float32).at[:, nodes.reshape(-1)].add(terms)  44.2 us
    gather x1, local copies, waits for them, and re-layouts, interpolate(): return jnp.sum(weights[None] * velocity[:, nodes], axis=1)  31.2 us
    gather x1, local copies, waits for them, and re-layouts, potential(): projected[:, nbrs.reshape(-1)]  24.2 us
    scatter x1, local copies, waits for them, and re-layouts, body(): jnp.zeros((slabs, capacity), jnp.int32).at[target, places].set(stencil_base)  22 us
    ppermute x3, starting transfers between devices, extended(): after = lax.ppermute(leading, axis, down)  17.2 us
    all_to_all x1, starting transfers between devices, body(): lax.all_to_all(outgoing, 'fluid', split_axis=0, concat_axis=0, tiled=True)  12.5 us
    all_to_all x1, starting transfers between devices, body(): lax.all_to_all(drag.reshape(3, slabs, capacity).transpose(1, 0, 2), 'flui...  12.3 us
  transfers between devices with their start and end apart: 9, of which 2 were waited for; matrix products, arithmetic and copies ran while one was open for 77% of the time, Pallas kernels for 0%

commit v1 on v0

v1 whole, which is shorter than its diff:
```python
import functools

import jax
import jax.numpy as jnp
from jax import lax
from jax.experimental import pallas as pl
from jax.experimental.pallas import tpu as pltpu
from jax.sharding import PartitionSpec as P

F32 = jnp.float32
BF16 = jnp.bfloat16
I32 = jnp.int32

RADIAL_REACH = 4.0
SLOTS = 8

SPEEDS = (
    (0, 0, 0),
    (1, 0, 0),
    (-1, 0, 0),
    (0, 1, 0),
    (0, -1, 0),
    (0, 0, 1),
    (0, 0, -1),
    (1, 1, 0),
    (-1, -1, 0),
    (1, -1, 0),
    (-1, 1, 0),
    (1, 0, 1),
    (-1, 0, -1),
    (1, 0, -1),
    (-1, 0, 1),
    (0, 1, 1),
    (0, -1, -1),
    (0, 1, -1),
    (0, -1, 1),
)
RISING = (11, 14, 15, 18)
FALLING = (12, 13, 16, 17)
FLAT = (0, 7, 8, 9, 10)
CALM = (0, 7, 8, 9, 10, 11, 12, 13, 14, 15, 16, 17, 18)

VMEM_LIMIT = 48 * 1024 * 1024


def halves(value):
    high = value.astype(BF16)
    low = (value - high.astype(F32)).astype(BF16)
    return high, low


def thirds(value):
    high = value.astype(BF16)
    rest = value - high.astype(F32)
    middle = rest.astype(BF16)
    low = (rest - middle.astype(F32)).astype(BF16)
    return high, middle, low


def mm(a, b):
    return jnp.dot(a, b, preferred_element_type=F32)


def mm_nt(a, b):
    return lax.dot_general(a, b, (((1,), (1,)), ((), ())), preferred_element_type=F32)


def iota(shape, dim):
    return lax.broadcasted_iota(I32, shape, dim)


def pack_kernel(slab_ref, base_ref, frac_ref, vel_ref, fric_ref, out_ref, rank_ref):
    atoms = slab_ref.shape[1]
    slabs = out_ref.shape[0]
    named = iota((slabs, atoms), 0) == slab_ref[...]
    one_hot = jnp.where(named, 1.0, 0.0)
    one_hot_b = one_hot.astype(BF16)
    earlier = jnp.where(iota((atoms, atoms), 0) < iota((atoms, atoms), 1), 1.0, 0.0).astype(BF16)
    before = mm(one_hot_b, earlier)
    rank = jnp.sum(one_hot * before, axis=0, keepdims=True)
    rank_ref[...] = rank
    mine = iota((SLOTS, atoms), 0).astype(F32) == rank
    rows = [frac_ref[c : c + 1, :] for c in range(3)]
    rows += [vel_ref[c : c + 1, :] for c in range(3)]
    rows += [fric_ref[...], base_ref[...].astype(F32)]
    spread = [jnp.where(mine, row, 0.0) for row in rows]
    spread.append(jnp.zeros((128 - SLOTS * len(rows), atoms), F32))
    high, middle, low = thirds(jnp.concatenate(spread, axis=0))
    out_ref[...] = mm_nt(one_hot_b, high) + (mm_nt(one_hot_b, middle) + mm_nt(one_hot_b, low))


def pack(slab, base, frac, vel, fric, slabs):
    atoms = slab.shape[1]
    return pl.pallas_call(
        pack_kernel,
        out_shape=(
            jax.ShapeDtypeStruct((slabs, 128), F32),
            jax.ShapeDtypeStruct((1, atoms), F32),
        ),
        name="pack",
        compiler_params=pltpu.CompilerParams(vmem_limit_bytes=VMEM_LIMIT),
        cost_estimate=pl.CostEstimate(flops=400_000_000, bytes_accessed=4_000_000, transcendentals=0),
    )(slab, base, frac, vel, fric)


def moments_of(d):
    m = [None] * 19
    quad = {}
    for name, (pp, nn, pn, np_) in dict(xy=(7, 8, 9, 10), xz=(11, 12, 13, 14), yz=(15, 16, 17, 18)).items():
        same, cross = d[pp] + d[nn], d[pn] + d[np_]
        odd_same, odd_cross = d[pp] - d[nn], d[pn] - d[np_]
        quad[name] = (same + cross, same - cross, odd_same + odd_cross, odd_same - odd_cross)
    sxy, m[4], m[10], m[12] = quad["xy"]
    sxz, m[5], m[11], m[13] = quad["xz"]
    syz, m[6], m[15], m[14] = quad["yz"]
    m[16], m[17], m[18] = sxy, sxz, syz
    ax, ay, az = d[1] + d[2], d[3] + d[4], d[5] + d[6]
    m[0] = (d[0] + ax) + (ay + az) + (sxy + (sxz + syz))
    m[1] = (d[1] - d[2]) + (m[10] + m[11])
    m[2] = (d[3] - d[4]) + (m[12] + m[15])
    m[3] = (d[5] - d[6]) + (m[13] + m[14])
    m[7] = ax + (sxy + sxz)
    m[8] = ay + (sxy + syz)
    m[9] = az + (sxz + syz)
    return m


def populations_of(m):
    f = [None] * 19
    for (pp, nn, pn, np_), (s, c, first, second) in (
        ((7, 8, 9, 10), (m[16], m[4], m[10], m[12])),
        ((11, 12, 13, 14), (m[17], m[5], m[11], m[13])),
        ((15, 16, 17, 18), (m[18], m[6], m[15], m[14])),
    ):
        same, cross = 0.25 * (s + c), 0.25 * (s - c)
        odd_same, odd_cross = 0.25 * (first + second), 0.25 * (first - second)
        f[pp], f[nn] = same + odd_same, same - odd_same
        f[pn], f[np_] = cross + odd_cross, cross - odd_cross
    for plus, minus, square, line, squares, lines in (
        (1, 2, m[7], m[1], (m[16], m[17]), (m[10], m[11])),
        (3, 4, m[8], m[2], (m[16], m[18]), (m[12], m[15])),
        (5, 6, m[9], m[3], (m[17], m[18]), (m[13], m[14])),
    ):
        even = 0.5 * (square - (squares[0] + squares[1]))
        odd = 0.5 * (line - (lines[0] + lines[1]))
        f[plus], f[minus] = even + odd, even - odd
    f[0] = m[0] - (m[7] + (m[8] + m[9])) + (m[16] + (m[17] + m[18]))
    return f


def equilibrium_of(density, u):
    ux, uy, uz = u
    rest = 1.0 - 1.5 * (ux * ux + uy * uy + uz * uz)
    eq = [None] * 19
    eq[0] = (1.0 / 3.0) * density * rest
    scale_axis, scale_diagonal = (1.0 / 18.0) * density, (1.0 / 36.0) * density
    for plus, minus, along, scale in (
        (1, 2, ux, scale_axis),
        (3, 4, uy, scale_axis),
        (5, 6, uz, scale_axis),
        (7, 8, ux + uy, scale_diagonal),
        (9, 10, ux - uy, scale_diagonal),
        (11, 12, ux + uz, scale_diagonal),
        (13, 14, ux - uz, scale_diagonal),
        (15, 16, uy + uz, scale_diagonal),
        (17, 18, uy - uz, scale_diagonal),
    ):
        even = rest + 4.5 * along * along
        odd = 3.0 * along
        eq[plus], eq[minus] = scale * (even + odd), scale * (even - odd)
    return eq


def shifted(plane, number):
    cx, cy, _ = SPEEDS[number]
    if cy:
        plane = pltpu.roll(plane, cy % plane.shape[1], 1)
    if cx:
        plane = pltpu.roll(plane, cx % plane.shape[0], 0)
    return plane


def edge(plane, number):
    width = plane.shape[0]
    return plane[0:1] if SPEEDS[number][0] > 0 else plane[width - 1 : width]


def relax_kernel(
    rates_ref, pops_ref, vel_ref, axis_ref, calm_ref, up_ref, down_ref, side_ref, side_up_ref, side_down_ref, post_ref
):
    cells = pops_ref.shape[1]
    width = cells // 2

    def chunk(step, carry):
        rows = pl.ds(pl.multiple_of(step * 8, 8), 8)
        f = [pops_ref[i, rows, :] for i in range(19)]
        low = moments_of(f)
        density = low[0]
        inverse = 1.0 / density
        u = [low[c] * inverse for c in (1, 2, 3)]
        for c in range(3):
            vel_ref[c, rows, :] = u[c]
        eq = equilibrium_of(density, u)
        m = moments_of([f[i] - eq[i] for i in range(19)])
        relaxed = populations_of([rates_ref[i] * m[i] for i in range(19)])
        for i in range(19):
            post_ref[i, rows, :] = f[i] - relaxed[i]
        return carry

    lax.fori_loop(0, cells // 8, chunk, 0)

    def plane(number, z):
        return shifted(post_ref[number, z * width : (z + 1) * width, :], number)

    axis_ref[...] = post_ref[1:7]
    edges = []
    for place, number in enumerate(CALM):
        if number in FLAT:
            for z in (0, 1):
                value = plane(number, z)
                calm_ref[place, z * width : (z + 1) * width, :] = value
                if number:
                    edges.append(edge(value, number))
    corners_up, corners_down = [], []
    for outgoing, numbers, stays, corners in (
        (up_ref, RISING, 1, corners_up),
        (down_ref, FALLING, 0, corners_down),
    ):
        for place, number in enumerate(numbers):
            value = plane(number, 1 - stays)
            calm_ref[CALM.index(number), stays * width : (stays + 1) * width, :] = value
            leaves = plane(number, stays)
            calm_ref[CALM.index(number), (1 - stays) * width : (2 - stays) * width, :] = leaves
            outgoing[place] = leaves
            if SPEEDS[number][0]:
                edges.append(edge(value, number))
                corners.append(edge(leaves, number))
    lanes = pops_ref.shape[2]
    side_ref[...] = jnp.concatenate(edges + [jnp.zeros((16 - len(edges), lanes), F32)], axis=0)
    side_up_ref[...] = jnp.concatenate(corners_up + [jnp.zeros((6, lanes), F32)], axis=0)
    side_down_ref[...] = jnp.concatenate(corners_down + [jnp.zeros((6, lanes), F32)], axis=0)


def relax(rates, pops):
    _, cells, lanes = pops.shape
    width = cells // 2
    vmem = pl.BlockSpec(memory_space=pltpu.VMEM)
    return pl.pallas_call(
        relax_kernel,
        in_specs=[pl.BlockSpec(memory_space=pltpu.SMEM), vmem],
        out_specs=[vmem] * 8,
        out_shape=(
            jax.ShapeDtypeStruct((3, cells, lanes), F32),
            jax.ShapeDtypeStruct((6, cells, lanes), F32),
            jax.ShapeDtypeStruct((13, cells, lanes), F32),
            jax.ShapeDtypeStruct((4, width, lanes), F32),
            jax.ShapeDtypeStruct((4, width, lanes), F32),
            jax.ShapeDtypeStruct((16, lanes), F32),
            jax.ShapeDtypeStruct((8, lanes), F32),
            jax.ShapeDtypeStruct((8, lanes), F32),
        ),
        scratch_shapes=[pltpu.VMEM((19, cells, lanes), F32)],
        name="relax",
        compiler_params=pltpu.CompilerParams(vmem_limit_bytes=VMEM_LIMIT),
        cost_estimate=pl.CostEstimate(flops=10_000_000, bytes_accessed=6_000_000, transcendentals=0),
    )(rates, pops)


def couple_kernel(mail_ref, vel_ref, reply_ref, force_ref, wy_hi, wy_lo, a_hi, a_lo):
    comps, cells, depth = vel_ref.shape
    width = cells // 2
    slots = mail_ref.shape[0]
    t = mail_ref[...].T
    field = lambda v: t[v * SLOTS : (v + 1) * SLOTS, :]
    fx, fy, fz = field(0), field(1), field(2)
    atom_vel = [field(3), field(4), field(5)]
    friction = field(6)
    base = field(7).astype(I32)
    x0 = (base // depth) % width
    y0 = base % depth
    y1 = (y0 + 1) % depth
    gx, gy, gz = 1.0 - fx, 1.0 - fy, 1.0 - fz
    row_y = iota((depth, slots), 0)
    row_x = iota((width, slots), 0)

    v_hi, v_lo = halves(vel_ref[...].reshape(comps * cells, depth))
    along_x = []
    replies = [[], [], []]
    for r in range(SLOTS):
        one = slice(r, r + 1)
        cols = slice(r * slots, (r + 1) * slots)
        wy = jnp.where(row_y == y0[one], gy[one], 0.0) + jnp.where(row_y == y1[one], fy[one], 0.0)
        wx = jnp.where(row_x == x0[one], gx[one], 0.0) + jnp.where(row_x == x0[one] + 1, fx[one], 0.0)
        hi, lo = halves(wy)
        wy_hi[:, cols] = hi
        wy_lo[:, cols] = lo
        seen = mm(v_hi, hi) + (mm(v_lo, hi) + mm(v_hi, lo))
        for c in range(3):
            near = seen[c * cells : c * cells + width]
            far = seen[c * cells + width : (c + 1) * cells]
            value = jnp.sum(wx * (near * gz[one] + far * fz[one]), axis=0, keepdims=True)
            replies[c].append(value)
            pull = friction[one] * (atom_vel[c][one] - value)
            for z, weight in ((0, gz[one]), (1, fz[one])):
                hi_a, lo_a = halves(wx * (weight * pull))
                start = c * cells + z * width
                a_hi[start : start + width, cols] = hi_a
                a_lo[start : start + width, cols] = lo_a
    rows = [row for c in range(3) for row in replies[c]]
    rows.append(jnp.zeros((128 - 3 * SLOTS, slots), F32))
    reply_ref[...] = jnp.concatenate(rows, axis=0).T
    spread = mm_nt(a_hi[...], wy_hi[...]) + (mm_nt(a_lo[...], wy_hi[...]) + mm_nt(a_hi[...], wy_lo[...]))
    force_ref[...] = spread.reshape(comps, cells, depth)


def couple(mail, vel):
    comps, cells, depth = vel.shape
    slabs = mail.shape[0]
    return pl.pallas_call(
        couple_kernel,
        out_shape=(
            jax.ShapeDtypeStruct((slabs, 128), F32),
            jax.ShapeDtypeStruct((comps, cells, depth), F32),
        ),
        scratch_shapes=[
            pltpu.VMEM((depth, SLOTS * slabs), BF16),
            pltpu.VMEM((depth, SLOTS * slabs), BF16),
            pltpu.VMEM((comps * cells, SLOTS * slabs), BF16),
            pltpu.VMEM((comps * cells, SLOTS * slabs), BF16),
        ],
        name="couple",
        compiler_params=pltpu.CompilerParams(vmem_limit_bytes=VMEM_LIMIT),
        cost_estimate=pl.CostEstimate(flops=1_000_000_000, bytes_accessed=6_000_000, transcendentals=0),
    )(mail, vel)


def push_kernel(axis_ref, force_ref, moved_ref, up_ref, down_ref, side_ref):
    cells = axis_ref.shape[1]
    width = cells // 2
    edges = []
    for number in (5, 6, 1, 2, 3, 4):
        place = number - 1
        sign = 0.5 if number % 2 else -0.5
        for z in (0, 1):
            rows = slice(z * width, (z + 1) * width)
            value = shifted(axis_ref[place, rows, :] + sign * force_ref[place // 2, rows, :], number)
            if number == 5:
                if z == 1:
                    up_ref[...] = value
                moved_ref[place, (1 - z) * width : (2 - z) * width, :] = value
            elif number == 6:
                if z == 0:
                    down_ref[...] = value
                moved_ref[place, (1 - z) * width : (2 - z) * width, :] = value
            else:
                moved_ref[place, rows, :] = value
                if number in (1, 2):
                    edges.append(edge(value, number))
    side_ref[...] = jnp.concatenate(edges + [jnp.zeros((4, axis_ref.shape[2]), F32)], axis=0)


def push(axis, force):
    _, cells, lanes = axis.shape
    width = cells // 2
    return pl.pallas_call(
        push_kernel,
        out_shape=(
            jax.ShapeDtypeStruct((6, cells, lanes), F32),
            jax.ShapeDtypeStruct((width, lanes), F32),
            jax.ShapeDtypeStruct((width, lanes), F32),
            jax.ShapeDtypeStruct((8, lanes), F32),
        ),
        name="push",
        compiler_params=pltpu.CompilerParams(vmem_limit_bytes=VMEM_LIMIT),
        cost_estimate=pl.CostEstimate(flops=200_000, bytes_accessed=1_500_000, transcendentals=0),
    )(axis, force)


def gather_kernel(calm_ref, moved_ref, up_ref, down_ref, side_ref, side_up_ref, side_down_ref, out_ref, near_ref):
    cells = calm_ref.shape[1]
    width = cells // 2
    for place, number in enumerate(CALM):
        out_ref[number] = calm_ref[place]
    for place in range(6):
        out_ref[place + 1] = moved_ref[place]
    at = 0
    for number in FLAT[1:]:
        row = 0 if SPEEDS[number][0] > 0 else width - 1
        for z in (0, 1):
            out_ref[number, z * width + row : z * width + row + 1, :] = side_ref[at : at + 1, :]
            at += 1
    for arrived, numbers, stays, corners in (
        (up_ref, RISING, 1, side_up_ref),
        (down_ref, FALLING, 0, side_down_ref),
    ):
        corner = 0
        for place, number in enumerate(numbers):
            start = (1 - stays) * width
            out_ref[number, start : start + width, :] = arrived[place]
            if SPEEDS[number][0]:
                row = 0 if SPEEDS[number][0] > 0 else width - 1
                out_ref[number, stays * width + row : stays * width + row + 1, :] = side_ref[at : at + 1, :]
                out_ref[number, start + row : start + row + 1, :] = corners[corner : corner + 1, :]
                at += 1
                corner += 1
    for place in (0, 1):
        for z in (0, 1):
            tile = z * width + (0 if place == 0 else width - 8)
            near_ref[2 * place + z] = moved_ref[place, tile : tile + 8, :]


def gather(calm, moved, up, down, side, side_up, side_down):
    _, cells, lanes = calm.shape
    return pl.pallas_call(
        gather_kernel,
        out_shape=(
            jax.ShapeDtypeStruct((19, cells, lanes), F32),
            jax.ShapeDtypeStruct((4, 8, lanes), F32),
        ),
        name="gather",
        compiler_params=pltpu.CompilerParams(vmem_limit_bytes=VMEM_LIMIT),
        cost_estimate=pl.CostEstimate(flops=1_000, bytes_accessed=3_000_000, transcendentals=0),
    )(calm, moved, up, down, side, side_up, side_down)


def finish_kernel(
    pops_ref,
    near_ref,
    up_ref,
    down_ref,
    side_ref,
    reply_ref,
    slab_ref,
    rank_ref,
    vel_ref,
    fric_ref,
    pull_ref,
    out_ref,
    force_ref,
    tiles,
    sems,
):
    cells = pops_ref.shape[1]
    width = cells // 2
    rows = iota((8, near_ref.shape[2]), 0)
    copies = []
    for place in (0, 1):
        for z in (0, 1):
            which = 2 * place + z
            kept = rows != (0 if place == 0 else 7)
            tiles[which] = jnp.where(kept, near_ref[which], side_ref[which : which + 1, :])
            start = z * width + (0 if place == 0 else width - 8)
            copies.append(
                pltpu.make_async_copy(tiles.at[which], out_ref.at[1 + place, pl.ds(start, 8), :], sems.at[which])
            )
    copies.append(pltpu.make_async_copy(up_ref, out_ref.at[5, pl.ds(0, width), :], sems.at[4]))
    copies.append(pltpu.make_async_copy(down_ref, out_ref.at[6, pl.ds(width, width), :], sems.at[5]))
    for copy in copies:
        copy.start()

    slabs, atoms = reply_ref.shape[0], slab_ref.shape[1]
    one_hot = jnp.where(iota((slabs, atoms), 0) == slab_ref[...], 1.0, 0.0).astype(BF16)
    high, middle, low = thirds(reply_ref[...].T)
    picked = mm(high, one_hot) + (mm(middle, one_hot) + mm(low, one_hot))
    mine = iota((SLOTS, atoms), 0).astype(F32) == rank_ref[...]
    for c in range(3):
        seen = jnp.sum(jnp.where(mine, picked[c * SLOTS : (c + 1) * SLOTS], 0.0), axis=0, keepdims=True)
        drag = fric_ref[...] * (seen - vel_ref[c : c + 1, :])
        force_ref[c : c + 1, :] = pull_ref[c : c + 1, :] + drag

    for copy in copies:
        copy.wait()


def finish(pops, near, up, down, side, reply, slab, rank, vel, fric, pull):
    atoms = slab.shape[1]
    vmem = pl.BlockSpec(memory_space=pltpu.VMEM)
    anywhere = pl.BlockSpec(memory_space=pl.ANY)
    return pl.pallas_call(
        finish_kernel,
        in_specs=[anywhere] + [vmem] * 10,
        out_specs=[anywhere, vmem],
        out_shape=(
            jax.ShapeDtypeStruct(pops.shape, F32),
            jax.ShapeDtypeStruct((3, atoms), F32),
        ),
        scratch_shapes=[pltpu.VMEM(near.shape, F32), pltpu.SemaphoreType.DMA((6,))],
        input_output_aliases={0: 0},
        name="finish",
        compiler_params=pltpu.CompilerParams(vmem_limit_bytes=VMEM_LIMIT),
        cost_estimate=pl.CostEstimate(flops=100_000_000, bytes_accessed=300_000, transcendentals=0),
    )(pops, near, up, down, side, reply, slab, rank, vel, fric, pull)


def potential_kernel(
    before_ref,
    own_ref,
    after_ref,
    nbr_ref,
    bond_ref,
    w_self_ref,
    w_nbr_ref,
    w_rbf_ref,
    w_out_ref,
    force_ref,
    new_ref,
    table,
    own_half,
    total,
):
    feats, atoms = own_ref.shape
    near, basis = nbr_ref.shape[0], w_rbf_ref.shape[1]
    block = 256
    for place, ref in enumerate((before_ref, own_ref, after_ref)):
        value = mm(w_nbr_ref[...], ref[...]).astype(BF16)
        table[place * feats : (place + 1) * feats, :] = (value.astype(F32) * 0.5).astype(BF16)
    own_half[...] = 0.5 * mm(w_self_ref[...], own_ref[...])
    total[...] = jnp.zeros_like(total)
    force_ref[...] = jnp.zeros_like(force_ref)
    rbf_hi, rbf_lo = halves(0.5 * w_rbf_ref[...])
    rbf = jnp.concatenate([rbf_hi, rbf_lo, rbf_hi], axis=1)
    spacing = RADIAL_REACH / (basis - 1)
    centers = iota((basis, block), 0).astype(F32) * spacing
    w_out = w_out_ref[...]
    rows = iota((atoms, block), 0)

    def one(k, carry):
        for part in range(atoms // block):
            cols = slice(part * block, (part + 1) * block)
            nbr = nbr_ref[pl.ds(k, 1), cols]
            place = nbr // atoms
            one_hot = jnp.where(rows == nbr % atoms, 1.0, 0.0).astype(BF16)
            seen = mm(table[...], one_hot)
            bond = [bond_ref[c, pl.ds(k, 1), cols] for c in range(3)]
            length = jnp.sqrt(bond[0] * bond[0] + bond[1] * bond[1] + bond[2] * bond[2] + 1e-6)
            scaled = (length - centers) * (1.0 / spacing)
            rad_hi, rad_lo = halves(jnp.exp(-scaled * scaled))
            radial = jnp.concatenate([rad_hi, rad_hi, rad_lo], axis=0)
            picked = jnp.where(
                place == 0, seen[:feats], jnp.where(place == 1, seen[feats : 2 * feats], seen[2 * feats :])
            )
            half = own_half[:, cols] + picked + mm(rbf, radial)
            hidden = half + half * jnp.tanh(half)
            total[:, cols] += hidden
            scalar = jnp.sum(hidden * w_out, axis=0, keepdims=True)
            for c in range(3):
                force_ref[c : c + 1, cols] += scalar * bond[c]
        return carry

    lax.fori_loop(0, near, one, 0)
    new_ref[...] = (own_ref[...].astype(F32) + total[...] * (1.0 / near)).astype(BF16)


def potential(before, own, after, nbrs, bonds, w_self, w_nbr, w_rbf, w_out):
    feats, atoms = own.shape
    return pl.pallas_call(
        potential_kernel,
        out_shape=(
            jax.ShapeDtypeStruct((3, atoms), F32),
            jax.ShapeDtypeStruct((feats, atoms), BF16),
        ),
        scratch_shapes=[
            pltpu.VMEM((3 * feats, atoms), BF16),
            pltpu.VMEM((feats, atoms), F32),
            pltpu.VMEM((feats, atoms), F32),
        ],
        name="potential",
        compiler_params=pltpu.CompilerParams(vmem_limit_bytes=VMEM_LIMIT),
        cost_estimate=pl.CostEstimate(flops=7_000_000_000, bytes_accessed=2_000_000, transcendentals=1_200_000),
    )(before, own, after, nbrs, bonds, w_self, w_nbr, w_rbf, w_out)


def body(
    slabs,
    populations,
    relax_rates,
    slab,
    stencil_base,
    frac,
    atom_vel,
    friction,
    features,
    neighbors,
    bonds,
    w_self,
    w_nbr,
    w_rbf,
    w_out,
):
    _, planes, width, depth = populations.shape
    atoms = slab.shape[0]
    up = [(i, (i + 1) % slabs) for i in range(slabs)]
    down = [(j, i) for i, j in up]
    across = [(0, 1), (1, 0)]
    both = ("fluid", "group")
    up_across = [(2 * i + g, 2 * j + 1 - g) for i, j in up for g in (0, 1)]
    down_across = [(2 * i + g, 2 * j + 1 - g) for i, j in down for g in (0, 1)]
    slab_row = slab.reshape(1, atoms)
    friction_row = friction.reshape(1, atoms)

    before = lax.ppermute(features, "fluid", up)
    after = lax.ppermute(features, "fluid", down)
    outgoing, rank = pack(slab_row, stencil_base.reshape(1, atoms), frac, atom_vel, friction_row, slabs)
    mail = lax.all_to_all(outgoing.reshape(slabs, 1, 128), "fluid", split_axis=0, concat_axis=0, tiled=True)

    vel, axis, calm, rising, falling, side, side_up, side_down = relax(
        relax_rates, populations.reshape(19, planes * width, depth)
    )
    rising = lax.ppermute(rising, "fluid", up)
    falling = lax.ppermute(falling, "fluid", down)
    side = lax.ppermute(side, "group", across)
    side_up = lax.ppermute(side_up, both, up_across)
    side_down = lax.ppermute(side_down, both, down_across)

    pull, new_features = potential(
        before,
        features,
        after,
        neighbors.T,
        bonds.transpose(0, 2, 1),
        w_self,
        w_nbr,
        w_rbf,
        w_out.reshape(-1, 1),
    )

    reply, force = couple(mail.reshape(slabs, 128), vel)
    reply = lax.all_to_all(reply.reshape(slabs, 1, 128), "fluid", split_axis=0, concat_axis=0, tiled=True)
    moved, late_up, late_down, late_side = push(axis, force)
    late_up = lax.ppermute(late_up, "fluid", up)
    late_down = lax.ppermute(late_down, "fluid", down)
    late_side = lax.ppermute(late_side, "group", across)
    pops, near = gather(calm, moved, rising, falling, side, side_up, side_down)
    pops, atom_force = finish(
        pops,
        near,
        late_up,
        late_down,
        late_side,
        reply.reshape(slabs, 128),
        slab_row,
        rank,
        atom_vel,
        friction_row,
        pull,
    )
    return pops.reshape(populations.shape), atom_force, new_features


def solution(mesh):
    in_specs = (
        P(None, "fluid", "group", None),
        P(),
        P(("fluid", "group"), None),
        P(("fluid", "group")),
        P(None, ("fluid", "group")),
        P(None, ("fluid", "group")),
        P(("fluid", "group")),
        P(None, ("fluid", "group")),
        P(("fluid", "group"), None),
        P(None, ("fluid", "group"), None),
        P(),
        P(),
        P(),
        P(),
    )
    out_specs = (
        P(None, "fluid", "group", None),
        P(None, ("fluid", "group")),
        P(None, ("fluid", "group")),
    )
    return jax.shard_map(
        functools.partial(body, mesh.shape["fluid"]),
        mesh=mesh,
        in_specs=in_specs,
        out_specs=out_specs,
        check_vma=False,
    )
```

time: 328 us -> 73 us (0.22); the launches traced: 322 us -> 72.7 us
  local copies, waits for them, and re-layouts: 166 us -> 3.8 us
  other arithmetic: 65.5 us -> 0 us
  matrix products: 33.9 us -> 0 us
  Pallas kernels: 0 us -> 16.5 us
    scatter x2 -> x0, local copies, waits for them, and re-layouts: 76.2 us -> none  [the longest x1 54.2 us: body(): jnp.zeros((slabs, 7, capacity), jnp.float32).at[target, :, places]]
    gather x3 -> x0, local copies, waits for them, and re-layouts: 58 us -> none  [the longest x1 31.2 us: interpolate(): return jnp.sum(weights[None] * velocity[:, nodes], axis=1)]
    scatter-add x1 -> x0, other arithmetic: 44.2 us -> none  [spread(): jnp.zeros((3, cells), jnp.float32).at[:, nodes.reshape(-1)].add(terms)]
    dot_general x10 -> x0, matrix products: 33.9 us -> none  [the longest x1 9.32 us: collide(): forcing = jnp.dot(inverse[:, 1:4], force, precision=lax.Precision.HIGHEST)]
    pallas_call x0 -> x7, Pallas kernels: none -> 16.5 us  [the longest x1 8.59 us: potential(): pl.pallas_call(potential_kernel, out_shape=(jax.ShapeDtypeStruct((3, atom...]
    all_to_all x3 -> x2, starting transfers between devices: 35 us -> 22.7 us  [the longest x1 13.9 us: body(): lax.all_to_all(outgoing.reshape(slabs, 1, 128), 'fluid', split_axis=0, co...]
    ppermute x6 -> x10, starting transfers between devices: 17.8 us -> 28.8 us  [the longest x1 5.96 us: body(): side_down = lax.ppermute(side_down, both, down_across)]
    unnamed x21 -> x0, other arithmetic: 9.22 us -> none
  transfers between devices with their start and end apart: 9 -> 12, of which waited for: 2 -> 0; matrix products, arithmetic and copies ran while one was open for 77% -> 0% of each run, Pallas kernels for 0% -> 19%
where the time goes in v1:
time: 73 us; the launch traced here: 72.7 us
  starting transfers between devices  51.6 us (71%)
  Pallas kernels  16.5 us (23%)
  local copies, waits for them, and re-layouts  3.8 us (5%)
  between operations  0.82 us (1%)
    all_to_all x1, starting transfers between devices, body(): lax.all_to_all(outgoing.reshape(slabs, 1, 128), 'fluid', split_axis=0, co...  13.9 us
    all_to_all x1, starting transfers between devices, body(): lax.all_to_all(reply.reshape(slabs, 1, 128), 'fluid', split_axis=0, conca...  8.87 us
    pallas_call x1, Pallas kernels, potential(): pl.pallas_call(potential_kernel, out_shape=(jax.ShapeDtypeStruct((3, atom...  8.59 us
    ppermute x1, starting transfers between devices, body(): side_down = lax.ppermute(side_down, both, down_across)  5.96 us
    ppermute x1, starting transfers between devices, body(): late_down = lax.ppermute(late_down, 'fluid', down)  5.96 us
    ppermute x1, starting transfers between devices, body(): after = lax.ppermute(features, 'fluid', down)  5.95 us
    ppermute x1, starting transfers between devices, body(): falling = lax.ppermute(falling, 'fluid', down)  5.94 us
    ppermute x1, starting transfers between devices, body(): late_side = lax.ppermute(late_side, 'group', across)  4.12 us
  transfers between devices with their start and end apart: 12, of which 0 were waited for; matrix products, arithmetic and copies ran while one was open for 0% of the time, Pallas kernels for 19%

profile of v1, /device:TPU:16, one launch (start us, length us, event | category | flops | bytes accessed | tf_op | source)
XLA Modules:
  0.0 72.7 jit_solution(18019654382037675068)
XLA Ops:
  0.6 0.0 copy-start.1
  0.7 0.8 %copy-done.1 = f32[3,512]{1,0:T(4,128)S(1)} copy-done((f32[3,512]{1,0:T(4,128)S(1)}, f32[3,512]{1,0:T(4,128)}, u32[]{:S(2)}) %copy-start.1) | copy-done | bytes 6168
  1.4 0.7 copy-done.3
  2.1 0.7 copy-done.5
  2.8 0.7 copy-done.13
  3.5 0.7 copy-done.14
  4.2 1.2 %pack.1 = (f32[128,128]{1,0:T(8,128)}, f32[1,512]{1,0:T(1,128)S(1)}) custom-call(s32[1,512]{1,0:T(1,128)S(1)} %bitcast.19, s32[1,512]{1,0:T(1,128)S(1)} %bitcast.25, f32[3,512]{1,0:T(4,128)S(1)} %copy-done.13, f32[3,512]{1,0:T(4,128)S(1)} %copy-done.1, f32[1,512]{1,0:T(1,128)S(1)} %bitcast.21), custom_call_target="tpu_custom_call" | custom-call | flops 400000000 | bytes 4000000 | tf_op jit(solution)/shard_map/pack/pallas_call | solution.py:94
  5.4 13.9 %all-to-all-start = ((f32[128,1,128]{2,1,0:T(1,128)}), f32[128,1,128]{2,1,0:T(1,128)S(1)}, u32[]{:S(2)}, u32[]{:S(2)}) async-start(f32[128,1,128]{2,1,0:T(1,128)} %bitcast.5), calls=%async_computation | async-start | bytes 131072 | tf_op jit(solution)/shard_map/all_to_all | solution.py:604
  19.3 0.1 collective-permute-start.8
  19.4 6.0 %collective-permute-start.9 = (bf16[128,512]{1,0:T(8,128)(2,1)S(1)}, bf16[128,512]{1,0:T(8,128)(2,1)S(1)}, u32[]{:S(2)}, u32[]{:S(2)}) collective-permute-start(bf16[128,512]{1,0:T(8,128)(2,1)S(1)} %copy-done.8), channel_id=1, source_target_pairs={{2,0},{4,2},{6,4},{8,6},{10,8},{12,10},{14,12},{16,14},{18,16},{20... | collective-permute-start | bytes 393224 | tf_op jit(solution)/shard_map/ppermute | solution.py:602
  25.4 1.7 %relax.1 = (f32[3,128,128]{2,1,0:T(8,128)S(1)}, f32[6,128,128]{2,1,0:T(8,128)S(1)}, f32[13,128,128]{2,1,0:T(8,128)S(1)}, f32[4,64,128]{2,1,0:T(8,128)S(1)}, f32[...) custom-call(f32[19]{0:T(128)S(1)} %copy-done.7, ...), custom_call_target="tpu_custom_call" | custom-call | flops 10000000 | bytes 6000000 | tf_op jit(solution)/shard_map/relax/pallas_call | solution.py:248
  27.1 0.7 collective-permute-start.2
  27.8 6.0 %collective-permute-start.4 = (f32[8,128]{1,0:T(8,128)S(1)}, f32[8,128]{1,0:T(8,128)S(1)}, u32[]{:S(2)}, u32[]{:S(2)}) collective-permute-start(f32[8,128]{1,0:T(8,128)S(1)} %get-tuple-element.35), channel_id=1, source_target_pairs={{2,1},{3,0},{4,3},{5,2},{6,5},{7,4},{8,7},{9,6},{10,9},{11,8},{12,... | collective-permute-start | bytes 12296 | tf_op jit(solution)/shard_map/ppermute | solution.py:613
  33.8 0.1 copy.22.w_rbf_ref
  33.9 0.1 copy.23.w_out_ref
  34.0 0.0 copy-start.9
  34.0 0.0 copy-start.10
  34.0 0.0 copy-start.11
  34.0 0.0 copy-start.12
  34.1 2.2 %couple.1 = (f32[128,128]{1,0:T(8,128)}, f32[3,128,128]{2,1,0:T(8,128)S(1)}) custom-call(f32[128,128]{1,0:T(8,128)S(1)} %bitcast.18, f32[3,128,128]{2,1,0:T(8,128)S(1)} %get-tuple-element.28.vel_ref), custom_call_target="tpu_custom_call" | custom-call | flops 1000000000 | bytes 6000000 | tf_op jit(solution)/shard_map/couple/pallas_call | solution.py:319
  36.2 8.9 %all-to-all-start.1 = ((f32[128,1,128]{2,1,0:T(1,128)}), f32[128,1,128]{2,1,0:T(1,128)S(1)}, u32[]{:S(2)}, u32[]{:S(2)}) async-start(f32[128,1,128]{2,1,0:T(1,128)} %bitcast.8), calls=%async_computation.1 | async-start | bytes 131072 | tf_op jit(solution)/shard_map/all_to_all | solution.py:628
  45.1 0.1 push.1
  45.2 0.0 collective-permute-done.3.side_up_ref
  45.2 0.1 collective-permute-start
  45.3 0.0 collective-permute-done.4.side_down_ref
  45.3 5.9 %collective-permute-start.1 = (f32[4,64,128]{2,1,0:T(8,128)S(1)}, f32[4,64,128]{2,1,0:T(8,128)S(1)}, u32[]{:S(2)}, u32[]{:S(2)}) collective-permute-start(f32[4,64,128]{2,1,0:T(8,128)S(1)} %get-tuple-element.32), channel_id=1, source_target_pairs={{2,0},{4,2},{6,4},{8,6},{10,8},{12,10},{14,12},{16,14},{18,16},{20... | collective-permute-start | bytes 393224 | tf_op jit(solution)/shard_map/ppermute | solution.py:610
  51.3 6.0 %collective-permute-start.6 = (f32[64,128]{1,0:T(8,128)S(1)}, f32[64,128]{1,0:T(8,128)S(1)}, u32[]{:S(2)}, u32[]{:S(2)}) collective-permute-start(f32[64,128]{1,0:T(8,128)S(1)} %get-tuple-element.39), channel_id=1, source_target_pairs={{2,0},{4,2},{6,4},{8,6},{10,8},{12,10},{14,12},{16,14},{18,16},{20... | collective-permute-start | bytes 98312 | tf_op jit(solution)/shard_map/ppermute | solution.py:631
  57.3 4.1 %collective-permute-start.7 = (f32[8,128]{1,0:T(8,128)S(1)}, f32[8,128]{1,0:T(8,128)S(1)}, u32[]{:S(2)}, u32[]{:S(2)}) collective-permute-start(f32[8,128]{1,0:T(8,128)S(1)} %get-tuple-element.40), channel_id=1, source_target_pairs={{0,1},{1,0},{2,3},{3,2},{4,5},{5,4},{6,7},{7,6},{8,9},{9,8},{10,11... | collective-permute-start | bytes 12296 | tf_op jit(solution)/shard_map/ppermute | solution.py:632
  61.4 8.6 %potential.1 = (f32[3,512]{1,0:T(4,128)S(1)}, bf16[128,512]{1,0:T(8,128)(2,1)}) custom-call(bf16[128,512]{1,0:T(8,128)(2,1)S(1)} %collective-permute-done.8.before_ref, bf16[128,512]{1,0:T(8,128)(2,1)S(1)} %copy-done.8, bf16[128,512]{1,0:T(8,128)(2,1)S(1)} %collective-permute-done.9.after_ref, s32[16,512]{1,0:T(8,128)S(1)} %bitcast.24, ...), custom_call_target="tpu_custom_call" | custom-call | flops 7000000000 | bytes 2000000 | tf_op jit(solution)/shard_map/potential/pallas_call | solution.py:556
  70.0 0.0 collective-permute-done.up_ref
  70.0 1.1 %gather.1 = (f32[19,128,128]{2,1,0:T(8,128)}, f32[4,8,128]{2,1,0:T(8,128)S(1)}) custom-call(f32[13,128,128]{2,1,0:T(8,128)S(1)} %get-tuple-element.25.calm_ref, f32[6,128,128]{2,1,0:T(8,128)S(1)} %get-tuple-element.30.moved_ref, f32[4,64,128]{2,1,0:T(8,128)S(1)} %collective-permute-done.up_ref, f32[4,64,128]{2,1,0:T(8,128)S(1)} %collective-permute-done.1.down_ref, ...), custom_call_target="tpu_custom_call" | custom-call | flops 1000 | bytes 3000000 | tf_op jit(solution)/shard_map/gather/pallas_call | solution.py:414
  71.2 1.5 %finish.1 = (f32[19,128,128]{2,1,0:T(8,128)}, f32[3,512]{1,0:T(4,128)}) custom-call(f32[19,128,128]{2,1,0:T(8,128)} %get-tuple-element.36.pops_ref, f32[4,8,128]{2,1,0:T(8,128)S(1)} %get-tuple-element.37.near_ref, f32[64,128]{1,0:T(8,128)S(1)} %collective-permute-done.5.up_ref, ...), custom_call_target="tpu_custom_call", output_to_operand_aliasing={{0}: (0, {})} | custom-call | flops 100000000 | bytes 300000 | tf_op jit(solution)/shard_map/finish/pallas_call | solution.py:479
  (35 shorter events, 0.1 us)
Async XLA Ops:
  0.6 24.7 %copy-start = (f32[19,2,64,128]{3,2,1,0:T(8,128)S(1)}, f32[19,2,64,128]{3,2,1,0:T(8,128)}, u32[]{:S(2)}) copy-start(f32[19,2,64,128]{3,2,1,0:T(8,128)} %param.14) | copy-start | bytes 3735556
  0.6 0.8 %copy-start.1 = (f32[3,512]{1,0:T(4,128)S(1)}, f32[3,512]{1,0:T(4,128)}, u32[]{:S(2)}) copy-start(f32[3,512]{1,0:T(4,128)} %vel_ref.3) | copy-start | bytes 18436
  1.4 0.7 copy-start.3
  2.1 0.7 copy-start.5
  2.8 0.7 copy-start.13
  3.5 0.7 copy-start.14
  4.2 15.1 %copy-start.8 = (bf16[128,512]{1,0:T(8,128)(2,1)S(1)}, bf16[128,512]{1,0:T(8,128)(2,1)}, u32[]{:S(2)}) copy-start(bf16[128,512]{1,0:T(8,128)(2,1)} %own_ref.1) | copy-start | bytes 393220
  4.2 21.2 %copy-start.7 = (f32[19]{0:T(128)S(1)}, f32[19]{0:T(128)}, u32[]{:S(2)}) copy-start(f32[19]{0:T(128)} %rates_ref.1) | copy-start | bytes 232
  4.2 29.6 %copy-start.15 = (f32[128,16]{0,1:T(8,128)S(1)}, f32[128,16]{0,1:T(8,128)}, u32[]{:S(2)}) copy-start(f32[128,16]{0,1:T(8,128)} %param.26) | copy-start | bytes 24580
  4.2 29.7 %copy-start.16 = (f32[128]{0:T(128)S(1)}, f32[128]{0:T(128)}, u32[]{:S(2)}) copy-start(f32[128]{0:T(128)} %param.27) | copy-start | bytes 1540
  5.4 28.6 %all-to-all-start = ((f32[128,1,128]{2,1,0:T(1,128)}), f32[128,1,128]{2,1,0:T(1,128)S(1)}, u32[]{:S(2)}, u32[]{:S(2)}) async-start(f32[128,1,128]{2,1,0:T(1,128)} %bitcast.5), calls=%async_computation | async-start | bytes 131072 | tf_op jit(solution)/shard_map/all_to_all | solution.py:604
  19.3 32.0 %collective-permute-start.8 = (bf16[128,512]{1,0:T(8,128)(2,1)S(1)}, bf16[128,512]{1,0:T(8,128)(2,1)S(1)}, u32[]{:S(2)}, u32[]{:S(2)}) collective-permute-start(bf16[128,512]{1,0:T(8,128)(2,1)S(1)} %copy-done.8), channel_id=1, source_target_pairs={{0,2},{2,4},{4,6},{6,8},{8,10},{10,12},{12,14},{14,16},{16,18},{18... | collective-permute-start | bytes 393224 | tf_op jit(solution)/shard_map/ppermute | solution.py:601
  19.4 37.9 %collective-permute-start.9 = (bf16[128,512]{1,0:T(8,128)(2,1)S(1)}, bf16[128,512]{1,0:T(8,128)(2,1)S(1)}, u32[]{:S(2)}, u32[]{:S(2)}) collective-permute-start(bf16[128,512]{1,0:T(8,128)(2,1)S(1)} %copy-done.8), channel_id=1, source_target_pairs={{2,0},{4,2},{6,4},{8,6},{10,8},{12,10},{14,12},{16,14},{18,16},{20... | collective-permute-start | bytes 393224 | tf_op jit(solution)/shard_map/ppermute | solution.py:602
  27.1 24.2 %collective-permute-start.2 = (f32[16,128]{1,0:T(8,128)S(1)}, f32[16,128]{1,0:T(8,128)S(1)}, u32[]{:S(2)}, u32[]{:S(2)}) collective-permute-start(f32[16,128]{1,0:T(8,128)S(1)} %get-tuple-element.33), channel_id=1, source_target_pairs={{0,1},{1,0},{2,3},{3,2},{4,5},{5,4},{6,7},{7,6},{8,9},{9,8},{10,11... | collective-permute-start | bytes 24584 | tf_op jit(solution)/shard_map/ppermute | solution.py:611
  27.8 17.4 %collective-permute-start.3 = (f32[8,128]{1,0:T(8,128)S(1)}, f32[8,128]{1,0:T(8,128)S(1)}, u32[]{:S(2)}, u32[]{:S(2)}) collective-permute-start(f32[8,128]{1,0:T(8,128)S(1)} %get-tuple-element.34), channel_id=1, source_target_pairs={{0,3},{1,2},{2,5},{3,4},{4,7},{5,6},{6,9},{7,8},{8,11},{9,10},{10,... | collective-permute-start | bytes 12296 | tf_op jit(solution)/shard_map/ppermute | solution.py:612
  27.8 17.5 %collective-permute-start.4 = (f32[8,128]{1,0:T(8,128)S(1)}, f32[8,128]{1,0:T(8,128)S(1)}, u32[]{:S(2)}, u32[]{:S(2)}) collective-permute-start(f32[8,128]{1,0:T(8,128)S(1)} %get-tuple-element.35), channel_id=1, source_target_pairs={{2,1},{3,0},{4,3},{5,2},{6,5},{7,4},{8,7},{9,6},{10,9},{11,8},{12,... | collective-permute-start | bytes 12296 | tf_op jit(solution)/shard_map/ppermute | solution.py:613
  34.0 27.4 %copy-start.9 = (f32[3,512,16]{1,2,0:T(8,128)S(1)}, f32[3,512,16]{1,2,0:T(8,128)}, u32[]{:S(2)}) copy-start(f32[3,512,16]{1,2,0:T(8,128)} %param.23) | copy-start | bytes 294916
  34.0 27.4 %copy-start.10 = (s32[512,16]{0,1:T(8,128)S(1)}, s32[512,16]{0,1:T(8,128)}, u32[]{:S(2)}) copy-start(s32[512,16]{0,1:T(8,128)} %param.22) | copy-start | bytes 98308
  34.0 27.4 %copy-start.11 = (bf16[128,128]{1,0:T(8,128)(2,1)S(1)}, bf16[128,128]{1,0:T(8,128)(2,1)}, u32[]{:S(2)}) copy-start(bf16[128,128]{1,0:T(8,128)(2,1)} %w_self_ref.1) | copy-start | bytes 98308
  34.0 27.3 %copy-start.12 = (bf16[128,128]{1,0:T(8,128)(2,1)S(1)}, bf16[128,128]{1,0:T(8,128)(2,1)}, u32[]{:S(2)}) copy-start(bf16[128,128]{1,0:T(8,128)(2,1)} %w_nbr_ref.1) | copy-start | bytes 98308
  36.2 34.9 %all-to-all-start.1 = ((f32[128,1,128]{2,1,0:T(1,128)}), f32[128,1,128]{2,1,0:T(1,128)S(1)}, u32[]{:S(2)}, u32[]{:S(2)}) async-start(f32[128,1,128]{2,1,0:T(1,128)} %bitcast.8), calls=%async_computation.1 | async-start | bytes 131072 | tf_op jit(solution)/shard_map/all_to_all | solution.py:628
  45.2 24.8 %collective-permute-start = (f32[4,64,128]{2,1,0:T(8,128)S(1)}, f32[4,64,128]{2,1,0:T(8,128)S(1)}, u32[]{:S(2)}, u32[]{:S(2)}) collective-permute-start(f32[4,64,128]{2,1,0:T(8,128)S(1)} %get-tuple-element.31), channel_id=1, source_target_pairs={{0,2},{2,4},{4,6},{6,8},{8,10},{10,12},{12,14},{14,16},{16,18},{18... | collective-permute-start | bytes 393224 | tf_op jit(solution)/shard_map/ppermute | solution.py:609
  45.3 24.7 %collective-permute-start.1 = (f32[4,64,128]{2,1,0:T(8,128)S(1)}, f32[4,64,128]{2,1,0:T(8,128)S(1)}, u32[]{:S(2)}, u32[]{:S(2)}) collective-permute-start(f32[4,64,128]{2,1,0:T(8,128)S(1)} %get-tuple-element.32), channel_id=1, source_target_pairs={{2,0},{4,2},{6,4},{8,6},{10,8},{12,10},{14,12},{16,14},{18,16},{20... | collective-permute-start | bytes 393224 | tf_op jit(solution)/shard_map/ppermute | solution.py:610
  51.3 19.9 %collective-permute-start.5 = (f32[64,128]{1,0:T(8,128)S(1)}, f32[64,128]{1,0:T(8,128)S(1)}, u32[]{:S(2)}, u32[]{:S(2)}) collective-permute-start(f32[64,128]{1,0:T(8,128)S(1)} %get-tuple-element.38), channel_id=1, source_target_pairs={{0,2},{2,4},{4,6},{6,8},{8,10},{10,12},{12,14},{14,16},{16,18},{18... | collective-permute-start | bytes 98312 | tf_op jit(solution)/shard_map/ppermute | solution.py:630
  51.3 19.9 %collective-permute-start.6 = (f32[64,128]{1,0:T(8,128)S(1)}, f32[64,128]{1,0:T(8,128)S(1)}, u32[]{:S(2)}, u32[]{:S(2)}) collective-permute-start(f32[64,128]{1,0:T(8,128)S(1)} %get-tuple-element.39), channel_id=1, source_target_pairs={{2,0},{4,2},{6,4},{8,6},{10,8},{12,10},{14,12},{16,14},{18,16},{20... | collective-permute-start | bytes 98312 | tf_op jit(solution)/shard_map/ppermute | solution.py:631
  57.3 13.9 %collective-permute-start.7 = (f32[8,128]{1,0:T(8,128)S(1)}, f32[8,128]{1,0:T(8,128)S(1)}, u32[]{:S(2)}, u32[]{:S(2)}) collective-permute-start(f32[8,128]{1,0:T(8,128)S(1)} %get-tuple-element.40), channel_id=1, source_target_pairs={{0,1},{1,0},{2,3},{3,2},{4,5},{5,4},{6,7},{7,6},{8,9},{9,8},{10,11... | collective-permute-start | bytes 12296 | tf_op jit(solution)/shard_map/ppermute | solution.py:632
  70.0 1.2 %copy-start.2 = (f32[3,512]{1,0:T(4,128)S(1)}, f32[3,512]{1,0:T(4,128)}, u32[]{:S(2)}) copy-start(f32[3,512]{1,0:T(4,128)} %vel_ref.3) | copy-start | bytes 18436
  70.0 1.2 %copy-start.4 = (s32[512,1]{0,1:T(1,128)S(1)}, s32[512,1]{0,1:T(1,128)}, u32[]{:S(2)}) copy-start(s32[512,1]{0,1:T(1,128)} %param.16) | copy-start | bytes 6148
  70.0 1.2 %copy-start.6 = (f32[512]{0:T(512)S(1)}, f32[512]{0:T(512)}, u32[]{:S(2)}) copy-start(f32[512]{0:T(512)} %param.20) | copy-start | bytes 6148

commit v2 on v1

v2 whole, which is shorter than its diff:
```python
import functools

import jax
import jax.numpy as jnp
from jax import lax
from jax.experimental import pallas as pl
from jax.experimental.pallas import tpu as pltpu
from jax.sharding import PartitionSpec as P

F32 = jnp.float32
BF16 = jnp.bfloat16
I32 = jnp.int32

RADIAL_REACH = 4.0
SLOTS = 8

SPEEDS = (
    (0, 0, 0),
    (1, 0, 0),
    (-1, 0, 0),
    (0, 1, 0),
    (0, -1, 0),
    (0, 0, 1),
    (0, 0, -1),
    (1, 1, 0),
    (-1, -1, 0),
    (1, -1, 0),
    (-1, 1, 0),
    (1, 0, 1),
    (-1, 0, -1),
    (1, 0, -1),
    (-1, 0, 1),
    (0, 1, 1),
    (0, -1, -1),
    (0, 1, -1),
    (0, -1, 1),
)
RISING = (11, 14, 15, 18)
FALLING = (12, 13, 16, 17)
FLAT = (0, 7, 8, 9, 10)
CALM = (0, 7, 8, 9, 10, 11, 12, 13, 14, 15, 16, 17, 18)

VMEM_LIMIT = 48 * 1024 * 1024


def halves(value):
    high = value.astype(BF16)
    low = (value - high.astype(F32)).astype(BF16)
    return high, low


def thirds(value):
    high = value.astype(BF16)
    rest = value - high.astype(F32)
    middle = rest.astype(BF16)
    low = (rest - middle.astype(F32)).astype(BF16)
    return high, middle, low


def mm(a, b):
    return jnp.dot(a, b, preferred_element_type=F32)


def mm_nt(a, b):
    return lax.dot_general(a, b, (((1,), (1,)), ((), ())), preferred_element_type=F32)


def iota(shape, dim):
    return lax.broadcasted_iota(I32, shape, dim)


def packed(slab, base, frac_ref, vel_ref, fric, slabs):
    atoms = slab.shape[1]
    named = iota((slabs, atoms), 0) == slab
    one_hot = jnp.where(named, 1.0, 0.0)
    one_hot_b = one_hot.astype(BF16)
    earlier = jnp.where(iota((atoms, atoms), 0) < iota((atoms, atoms), 1), 1.0, 0.0).astype(BF16)
    before = mm(one_hot_b, earlier)
    rank = jnp.sum(one_hot * before, axis=0, keepdims=True)
    mine = iota((SLOTS, atoms), 0).astype(F32) == rank
    rows = [frac_ref[c : c + 1, :] for c in range(3)]
    rows += [vel_ref[c : c + 1, :] for c in range(3)]
    rows += [fric, base.astype(F32)]
    spread = [jnp.where(mine, row, 0.0) for row in rows]
    spread.append(jnp.zeros((128 - SLOTS * len(rows), atoms), F32))
    high, middle, low = thirds(jnp.concatenate(spread, axis=0))
    return mm_nt(one_hot_b, high) + (mm_nt(one_hot_b, middle) + mm_nt(one_hot_b, low)), rank


def moments_of(d):
    m = [None] * 19
    quad = {}
    for name, (pp, nn, pn, np_) in dict(xy=(7, 8, 9, 10), xz=(11, 12, 13, 14), yz=(15, 16, 17, 18)).items():
        same, cross = d[pp] + d[nn], d[pn] + d[np_]
        odd_same, odd_cross = d[pp] - d[nn], d[pn] - d[np_]
        quad[name] = (same + cross, same - cross, odd_same + odd_cross, odd_same - odd_cross)
    sxy, m[4], m[10], m[12] = quad["xy"]
    sxz, m[5], m[11], m[13] = quad["xz"]
    syz, m[6], m[15], m[14] = quad["yz"]
    m[16], m[17], m[18] = sxy, sxz, syz
    ax, ay, az = d[1] + d[2], d[3] + d[4], d[5] + d[6]
    m[0] = (d[0] + ax) + (ay + az) + (sxy + (sxz + syz))
    m[1] = (d[1] - d[2]) + (m[10] + m[11])
    m[2] = (d[3] - d[4]) + (m[12] + m[15])
    m[3] = (d[5] - d[6]) + (m[13] + m[14])
    m[7] = ax + (sxy + sxz)
    m[8] = ay + (sxy + syz)
    m[9] = az + (sxz + syz)
    return m


def populations_of(m):
    f = [None] * 19
    for (pp, nn, pn, np_), (s, c, first, second) in (
        ((7, 8, 9, 10), (m[16], m[4], m[10], m[12])),
        ((11, 12, 13, 14), (m[17], m[5], m[11], m[13])),
        ((15, 16, 17, 18), (m[18], m[6], m[15], m[14])),
    ):
        same, cross = 0.25 * (s + c), 0.25 * (s - c)
        odd_same, odd_cross = 0.25 * (first + second), 0.25 * (first - second)
        f[pp], f[nn] = same + odd_same, same - odd_same
        f[pn], f[np_] = cross + odd_cross, cross - odd_cross
    for plus, minus, square, line, squares, lines in (
        (1, 2, m[7], m[1], (m[16], m[17]), (m[10], m[11])),
        (3, 4, m[8], m[2], (m[16], m[18]), (m[12], m[15])),
        (5, 6, m[9], m[3], (m[17], m[18]), (m[13], m[14])),
    ):
        even = 0.5 * (square - (squares[0] + squares[1]))
        odd = 0.5 * (line - (lines[0] + lines[1]))
        f[plus], f[minus] = even + odd, even - odd
    f[0] = m[0] - (m[7] + (m[8] + m[9])) + (m[16] + (m[17] + m[18]))
    return f


def equilibrium_of(density, u):
    ux, uy, uz = u
    rest = 1.0 - 1.5 * (ux * ux + uy * uy + uz * uz)
    eq = [None] * 19
    eq[0] = (1.0 / 3.0) * density * rest
    scale_axis, scale_diagonal = (1.0 / 18.0) * density, (1.0 / 36.0) * density
    for plus, minus, along, scale in (
        (1, 2, ux, scale_axis),
        (3, 4, uy, scale_axis),
        (5, 6, uz, scale_axis),
        (7, 8, ux + uy, scale_diagonal),
        (9, 10, ux - uy, scale_diagonal),
        (11, 12, ux + uz, scale_diagonal),
        (13, 14, ux - uz, scale_diagonal),
        (15, 16, uy + uz, scale_diagonal),
        (17, 18, uy - uz, scale_diagonal),
    ):
        even = rest + 4.5 * along * along
        odd = 3.0 * along
        eq[plus], eq[minus] = scale * (even + odd), scale * (even - odd)
    return eq


def shifted(plane, number):
    cx, cy, _ = SPEEDS[number]
    if cy:
        plane = pltpu.roll(plane, cy % plane.shape[1], 1)
    if cx:
        plane = pltpu.roll(plane, cx % plane.shape[0], 0)
    return plane


def edge(plane, number):
    width = plane.shape[0]
    return plane[0:1] if SPEEDS[number][0] > 0 else plane[width - 1 : width]


def even_device():
    return lax.axis_index("fluid") % 2 == 0


def begin_kernel(
    rates_ref,
    pops_hbm,
    slab_hbm,
    base_hbm,
    frac_hbm,
    atom_vel_hbm,
    fric_hbm,
    feat_hbm,
    mail_ref,
    rank_ref,
    vel_ref,
    axis_ref,
    calm_ref,
    near_ref,
    far_ref,
    side_ref,
    pops_ref,
    post_ref,
    slab_ref,
    base_ref,
    frac_ref,
    atom_vel_ref,
    fric_ref,
    sems,
):
    cells = pops_ref.shape[1]
    width = cells // 2
    feats = feat_hbm.shape[0]
    pairs = (
        (slab_hbm, slab_ref),
        (base_hbm, base_ref),
        (frac_hbm, frac_ref),
        (atom_vel_hbm, atom_vel_ref),
        (fric_hbm, fric_ref),
        (pops_hbm, pops_ref),
        (feat_hbm, near_ref.at[pl.ds(0, feats), :]),
        (feat_hbm, far_ref.at[pl.ds(0, feats), :]),
    )
    copies = [pltpu.make_async_copy(src, dst, sems.at[at]) for at, (src, dst) in enumerate(pairs)]
    for copy in copies:
        copy.start()
    for copy in copies[:5]:
        copy.wait()
    mail, rank = packed(slab_ref[...], base_ref[...], frac_ref, atom_vel_ref, fric_ref[...], mail_ref.shape[0])
    mail_ref[...] = mail
    rank_ref[...] = rank
    copies[5].wait()

    def chunk(step, carry):
        rows = pl.ds(pl.multiple_of(step * 8, 8), 8)
        f = [pops_ref[i, rows, :] for i in range(19)]
        low = moments_of(f)
        density = low[0]
        inverse = 1.0 / density
        u = [low[c] * inverse for c in (1, 2, 3)]
        for c in range(3):
            vel_ref[c, rows, :] = u[c]
        eq = equilibrium_of(density, u)
        m = moments_of([f[i] - eq[i] for i in range(19)])
        relaxed = populations_of([rates_ref[i] * m[i] for i in range(19)])
        for i in range(19):
            post_ref[i, rows, :] = f[i] - relaxed[i]
        return carry

    lax.fori_loop(0, cells // 8, chunk, 0)

    def plane(number, z):
        return shifted(post_ref[number, z * width : (z + 1) * width, :], number)

    axis_ref[...] = post_ref[1:7]
    edges = []
    for place, number in enumerate(CALM):
        if number in FLAT:
            for z in (0, 1):
                value = plane(number, z)
                calm_ref[place, z * width : (z + 1) * width, :] = value
                if number:
                    edges.append(edge(value, number))
    lanes = pops_ref.shape[2]
    leaving = []
    for numbers, stays in ((RISING, 1), (FALLING, 0)):
        leaving.append([])
        for number in numbers:
            value = plane(number, 1 - stays)
            calm_ref[CALM.index(number), stays * width : (stays + 1) * width, :] = value
            leaving[-1].append(plane(number, stays))
            if SPEEDS[number][0]:
                edges.append(edge(value, number))
    even = even_device()
    for place, (rises, falls) in enumerate(zip(*leaving)):
        cols = slice(place * lanes, (place + 1) * lanes)
        near_ref[feats : feats + width, cols] = jnp.where(even, rises, falls).astype(BF16)
        far_ref[feats : feats + width, cols] = jnp.where(even, falls, rises).astype(BF16)
    side_ref[...] = jnp.concatenate(edges + [jnp.zeros((16 - len(edges), lanes), F32)], axis=0)
    for copy in copies[6:]:
        copy.wait()


def begin(rates, pops, slab, base, frac, atom_vel, fric, feat, slabs):
    _, cells, lanes = pops.shape
    width = cells // 2
    feats, atoms = feat.shape
    vmem = pl.BlockSpec(memory_space=pltpu.VMEM)
    outside = [pltpu.with_memory_space_constraint(x, pltpu.HBM) for x in (pops, slab, base, frac, atom_vel, fric, feat)]
    return pl.pallas_call(
        begin_kernel,
        in_specs=[pl.BlockSpec(memory_space=pltpu.SMEM)] + [pl.BlockSpec(memory_space=pltpu.HBM)] * 7,
        out_specs=[vmem] * 8,
        out_shape=(
            jax.ShapeDtypeStruct((slabs, 128), F32),
            jax.ShapeDtypeStruct((1, atoms), F32),
            jax.ShapeDtypeStruct((3, cells, lanes), F32),
            jax.ShapeDtypeStruct((6, cells, lanes), F32),
            jax.ShapeDtypeStruct((13, cells, lanes), F32),
            jax.ShapeDtypeStruct((feats + width, 4 * lanes), BF16),
            jax.ShapeDtypeStruct((feats + width, 4 * lanes), BF16),
            jax.ShapeDtypeStruct((16, lanes), F32),
        ),
        scratch_shapes=[
            pltpu.VMEM((19, cells, lanes), F32),
            pltpu.VMEM((19, cells, lanes), F32),
            pltpu.VMEM((1, atoms), I32),
            pltpu.VMEM((1, atoms), I32),
            pltpu.VMEM((3, atoms), F32),
            pltpu.VMEM((3, atoms), F32),
            pltpu.VMEM((1, atoms), F32),
            pltpu.SemaphoreType.DMA((8,)),
        ],
        name="begin",
        compiler_params=pltpu.CompilerParams(vmem_limit_bytes=VMEM_LIMIT),
        cost_estimate=pl.CostEstimate(flops=400_000_000, bytes_accessed=6_000_000, transcendentals=0),
    )(rates, *outside)


def look_kernel(mail_ref, vel_ref, reply_ref, slot_ref, wy_hi, wy_lo):
    comps, cells, depth = vel_ref.shape
    width = cells // 2
    slots = mail_ref.shape[0]
    t = mail_ref[...].T
    field = lambda v: t[v * SLOTS : (v + 1) * SLOTS, :]
    fx, fy, fz = field(0), field(1), field(2)
    atom_vel = [field(3), field(4), field(5)]
    friction = field(6)
    base = field(7).astype(I32)
    x0 = (base // depth) % width
    y0 = base % depth
    y1 = (y0 + 1) % depth
    gx, gy, gz = 1.0 - fx, 1.0 - fy, 1.0 - fz
    row_y = iota((depth, slots), 0)
    row_x = iota((width, slots), 0)

    v_hi, v_lo = halves(vel_ref[...].reshape(comps * cells, depth))
    values = [[], [], []]
    for r in range(SLOTS):
        one = slice(r, r + 1)
        cols = slice(r * slots, (r + 1) * slots)
        wy = jnp.where(row_y == y0[one], gy[one], 0.0) + jnp.where(row_y == y1[one], fy[one], 0.0)
        wx = jnp.where(row_x == x0[one], gx[one], 0.0) + jnp.where(row_x == x0[one] + 1, fx[one], 0.0)
        hi, lo = halves(wy)
        wy_hi[:, cols] = hi
        wy_lo[:, cols] = lo
        seen = mm(v_hi, hi) + (mm(v_lo, hi) + mm(v_hi, lo))
        for c in range(3):
            close = seen[c * cells : c * cells + width]
            beyond = seen[c * cells + width : (c + 1) * cells]
            values[c].append(jnp.sum(wx * (close * gz[one] + beyond * fz[one]), axis=0, keepdims=True))
    rows = jnp.concatenate([row for c in range(3) for row in values[c]], axis=0)
    reply_ref[...] = jnp.concatenate([rows, jnp.zeros((128 - 3 * SLOTS, slots), F32)], axis=0).T
    slot_ref[0:SLOTS, :] = x0.astype(F32)
    slot_ref[SLOTS : 2 * SLOTS, :] = fx
    slot_ref[2 * SLOTS : 3 * SLOTS, :] = fz
    for c in range(3):
        pull = friction * (atom_vel[c] - rows[c * SLOTS : (c + 1) * SLOTS])
        slot_ref[(3 + c) * SLOTS : (4 + c) * SLOTS, :] = pull


def look(mail, vel):
    _, _, depth = vel.shape
    slabs = mail.shape[0]
    return pl.pallas_call(
        look_kernel,
        out_shape=(
            jax.ShapeDtypeStruct((slabs, 128), F32),
            jax.ShapeDtypeStruct((6 * SLOTS, slabs), F32),
            jax.ShapeDtypeStruct((depth, SLOTS * slabs), BF16),
            jax.ShapeDtypeStruct((depth, SLOTS * slabs), BF16),
        ),
        name="look",
        compiler_params=pltpu.CompilerParams(vmem_limit_bytes=VMEM_LIMIT),
        cost_estimate=pl.CostEstimate(flops=500_000_000, bytes_accessed=1_000_000, transcendentals=0),
    )(mail, vel)


def halos(near_ref, far_ref, width):
    lanes = near_ref.shape[1] // 4
    even = even_device()
    below, above = [], []
    for place in range(4):
        cols = slice(place * lanes, (place + 1) * lanes)
        near = near_ref[near_ref.shape[0] - width :, cols].astype(F32)
        far = far_ref[far_ref.shape[0] - width :, cols].astype(F32)
        below.append(jnp.where(even, far, near))
        above.append(jnp.where(even, near, far))
    return below, above


def push_kernel(
    axis_ref,
    slot_ref,
    wy_hi,
    wy_lo,
    early_ref,
    near_ref,
    far_ref,
    moved_ref,
    late_near_ref,
    late_far_ref,
    side_ref,
    force_ref,
    a_hi,
    a_lo,
):
    cells = axis_ref.shape[1]
    width = cells // 2
    slots = slot_ref.shape[1]
    row_x = iota((width, slots), 0)
    for r in range(SLOTS):
        cols = slice(r * slots, (r + 1) * slots)
        row = lambda v: slot_ref[v * SLOTS + r : v * SLOTS + r + 1, :]
        x0, fx, fz = row(0).astype(I32), row(1), row(2)
        wx = jnp.where(row_x == x0, 1.0 - fx, 0.0) + jnp.where(row_x == x0 + 1, fx, 0.0)
        for c in range(3):
            for z, weight in ((0, 1.0 - fz), (1, fz)):
                hi, lo = halves(wx * (weight * row(3 + c)))
                start = c * cells + z * width
                a_hi[start : start + width, cols] = hi
                a_lo[start : start + width, cols] = lo
    for c in (2, 0, 1):
        rows = slice(c * cells, (c + 1) * cells)
        force_ref[c] = mm_nt(a_hi[rows], wy_hi[...]) + (mm_nt(a_lo[rows], wy_hi[...]) + mm_nt(a_hi[rows], wy_lo[...]))
    edges = []
    for number in (5, 6, 1, 2, 3, 4):
        place = number - 1
        sign = 0.5 if number % 2 else -0.5
        for z in (0, 1):
            rows = slice(z * width, (z + 1) * width)
            value = shifted(axis_ref[place, rows, :] + sign * force_ref[place // 2, rows, :], number)
            if number == 5:
                if z == 1:
                    rises = value
                moved_ref[place, (1 - z) * width : (2 - z) * width, :] = value
            elif number == 6:
                if z == 0:
                    falls = value
                moved_ref[place, (1 - z) * width : (2 - z) * width, :] = value
            else:
                moved_ref[place, rows, :] = value
                if number in (1, 2):
                    edges.append(edge(value, number))
    even = even_device()
    late_near_ref[...] = jnp.where(even, rises, falls)
    late_far_ref[...] = jnp.where(even, falls, rises)
    for planes, numbers in zip(halos(near_ref, far_ref, width), (RISING, FALLING)):
        for plane, number in zip(planes, numbers):
            if SPEEDS[number][0]:
                edges.append(edge(plane, number))
    side_ref[0:16, :] = early_ref[...]
    side_ref[16:24, :] = jnp.concatenate(edges, axis=0)


def push(axis, slot, wy_hi, wy_lo, early, near, far):
    _, cells, lanes = axis.shape
    slots = wy_hi.shape[1]
    width = cells // 2
    return pl.pallas_call(
        push_kernel,
        out_shape=(
            jax.ShapeDtypeStruct((6, cells, lanes), F32),
            jax.ShapeDtypeStruct((width, lanes), F32),
            jax.ShapeDtypeStruct((width, lanes), F32),
            jax.ShapeDtypeStruct((24, lanes), F32),
        ),
        scratch_shapes=[
            pltpu.VMEM((3, cells, lanes), F32),
            pltpu.VMEM((3 * cells, slots), BF16),
            pltpu.VMEM((3 * cells, slots), BF16),
        ],
        name="push",
        compiler_params=pltpu.CompilerParams(vmem_limit_bytes=VMEM_LIMIT),
        cost_estimate=pl.CostEstimate(flops=500_000_000, bytes_accessed=1_500_000, transcendentals=0),
    )(axis, slot, wy_hi, wy_lo, early, near, far)


def gather_kernel(calm_ref, moved_ref, near_ref, far_ref, side_ref, late_near_ref, late_far_ref, out_ref):
    cells = calm_ref.shape[1]
    width = cells // 2

    def put(number, z, at):
        row = z * width + (0 if SPEEDS[number][0] > 0 else width - 1)
        out_ref[number, row : row + 1, :] = side_ref[at : at + 1, :]

    for place, number in enumerate(CALM):
        if number in FLAT:
            out_ref[number] = calm_ref[place]
    for place in range(4):
        out_ref[place + 1] = moved_ref[place]
    even = even_device()
    out_ref[5, width:, :] = moved_ref[4, width:, :]
    out_ref[5, :width, :] = jnp.where(even, late_far_ref[...], late_near_ref[...])
    out_ref[6, :width, :] = moved_ref[5, :width, :]
    out_ref[6, width:, :] = jnp.where(even, late_near_ref[...], late_far_ref[...])
    at, corner = 0, 20
    for number in FLAT[1:]:
        for z in (0, 1):
            put(number, z, at)
            at += 1
    below, above = halos(near_ref, far_ref, width)
    for arrived, numbers, stays in ((below, RISING, 1), (above, FALLING, 0)):
        for place, number in enumerate(numbers):
            kept, new = stays * width, (1 - stays) * width
            out_ref[number, kept : kept + width, :] = calm_ref[CALM.index(number), kept : kept + width, :]
            out_ref[number, new : new + width, :] = arrived[place]
            if SPEEDS[number][0]:
                put(number, stays, at)
                put(number, 1 - stays, corner)
                at += 1
                corner += 1
    for number in (1, 2):
        for z in (0, 1):
            put(number, z, 16 + 2 * (number - 1) + z)


def gather(calm, moved, near, far, side, late_near, late_far):
    _, cells, lanes = calm.shape
    return pl.pallas_call(
        gather_kernel,
        out_shape=jax.ShapeDtypeStruct((19, cells, lanes), F32),
        name="gather",
        compiler_params=pltpu.CompilerParams(vmem_limit_bytes=VMEM_LIMIT),
        cost_estimate=pl.CostEstimate(flops=1_000, bytes_accessed=3_000_000, transcendentals=0),
    )(calm, moved, near, far, side, late_near, late_far)


def finish_kernel(reply_ref, slab_ref, rank_ref, vel_ref, fric_ref, pull_ref, force_ref):
    slabs, atoms = reply_ref.shape[0], slab_ref.shape[1]
    one_hot = jnp.where(iota((slabs, atoms), 0) == slab_ref[...], 1.0, 0.0).astype(BF16)
    high, low = halves(reply_ref[...].T[: 3 * SLOTS])
    picked = mm(high, one_hot) + mm(low, one_hot)
    mine = iota((SLOTS, atoms), 0).astype(F32) == rank_ref[...]
    for c in range(3):
        seen = jnp.sum(jnp.where(mine, picked[c * SLOTS : (c + 1) * SLOTS], 0.0), axis=0, keepdims=True)
        drag = fric_ref[...] * (seen - vel_ref[c : c + 1, :])
        force_ref[c : c + 1, :] = pull_ref[c : c + 1, :] + drag


def finish(reply, slab, rank, vel, fric, pull):
    atoms = slab.shape[1]
    return pl.pallas_call(
        finish_kernel,
        out_shape=jax.ShapeDtypeStruct((3, atoms), F32),
        name="finish",
        compiler_params=pltpu.CompilerParams(vmem_limit_bytes=VMEM_LIMIT),
        cost_estimate=pl.CostEstimate(flops=20_000_000, bytes_accessed=100_000, transcendentals=0),
    )(reply, slab, rank, vel, fric, pull)


def potential_kernel(
    near_ref,
    own_ref,
    far_ref,
    nbr_ref,
    bond_ref,
    w_self_ref,
    w_nbr_ref,
    w_rbf_ref,
    w_out_ref,
    force_ref,
    new_ref,
    table,
    own_half,
):
    feats, atoms = own_ref.shape
    count, basis = nbr_ref.shape[0], w_rbf_ref.shape[1]
    block = 256
    above = jnp.where(even_device(), 2 * feats, 0)
    for start, ref in ((above, near_ref), (feats, own_ref), (2 * feats - above, far_ref)):
        value = mm(w_nbr_ref[...], ref[0:feats, :]).astype(BF16)
        rows = pl.ds(start if isinstance(start, int) else pl.multiple_of(start, feats), feats)
        table[rows, :] = (value.astype(F32) * 0.5).astype(BF16)
    own_half[...] = 0.5 * mm(w_self_ref[...], own_ref[...])
    rbf_hi, rbf_lo = halves(0.5 * w_rbf_ref[...])
    rbf = jnp.concatenate([rbf_hi, rbf_lo, rbf_hi], axis=1)
    spacing = RADIAL_REACH / (basis - 1)
    centers = iota((basis, block), 0).astype(F32) * spacing
    w_out = w_out_ref[...]
    rows = iota((atoms, block), 0)

    def one(part, carry):
        cols = pl.ds(pl.multiple_of(part * block, block), block)
        total, force = None, None
        for k in range(count):
            nbr = nbr_ref[k : k + 1, cols]
            place = nbr // atoms
            one_hot = jnp.where(rows == nbr % atoms, 1.0, 0.0).astype(BF16)
            bond = [bond_ref[c, k : k + 1, cols] for c in range(3)]
            length = jnp.sqrt(bond[0] * bond[0] + bond[1] * bond[1] + bond[2] * bond[2] + 1e-6)
            scaled = (length - centers) * (1.0 / spacing)
            rad_hi, rad_lo = halves(jnp.exp(-scaled * scaled))
            radial = jnp.concatenate([rad_hi, rad_hi, rad_lo], axis=0)
            seen = mm(table[...], one_hot)
            picked = jnp.where(
                place == 0, seen[:feats], jnp.where(place == 1, seen[feats : 2 * feats], seen[2 * feats :])
            )
            half = own_half[:, cols] + picked + mm(rbf, radial)
            hidden = half + half * jnp.tanh(half)
            scalar = jnp.sum(hidden * w_out, axis=0, keepdims=True)
            terms = [scalar * b for b in bond]
            total = hidden if total is None else total + hidden
            force = terms if force is None else [f + t for f, t in zip(force, terms)]
        for c in range(3):
            force_ref[c : c + 1, cols] = force[c]
        new_ref[:, cols] = (own_ref[:, cols].astype(F32) + total * (1.0 / count)).astype(BF16)
        return carry

    lax.fori_loop(0, atoms // block, one, 0)


def potential(near, own, far, nbrs, bonds, w_self, w_nbr, w_rbf, w_out):
    feats, atoms = own.shape
    return pl.pallas_call(
        potential_kernel,
        out_shape=(
            jax.ShapeDtypeStruct((3, atoms), F32),
            jax.ShapeDtypeStruct((feats, atoms), BF16),
        ),
        scratch_shapes=[
            pltpu.VMEM((3 * feats, atoms), BF16),
            pltpu.VMEM((feats, atoms), F32),
        ],
        name="potential",
        compiler_params=pltpu.CompilerParams(vmem_limit_bytes=VMEM_LIMIT),
        cost_estimate=pl.CostEstimate(flops=1_000_000, bytes_accessed=100_000, transcendentals=0),
    )(near, own, far, nbrs, bonds, w_self, w_nbr, w_rbf, w_out)


def body(
    slabs,
    populations,
    relax_rates,
    slab,
    stencil_base,
    frac,
    atom_vel,
    friction,
    features,
    neighbors,
    bonds,
    w_self,
    w_nbr,
    w_rbf,
    w_out,
):
    _, planes, width, depth = populations.shape
    atoms = slab.shape[0]
    chip = [(i, i ^ 1) for i in range(slabs)]
    link = [(i, (i - 1 if i % 2 == 0 else i + 1) % slabs) for i in range(slabs)]
    across = [(0, 1), (1, 0)]
    slab_row = slab.reshape(1, atoms)
    friction_row = friction.reshape(1, atoms)

    mail, rank, vel, axis, calm, near, far, side = begin(
        relax_rates,
        populations.reshape(19, planes * width, depth),
        slab_row,
        stencil_base.reshape(1, atoms),
        frac,
        atom_vel,
        friction_row,
        features,
        slabs,
    )
    mail = lax.all_to_all(mail.reshape(slabs, 1, 128), "fluid", split_axis=0, concat_axis=0, tiled=True)
    far = lax.ppermute(far, "fluid", link)
    near = lax.ppermute(near, "fluid", chip)
    pull, new_features = potential(
        near,
        features,
        far,
        neighbors.T,
        bonds.transpose(0, 2, 1),
        w_self,
        w_nbr,
        w_rbf,
        w_out.reshape(-1, 1),
    )
    mail, pull = lax.optimization_barrier((mail, pull))

    reply, slot, wy_hi, wy_lo = look(mail.reshape(slabs, 128), vel)
    reply = lax.all_to_all(reply.reshape(slabs, 1, 128), "fluid", split_axis=0, concat_axis=0, tiled=True)
    moved, late_near, late_far, side = push(axis, slot, wy_hi, wy_lo, side, near, far)
    side = lax.ppermute(side, "group", across)
    late_far = lax.ppermute(late_far, "fluid", link)
    late_near = lax.ppermute(late_near, "fluid", chip)
    pops = gather(calm, moved, near, far, side, late_near, late_far)
    atom_force = finish(reply.reshape(slabs, 128), slab_row, rank, atom_vel, friction_row, pull)
    return pops.reshape(populations.shape), atom_force, new_features


def solution(mesh):
    in_specs = (
        P(None, "fluid", "group", None),
        P(),
        P(("fluid", "group"), None),
        P(("fluid", "group")),
        P(None, ("fluid", "group")),
        P(None, ("fluid", "group")),
        P(("fluid", "group")),
        P(None, ("fluid", "group")),
        P(("fluid", "group"), None),
        P(None, ("fluid", "group"), None),
        P(),
        P(),
        P(),
        P(),
    )
    out_specs = (
        P(None, "fluid", "group", None),
        P(None, ("fluid", "group")),
        P(None, ("fluid", "group")),
    )
    return jax.shard_map(
        functools.partial(body, mesh.shape["fluid"]),
        mesh=mesh,
        in_specs=in_specs,
        out_specs=out_specs,
        check_vma=False,
    )
```

time: 73 us -> 55.1 us (0.75)
  starting transfers between devices: 51.6 us -> 29.9 us
  waiting for transfers between devices: 0.03 us -> 8.94 us
  local copies, waits for them, and re-layouts: 3.8 us -> 0.97 us
  Pallas kernels: 16.5 us -> 14.2 us
    ppermute x9 -> x4, starting transfers between devices: 28.1 us -> 15.3 us  [the longest x1 8.87 us: body(): far = lax.ppermute(far, 'fluid', link)]
    all_to_all x1, starting transfers between devices: 13.9 us -> 6.19 us  [body(): lax.all_to_all(mail.reshape(slabs, 1, 128), 'fluid', split_axis=0, concat...]
    ppermute x1, waiting for transfers between devices: 0.01 us -> 4.6 us  [body(): side = lax.ppermute(side, 'group', across)]
    all_to_all x1, waiting for transfers between devices: 0.01 us -> 4.33 us  [body(): lax.all_to_all(mail.reshape(slabs, 1, 128), 'fluid', split_axis=0, concat...]
    pallas_call x1, Pallas kernels: 8.59 us -> 5.74 us  [potential(): pl.pallas_call(potential_kernel, out_shape=(jax.ShapeDtypeStruct((3, atom...]
    unnamed x35 -> x23, local copies, waits for them, and re-layouts: 3.68 us -> 0.86 us
    all_to_all x1, starting transfers between devices: 8.87 us -> 7.91 us  [body(): lax.all_to_all(reply.reshape(slabs, 1, 128), 'fluid', split_axis=0, conca...]
    pallas_call x1, Pallas kernels: 0.1 us -> 1.03 us  [push(): pl.pallas_call(push_kernel, out_shape=(jax.ShapeDtypeStruct((6, cells, la...]
  transfers between devices with their start and end apart: 12 -> 7, of which waited for: 0 -> 2; matrix products, arithmetic and copies ran while one was open for 0% -> 0% of each run, Pallas kernels for 19% -> 14%
where the time goes in v2:
time: 55.1 us; the launch traced here: 54.9 us
  starting transfers between devices  29.9 us (54%)
  Pallas kernels  14.2 us (26%)
  waiting for transfers between devices  8.94 us (16%)
  local copies, waits for them, and re-layouts  0.97 us (2%)
  between operations  0.82 us (1%)
    ppermute x1, starting transfers between devices, body(): far = lax.ppermute(far, 'fluid', link)  8.87 us
    all_to_all x1, starting transfers between devices, body(): lax.all_to_all(reply.reshape(slabs, 1, 128), 'fluid', split_axis=0, conca...  7.91 us
    ppermute x1, starting transfers between devices, body(): late_far = lax.ppermute(late_far, 'fluid', link)  6.2 us
    all_to_all x1, starting transfers between devices, body(): lax.all_to_all(mail.reshape(slabs, 1, 128), 'fluid', split_axis=0, concat...  6.19 us
    pallas_call x1, Pallas kernels, potential(): pl.pallas_call(potential_kernel, out_shape=(jax.ShapeDtypeStruct((3, atom...  5.74 us
    ppermute x1, waiting for transfers between devices, body(): side = lax.ppermute(side, 'group', across)  4.6 us
    all_to_all x1, waiting for transfers between devices, body(): lax.all_to_all(mail.reshape(slabs, 1, 128), 'fluid', split_axis=0, concat...  4.33 us
    pallas_call x1, Pallas kernels, begin(): pl.pallas_call(begin_kernel, in_specs=[pl.BlockSpec(memory_space=pltpu.SM...  3.8 us
  transfers between devices with their start and end apart: 7, of which 2 were waited for; matrix products, arithmetic and copies ran while one was open for 0% of the time, Pallas kernels for 14%

profile of v2, /device:TPU:16, one launch (start us, length us, event | category | flops | bytes accessed | tf_op | source)
XLA Modules:
  0.0 54.9 jit_solution(11892160914571975720)
XLA Ops:
  0.6 0.0 copy-start
  0.6 0.0 copy-start.4
  0.7 0.0 copy-start.3
  0.7 0.0 copy-start.1
  0.7 0.0 copy-start.2
  0.7 0.0 copy-start.8
  0.7 0.7 %copy-done.8 = f32[19]{0:T(128)S(1)} copy-done((f32[19]{0:T(128)S(1)}, f32[19]{0:T(128)}, u32[]{:S(2)}) %copy-start.8) | copy-done | bytes 100
  1.4 3.8 %begin.1 = (f32[128,128]{1,0:T(8,128)}, f32[1,512]{1,0:T(1,128)S(1)}, f32[3,128,128]{2,1,0:T(8,128)S(1)}, f32[6,128,128]{2,1,0:T(8,128)S(1)}, f32[13,128,128]{2,...) custom-call(f32[19]{0:T(128)S(1)} %copy-done.8, ...), custom_call_target="tpu_custom_call" | custom-call | flops 400000000 | bytes 6000000 | tf_op jit(solution)/shard_map/begin/pallas_call | solution.py:281
  5.2 0.1 collective-permute-start
  5.3 8.9 %collective-permute-start.1 = (bf16[192,512]{1,0:T(8,128)(2,1)S(1)}, bf16[192,512]{1,0:T(8,128)(2,1)S(1)}, u32[]{:S(2)}, u32[]{:S(2)}) collective-permute-start(bf16[192,512]{1,0:T(8,128)(2,1)S(1)} %get-tuple-element.27), channel_id=1, source_target_pairs={{0,254},{2,4},{4,2},{6,8},{8,6},{10,12},{12,10},{14,16},{16,14},{1... | collective-permute-start | bytes 589832 | tf_op jit(solution)/shard_map/ppermute | solution.py:659
  14.2 6.2 %all-to-all-start = ((f32[128,1,128]{2,1,0:T(1,128)}), f32[128,1,128]{2,1,0:T(1,128)S(1)}, u32[]{:S(2)}, u32[]{:S(2)}) async-start(f32[128,1,128]{2,1,0:T(1,128)} %bitcast.5), calls=%async_computation | async-start | bytes 131072 | tf_op jit(solution)/shard_map/all_to_all | solution.py:658
  20.4 0.0 copy-done.9
  20.4 0.1 copy.20.w_rbf_ref
  20.5 0.1 copy.21.w_out_ref
  20.6 0.0 collective-permute-done.near_ref
  20.6 0.0 collective-permute-done.1.far_ref
  20.7 5.7 %potential.1 = (f32[3,512]{1,0:T(4,128)S(1)}, bf16[128,512]{1,0:T(8,128)(2,1)}) custom-call(bf16[192,512]{1,0:T(8,128)(2,1)S(1)} %collective-permute-done.near_ref, bf16[128,512]{1,0:T(8,128)(2,1)S(1)} %copy-done, bf16[192,512]{1,0:T(8,128)(2,1)S(1)} %collective-permute-done.1.far_ref, s32[16,512]{1,0:T(8,128)S(1)} %bitcast.19, f32[3,16,512]{2,1,0:T(8,128)S(1)} %bitcast.17, ...), custom_call_target="tpu_custom_call" | custom-call | flops 1000000 | bytes 100000 | tf_op jit(solution)/shard_map/potential/pallas_call | solution.py:606
  26.4 4.3 %all-to-all-done = f32[128,1,128]{2,1,0:T(1,128)S(1)} async-done(((f32[128,1,128]{2,1,0:T(1,128)}), f32[128,1,128]{2,1,0:T(1,128)S(1)}, u32[]{:S(2)}, u32[]{:S(2)}) %all-to-all-start) | async-done | bytes 65568 | tf_op jit(solution)/shard_map/all_to_all | solution.py:658
  30.8 1.6 %look.1 = (f32[128,128]{1,0:T(8,128)}, f32[48,128]{1,0:T(8,128)S(1)}, bf16[128,1024]{1,0:T(8,128)(2,1)S(1)}, bf16[128,1024]{1,0:T(8,128)(2,1)S(1)}) custom-call(f32[128,128]{1,0:T(8,128)S(1)} %bitcast.18, f32[3,128,128]{2,1,0:T(8,128)S(1)} %get-tuple-element.30.vel_ref), custom_call_target="tpu_custom_call" | custom-call | flops 500000000 | bytes 1000000 | tf_op jit(solution)/shard_map/look/pallas_call | solution.py:356
  32.4 7.9 %all-to-all-start.1 = ((f32[128,1,128]{2,1,0:T(1,128)}), f32[128,1,128]{2,1,0:T(1,128)S(1)}, u32[]{:S(2)}, u32[]{:S(2)}) async-start(f32[128,1,128]{2,1,0:T(1,128)} %bitcast.12), calls=%async_computation.1 | async-start | bytes 131072 | tf_op jit(solution)/shard_map/all_to_all | solution.py:675
  40.3 1.0 %push.1 = (f32[6,128,128]{2,1,0:T(8,128)S(1)}, f32[64,128]{1,0:T(8,128)S(1)}, f32[64,128]{1,0:T(8,128)S(1)}, f32[24,128]{1,0:T(8,128)S(1)}) custom-call(f32[6,128,128]{2,1,0:T(8,128)S(1)} %get-tuple-element.24.axis_ref, f32[48,128]{1,0:T(8,128)S(1)} %get-tuple-element.31.slot_ref, bf16[128,1024]{1,0:T(8,128)(2,1)S(1)} %get-tuple-element.32.wy_hi, ...), custom_call_target="tpu_custom_call" | custom-call | flops 500000000 | bytes 1500000 | tf_op jit(solution)/shard_map/push/pallas_call | solution.py:451
  41.3 0.1 collective-permute-start.3
  41.4 6.2 %collective-permute-start.4 = (f32[64,128]{1,0:T(8,128)S(1)}, f32[64,128]{1,0:T(8,128)S(1)}, u32[]{:S(2)}, u32[]{:S(2)}) collective-permute-start(f32[64,128]{1,0:T(8,128)S(1)} %get-tuple-element.38), channel_id=1, source_target_pairs={{0,254},{2,4},{4,2},{6,8},{8,6},{10,12},{12,10},{14,16},{16,14},{1... | collective-permute-start | bytes 98312 | tf_op jit(solution)/shard_map/ppermute | solution.py:678
  47.6 0.6 %collective-permute-start.2 = (f32[24,128]{1,0:T(8,128)S(1)}, f32[24,128]{1,0:T(8,128)S(1)}, u32[]{:S(2)}, u32[]{:S(2)}) collective-permute-start(f32[24,128]{1,0:T(8,128)S(1)} %get-tuple-element.36), channel_id=1, source_target_pairs={{0,1},{1,0},{2,3},{3,2},{4,5},{5,4},{6,7},{7,6},{8,9},{9,8},{10,11... | collective-permute-start | bytes 36872 | tf_op jit(solution)/shard_map/ppermute | solution.py:677
  48.2 4.6 %collective-permute-done.2.side_ref = f32[24,128]{1,0:T(8,128)S(1)} collective-permute-done((f32[24,128]{1,0:T(8,128)S(1)}, f32[24,128]{1,0:T(8,128)S(1)}, u32[]{:S(2)}, u32[]{:S(2)}) %collective-permute-start.2) | collective-permute-done | bytes 12320 | tf_op jit(solution)/shard_map/ppermute | solution.py:677
  52.8 0.0 collective-permute-done.3.late_near_ref
  52.8 0.0 collective-permute-done.4.late_far_ref
  52.9 0.0 copy-start.6
  52.9 0.0 copy-start.7
  52.9 1.1 %gather.1 = f32[19,128,128]{2,1,0:T(8,128)} custom-call(f32[13,128,128]{2,1,0:T(8,128)S(1)} %get-tuple-element.23.calm_ref, f32[6,128,128]{2,1,0:T(8,128)S(1)} %get-tuple-element.35.moved_ref, bf16[192,512]{1,0:T(8,128)(2,1)S(1)} %collective-permute-done.near_ref, bf16[192,512]{1,0:T(8,128)(2,1)S(1)} %collective-permute-done.1.far_ref, ...), custom_call_target="tpu_custom_call" | custom-call | flops 1000 | bytes 3000000 | tf_op jit(solution)/shard_map/gather/pallas_call | solution.py:511
  54.0 0.0 all-to-all-done.1
  54.0 0.8 %finish.1 = f32[3,512]{1,0:T(4,128)} custom-call(f32[128,128]{1,0:T(8,128)S(1)} %bitcast.16, s32[1,512]{1,0:T(1,128)S(1)} %bitcast.21, f32[1,512]{1,0:T(1,128)S(1)} %get-tuple-element.40.rank_ref, f32[3,512]{1,0:T(4,128)S(1)} %copy-done.5, f32[1,512]{1,0:T(1,128)S(1)} %bitcast.23, f32[3,512]{1,0:T(4,128)S(1)} %get-tuple-element.41.pull_ref), custom_call_target="tpu_custom_call" | custom-call | flops 20000000 | bytes 100000 | tf_op jit(solution)/shard_map/finish/pallas_call | solution.py:534
  (12 shorter events, 0.0 us)
Async XLA Ops:
  0.6 20.0 %copy-start = (bf16[128,512]{1,0:T(8,128)(2,1)S(1)}, bf16[128,512]{1,0:T(8,128)(2,1)}, u32[]{:S(2)}) copy-start(bf16[128,512]{1,0:T(8,128)(2,1)} %own_ref.1) | copy-start | bytes 393220
  0.6 20.0 %copy-start.4 = (bf16[128,128]{1,0:T(8,128)(2,1)S(1)}, bf16[128,128]{1,0:T(8,128)(2,1)}, u32[]{:S(2)}) copy-start(bf16[128,128]{1,0:T(8,128)(2,1)} %w_nbr_ref.1) | copy-start | bytes 98308
  0.7 20.0 %copy-start.3 = (bf16[128,128]{1,0:T(8,128)(2,1)S(1)}, bf16[128,128]{1,0:T(8,128)(2,1)}, u32[]{:S(2)}) copy-start(bf16[128,128]{1,0:T(8,128)(2,1)} %w_self_ref.1) | copy-start | bytes 98308
  0.7 20.0 %copy-start.1 = (f32[3,512,16]{1,2,0:T(8,128)S(1)}, f32[3,512,16]{1,2,0:T(8,128)}, u32[]{:S(2)}) copy-start(f32[3,512,16]{1,2,0:T(8,128)} %param.23) | copy-start | bytes 294916
  0.7 20.0 %copy-start.2 = (s32[512,16]{0,1:T(8,128)S(1)}, s32[512,16]{0,1:T(8,128)}, u32[]{:S(2)}) copy-start(s32[512,16]{0,1:T(8,128)} %param.22) | copy-start | bytes 98308
  0.7 0.7 %copy-start.8 = (f32[19]{0:T(128)S(1)}, f32[19]{0:T(128)}, u32[]{:S(2)}) copy-start(f32[19]{0:T(128)} %rates_ref.1) | copy-start | bytes 232
  1.4 19.0 %copy-start.9 = (f32[128,16]{0,1:T(8,128)S(1)}, f32[128,16]{0,1:T(8,128)}, u32[]{:S(2)}) copy-start(f32[128,16]{0,1:T(8,128)} %param.26) | copy-start | bytes 24580
  1.4 19.1 %copy-start.10 = (f32[128]{0:T(128)S(1)}, f32[128]{0:T(128)}, u32[]{:S(2)}) copy-start(f32[128]{0:T(128)} %param.27) | copy-start | bytes 1540
  5.2 15.4 %collective-permute-start = (bf16[192,512]{1,0:T(8,128)(2,1)S(1)}, bf16[192,512]{1,0:T(8,128)(2,1)S(1)}, u32[]{:S(2)}, u32[]{:S(2)}) collective-permute-start(bf16[192,512]{1,0:T(8,128)(2,1)S(1)} %get-tuple-element.26), channel_id=1, source_target_pairs={{0,2},{2,0},{4,6},{6,4},{8,10},{10,8},{12,14},{14,12},{16,18},{18,... | collective-permute-start | bytes 589832 | tf_op jit(solution)/shard_map/ppermute | solution.py:660
  5.3 15.3 %collective-permute-start.1 = (bf16[192,512]{1,0:T(8,128)(2,1)S(1)}, bf16[192,512]{1,0:T(8,128)(2,1)S(1)}, u32[]{:S(2)}, u32[]{:S(2)}) collective-permute-start(bf16[192,512]{1,0:T(8,128)(2,1)S(1)} %get-tuple-element.27), channel_id=1, source_target_pairs={{0,254},{2,4},{4,2},{6,8},{8,6},{10,12},{12,10},{14,16},{16,14},{1... | collective-permute-start | bytes 589832 | tf_op jit(solution)/shard_map/ppermute | solution.py:659
  14.2 16.6 %all-to-all-start = ((f32[128,1,128]{2,1,0:T(1,128)}), f32[128,1,128]{2,1,0:T(1,128)S(1)}, u32[]{:S(2)}, u32[]{:S(2)}) async-start(f32[128,1,128]{2,1,0:T(1,128)} %bitcast.5), calls=%async_computation | async-start | bytes 131072 | tf_op jit(solution)/shard_map/all_to_all | solution.py:658
  32.4 21.6 %all-to-all-start.1 = ((f32[128,1,128]{2,1,0:T(1,128)}), f32[128,1,128]{2,1,0:T(1,128)S(1)}, u32[]{:S(2)}, u32[]{:S(2)}) async-start(f32[128,1,128]{2,1,0:T(1,128)} %bitcast.12), calls=%async_computation.1 | async-start | bytes 131072 | tf_op jit(solution)/shard_map/all_to_all | solution.py:675
  41.3 11.5 %collective-permute-start.3 = (f32[64,128]{1,0:T(8,128)S(1)}, f32[64,128]{1,0:T(8,128)S(1)}, u32[]{:S(2)}, u32[]{:S(2)}) collective-permute-start(f32[64,128]{1,0:T(8,128)S(1)} %get-tuple-element.37), channel_id=1, source_target_pairs={{0,2},{2,0},{4,6},{6,4},{8,10},{10,8},{12,14},{14,12},{16,18},{18,... | collective-permute-start | bytes 98312 | tf_op jit(solution)/shard_map/ppermute | solution.py:679
  41.4 11.4 %collective-permute-start.4 = (f32[64,128]{1,0:T(8,128)S(1)}, f32[64,128]{1,0:T(8,128)S(1)}, u32[]{:S(2)}, u32[]{:S(2)}) collective-permute-start(f32[64,128]{1,0:T(8,128)S(1)} %get-tuple-element.38), channel_id=1, source_target_pairs={{0,254},{2,4},{4,2},{6,8},{8,6},{10,12},{12,10},{14,16},{16,14},{1... | collective-permute-start | bytes 98312 | tf_op jit(solution)/shard_map/ppermute | solution.py:678
  47.6 5.2 %collective-permute-start.2 = (f32[24,128]{1,0:T(8,128)S(1)}, f32[24,128]{1,0:T(8,128)S(1)}, u32[]{:S(2)}, u32[]{:S(2)}) collective-permute-start(f32[24,128]{1,0:T(8,128)S(1)} %get-tuple-element.36), channel_id=1, source_target_pairs={{0,1},{1,0},{2,3},{3,2},{4,5},{5,4},{6,7},{7,6},{8,9},{9,8},{10,11... | collective-permute-start | bytes 36872 | tf_op jit(solution)/shard_map/ppermute | solution.py:677
  52.8 1.2 %copy-start.5 = (f32[3,512]{1,0:T(4,128)S(1)}, f32[3,512]{1,0:T(4,128)}, u32[]{:S(2)}) copy-start(f32[3,512]{1,0:T(4,128)} %vel_ref.1) | copy-start | bytes 18436
  52.9 1.2 %copy-start.6 = (s32[512,1]{0,1:T(1,128)S(1)}, s32[512,1]{0,1:T(1,128)}, u32[]{:S(2)}) copy-start(s32[512,1]{0,1:T(1,128)} %param.16) | copy-start | bytes 6148
  52.9 1.2 %copy-start.7 = (f32[512]{0:T(512)S(1)}, f32[512]{0:T(512)}, u32[]{:S(2)}) copy-start(f32[512]{0:T(512)} %param.20) | copy-start | bytes 6148

commit v3 on v2

--- a/solution.py
+++ b/solution.py
@@ -41,6 +41,9 @@
 CALM = (0, 7, 8, 9, 10, 11, 12, 13, 14, 15, 16, 17, 18)
 
 VMEM_LIMIT = 48 * 1024 * 1024
+STREAM_FLOPS = 4_000_000_000
+FIRST_FLOPS = 3_500_000_000
+SECOND_FLOPS = 500_000_000
 
 
 def halves(value):
@@ -69,12 +72,11 @@
     return lax.broadcasted_iota(I32, shape, dim)
 
 
-def packed(slab, base, frac_ref, vel_ref, fric, slabs):
+def packed(slab, base, frac_ref, vel_ref, fric, slabs, earlier):
     atoms = slab.shape[1]
     named = iota((slabs, atoms), 0) == slab
     one_hot = jnp.where(named, 1.0, 0.0)
     one_hot_b = one_hot.astype(BF16)
-    earlier = jnp.where(iota((atoms, atoms), 0) < iota((atoms, atoms), 1), 1.0, 0.0).astype(BF16)
     before = mm(one_hot_b, earlier)
     rank = jnp.sum(one_hot * before, axis=0, keepdims=True)
     mine = iota((SLOTS, atoms), 0).astype(F32) == rank
@@ -82,7 +84,6 @@
     rows += [vel_ref[c : c + 1, :] for c in range(3)]
     rows += [fric, base.astype(F32)]
     spread = [jnp.where(mine, row, 0.0) for row in rows]
-    spread.append(jnp.zeros((128 - SLOTS * len(rows), atoms), F32))
     high, middle, low = thirds(jnp.concatenate(spread, axis=0))
     return mm_nt(one_hot_b, high) + (mm_nt(one_hot_b, middle) + mm_nt(one_hot_b, low)), rank
 
@@ -169,58 +170,65 @@
     return plane[0:1] if SPEEDS[number][0] > 0 else plane[width - 1 : width]
 
 
-def even_device():
-    return lax.axis_index("fluid") % 2 == 0
-
-
-def begin_kernel(
-    rates_ref,
-    pops_hbm,
-    slab_hbm,
-    base_hbm,
-    frac_hbm,
-    atom_vel_hbm,
-    fric_hbm,
-    feat_hbm,
-    mail_ref,
-    rank_ref,
-    vel_ref,
-    axis_ref,
-    calm_ref,
-    near_ref,
-    far_ref,
-    side_ref,
-    pops_ref,
-    post_ref,
-    slab_ref,
-    base_ref,
-    frac_ref,
-    atom_vel_ref,
-    fric_ref,
-    sems,
+def pack_kernel(
+    slab_hbm, base_hbm, frac_hbm, vel_hbm, fric_hbm, mail_ref, rank_ref, slab_ref, base_ref, frac_ref, vel_ref, fric_ref, sems
 ):
-    cells = pops_ref.shape[1]
-    width = cells // 2
-    feats = feat_hbm.shape[0]
     pairs = (
         (slab_hbm, slab_ref),
         (base_hbm, base_ref),
         (frac_hbm, frac_ref),
-        (atom_vel_hbm, atom_vel_ref),
+        (vel_hbm, vel_ref),
         (fric_hbm, fric_ref),
-        (pops_hbm, pops_ref),
-        (feat_hbm, near_ref.at[pl.ds(0, feats), :]),
-        (feat_hbm, far_ref.at[pl.ds(0, feats), :]),
     )
     copies = [pltpu.make_async_copy(src, dst, sems.at[at]) for at, (src, dst) in enumerate(pairs)]
     for copy in copies:
         copy.start()
-    for copy in copies[:5]:
+    atoms = slab_ref.shape[1]
+    earlier = jnp.where(iota((atoms, atoms), 0) < iota((atoms, atoms), 1), 1.0, 0.0).astype(BF16)
+    for copy in copies:
         copy.wait()
-    mail, rank = packed(slab_ref[...], base_ref[...], frac_ref, atom_vel_ref, fric_ref[...], mail_ref.shape[0])
-    mail_ref[...] = mail
+    mail, rank = packed(
+        slab_ref[...], base_ref[...], frac_ref, vel_ref, fric_ref[...], mail_ref.shape[0], earlier
+    )
+    filled = mail.shape[1]
+    mail_ref[:, :filled] = mail
+    mail_ref[:, filled:] = jnp.zeros((mail.shape[0], mail_ref.shape[1] - filled), F32)
     rank_ref[...] = rank
-    copies[5].wait()
+
+
+def pack(slab, base, frac, vel, fric, slabs):
+    atoms = slab.shape[1]
+    vmem = pl.BlockSpec(memory_space=pltpu.VMEM)
+    outside = [pltpu.with_memory_space_constraint(x, pltpu.HBM) for x in (slab, base, frac, vel, fric)]
+    return pl.pallas_call(
+        pack_kernel,
+        in_specs=[pl.BlockSpec(memory_space=pltpu.HBM)] * 5,
+        out_specs=[vmem] * 2,
+        out_shape=(
+            jax.ShapeDtypeStruct((slabs, 128), F32),
+            jax.ShapeDtypeStruct((1, atoms), F32),
+        ),
+        scratch_shapes=[
+            pltpu.VMEM((1, atoms), I32),
+            pltpu.VMEM((1, atoms), I32),
+            pltpu.VMEM((3, atoms), F32),
+            pltpu.VMEM((3, atoms), F32),
+            pltpu.VMEM((1, atoms), F32),
+            pltpu.SemaphoreType.DMA((5,)),
+        ],
+        name="pack",
+        compiler_params=pltpu.CompilerParams(vmem_limit_bytes=VMEM_LIMIT),
+        cost_estimate=pl.CostEstimate(flops=400_000_000, bytes_accessed=4_000_000, transcendentals=0),
+    )(*outside)
+
+
+def even_device():
+    return lax.axis_index("fluid") % 2 == 0
+
+
+def relax_kernel(rates_ref, pops_ref, rest_ref, axis_ref, vel_ref, near_ref, far_ref):
+    cells = pops_ref.shape[1]
+    width = cells // 2
 
     def chunk(step, carry):
         rows = pl.ds(pl.multiple_of(step * 8, 8), 8)
@@ -235,15 +243,31 @@
         m = moments_of([f[i] - eq[i] for i in range(19)])
         relaxed = populations_of([rates_ref[i] * m[i] for i in range(19)])
         for i in range(19):
-            post_ref[i, rows, :] = f[i] - relaxed[i]
+            if i in CALM:
+                rest_ref[CALM.index(i), rows, :] = f[i] - relaxed[i]
+            else:
+                axis_ref[i - 1, rows, :] = f[i] - relaxed[i]
         return carry
 
     lax.fori_loop(0, cells // 8, chunk, 0)
 
+    lanes = pops_ref.shape[2]
+    even = even_device()
+    for place, (rising, falling) in enumerate(zip(RISING, FALLING)):
+        cols = slice(place * lanes, (place + 1) * lanes)
+        rises = shifted(rest_ref[CALM.index(rising), width:, :], rising)
+        falls = shifted(rest_ref[CALM.index(falling), :width, :], falling)
+        near_ref[:, cols] = jnp.where(even, rises, falls).astype(BF16)
+        far_ref[:, cols] = jnp.where(even, falls, rises).astype(BF16)
+
+
+def stream_kernel(rest_ref, calm_ref, side_ref):
+    cells, lanes = rest_ref.shape[1:]
+    width = cells // 2
+
     def plane(number, z):
-        return shifted(post_ref[number, z * width : (z + 1) * width, :], number)
-
-    axis_ref[...] = post_ref[1:7]
+        return shifted(rest_ref[CALM.index(number), z * width : (z + 1) * width, :], number)
+
     edges = []
     for place, number in enumerate(CALM):
         if number in FLAT:
@@ -252,60 +276,48 @@
                 calm_ref[place, z * width : (z + 1) * width, :] = value
                 if number:
                     edges.append(edge(value, number))
-    lanes = pops_ref.shape[2]
-    leaving = []
     for numbers, stays in ((RISING, 1), (FALLING, 0)):
-        leaving.append([])
         for number in numbers:
             value = plane(number, 1 - stays)
             calm_ref[CALM.index(number), stays * width : (stays + 1) * width, :] = value
-            leaving[-1].append(plane(number, stays))
             if SPEEDS[number][0]:
                 edges.append(edge(value, number))
-    even = even_device()
-    for place, (rises, falls) in enumerate(zip(*leaving)):
-        cols = slice(place * lanes, (place + 1) * lanes)
-        near_ref[feats : feats + width, cols] = jnp.where(even, rises, falls).astype(BF16)
-        far_ref[feats : feats + width, cols] = jnp.where(even, falls, rises).astype(BF16)
     side_ref[...] = jnp.concatenate(edges + [jnp.zeros((16 - len(edges), lanes), F32)], axis=0)
-    for copy in copies[6:]:
-        copy.wait()
-
-
-def begin(rates, pops, slab, base, frac, atom_vel, fric, feat, slabs):
+
+
+def stream(rest):
+    _, cells, lanes = rest.shape
+    return pl.pallas_call(
+        stream_kernel,
+        out_shape=(
+            jax.ShapeDtypeStruct((13, cells, lanes), F32),
+            jax.ShapeDtypeStruct((16, lanes), F32),
+        ),
+        name="stream",
+        compiler_params=pltpu.CompilerParams(vmem_limit_bytes=VMEM_LIMIT),
+        cost_estimate=pl.CostEstimate(flops=STREAM_FLOPS, bytes_accessed=100_000, transcendentals=0),
+    )(rest)
+
+
+def relax(rates, pops):
     _, cells, lanes = pops.shape
     width = cells // 2
-    feats, atoms = feat.shape
     vmem = pl.BlockSpec(memory_space=pltpu.VMEM)
-    outside = [pltpu.with_memory_space_constraint(x, pltpu.HBM) for x in (pops, slab, base, frac, atom_vel, fric, feat)]
     return pl.pallas_call(
-        begin_kernel,
-        in_specs=[pl.BlockSpec(memory_space=pltpu.SMEM)] + [pl.BlockSpec(memory_space=pltpu.HBM)] * 7,
-        out_specs=[vmem] * 8,
+        relax_kernel,
+        in_specs=[pl.BlockSpec(memory_space=pltpu.SMEM), vmem],
+        out_specs=[vmem] * 5,
         out_shape=(
-            jax.ShapeDtypeStruct((slabs, 128), F32),
-            jax.ShapeDtypeStruct((1, atoms), F32),
+            jax.ShapeDtypeStruct((13, cells, lanes), F32),
+            jax.ShapeDtypeStruct((6, cells, lanes), F32),
             jax.ShapeDtypeStruct((3, cells, lanes), F32),
-            jax.ShapeDtypeStruct((6, cells, lanes), F32),
-            jax.ShapeDtypeStruct((13, cells, lanes), F32),
-            jax.ShapeDtypeStruct((feats + width, 4 * lanes), BF16),
-            jax.ShapeDtypeStruct((feats + width, 4 * lanes), BF16),
-            jax.ShapeDtypeStruct((16, lanes), F32),
+            jax.ShapeDtypeStruct((width, 4 * lanes), BF16),
+            jax.ShapeDtypeStruct((width, 4 * lanes), BF16),
         ),
-        scratch_shapes=[
-            pltpu.VMEM((19, cells, lanes), F32),
-            pltpu.VMEM((19, cells, lanes), F32),
-            pltpu.VMEM((1, atoms), I32),
-            pltpu.VMEM((1, atoms), I32),
-            pltpu.VMEM((3, atoms), F32),
-            pltpu.VMEM((3, atoms), F32),
-            pltpu.VMEM((1, atoms), F32),
-            pltpu.SemaphoreType.DMA((8,)),
-        ],
-        name="begin",
+        name="relax",
         compiler_params=pltpu.CompilerParams(vmem_limit_bytes=VMEM_LIMIT),
-        cost_estimate=pl.CostEstimate(flops=400_000_000, bytes_accessed=6_000_000, transcendentals=0),
-    )(rates, *outside)
+        cost_estimate=pl.CostEstimate(flops=10_000_000, bytes_accessed=6_000_000, transcendentals=0),
+    )(rates, pops)
 
 
 def look_kernel(mail_ref, vel_ref, reply_ref, slot_ref, wy_hi, wy_lo):
@@ -367,14 +379,14 @@
     )(mail, vel)
 
 
-def halos(near_ref, far_ref, width):
+def halos(near_ref, far_ref):
     lanes = near_ref.shape[1] // 4
     even = even_device()
     below, above = [], []
     for place in range(4):
         cols = slice(place * lanes, (place + 1) * lanes)
-        near = near_ref[near_ref.shape[0] - width :, cols].astype(F32)
-        far = far_ref[far_ref.shape[0] - width :, cols].astype(F32)
+        near = near_ref[:, cols].astype(F32)
+        far = far_ref[:, cols].astype(F32)
         below.append(jnp.where(even, far, near))
         above.append(jnp.where(even, near, far))
     return below, above
@@ -436,7 +448,7 @@
     even = even_device()
     late_near_ref[...] = jnp.where(even, rises, falls)
     late_far_ref[...] = jnp.where(even, falls, rises)
-    for planes, numbers in zip(halos(near_ref, far_ref, width), (RISING, FALLING)):
+    for planes, numbers in zip(halos(near_ref, far_ref), (RISING, FALLING)):
         for plane, number in zip(planes, numbers):
             if SPEEDS[number][0]:
                 edges.append(edge(plane, number))
@@ -490,7 +502,7 @@
         for z in (0, 1):
             put(number, z, at)
             at += 1
-    below, above = halos(near_ref, far_ref, width)
+    below, above = halos(near_ref, far_ref)
     for arrived, numbers, stays in ((below, RISING, 1), (above, FALLING, 0)):
         for place, number in enumerate(numbers):
             kept, new = stays * width, (1 - stays) * width
@@ -540,7 +552,41 @@
     )(reply, slab, rank, vel, fric, pull)
 
 
-def potential_kernel(
+def message(table, own_half, rbf, w_out, nbrs, bonds, spacing, basis):
+    feats, block = own_half.shape
+    atoms = table.shape[1]
+    centers = iota((basis, block), 0).astype(F32) * spacing
+    rows = iota((atoms, block), 0)
+    total, force = None, None
+    for nbr, bond in zip(nbrs, bonds):
+        place = nbr // atoms
+        one_hot = jnp.where(rows == nbr % atoms, 1.0, 0.0).astype(BF16)
+        length = jnp.sqrt(bond[0] * bond[0] + bond[1] * bond[1] + bond[2] * bond[2] + 1e-6)
+        scaled = (length - centers) * (1.0 / spacing)
+        rad_hi, rad_lo = halves(jnp.exp(-scaled * scaled))
+        radial = jnp.concatenate([rad_hi, rad_hi, rad_lo, jnp.zeros((feats - 3 * basis, block), BF16)], axis=0)
+        seen = mm(table[...], one_hot)
+        picked = jnp.where(place == 0, seen[:feats], jnp.where(place == 1, seen[feats : 2 * feats], seen[2 * feats :]))
+        half = own_half + picked + mm(rbf, radial)
+        hidden = half + half * jnp.tanh(half)
+        scalar = jnp.sum(hidden * w_out, axis=0, keepdims=True)
+        terms = [scalar * b for b in bond]
+        total = hidden if total is None else total + hidden
+        force = terms if force is None else [f + t for f, t in zip(force, terms)]
+    return total, force
+
+
+def potential_table(near_ref, own_ref, far_ref, w_self_ref, w_nbr_ref, table, own_half):
+    feats = own_ref.shape[0]
+    above = jnp.where(even_device(), 2 * feats, 0)
+    for start, ref in ((above, near_ref), (feats, own_ref), (2 * feats - above, far_ref)):
+        value = mm(w_nbr_ref[...], ref[...]).astype(BF16)
+        rows = pl.ds(start if isinstance(start, int) else pl.multiple_of(start, feats), feats)
+        table[rows, :] = (value.astype(F32) * 0.5).astype(BF16)
+    own_half[...] = 0.5 * mm(w_self_ref[...], own_ref[...])
+
+
+def potential_first_kernel(
     near_ref,
     own_ref,
     far_ref,
@@ -555,68 +601,75 @@
     table,
     own_half,
 ):
-    feats, atoms = own_ref.shape
-    count, basis = nbr_ref.shape[0], w_rbf_ref.shape[1]
-    block = 256
-    above = jnp.where(even_device(), 2 * feats, 0)
-    for start, ref in ((above, near_ref), (feats, own_ref), (2 * feats - above, far_ref)):
-        value = mm(w_nbr_ref[...], ref[0:feats, :]).astype(BF16)
-        rows = pl.ds(start if isinstance(start, int) else pl.multiple_of(start, feats), feats)
-        table[rows, :] = (value.astype(F32) * 0.5).astype(BF16)
-    own_half[...] = 0.5 * mm(w_self_ref[...], own_ref[...])
+    potential_table(near_ref, own_ref, far_ref, w_self_ref, w_nbr_ref, table, own_half)
+    potential_block(0, own_ref, nbr_ref, bond_ref, w_rbf_ref, w_out_ref, table, own_half, force_ref, new_ref)
+
+
+def potential_block(start, own_ref, nbr_ref, bond_ref, w_rbf_ref, w_out_ref, table_ref, half_ref, force_ref, new_ref):
+    block = force_ref.shape[1] - start
+    count, basis = nbr_ref.shape[0], w_rbf_ref.shape[0]
+    cols = slice(start, start + block)
+    feats = own_ref.shape[0]
     rbf_hi, rbf_lo = halves(0.5 * w_rbf_ref[...])
-    rbf = jnp.concatenate([rbf_hi, rbf_lo, rbf_hi], axis=1)
-    spacing = RADIAL_REACH / (basis - 1)
-    centers = iota((basis, block), 0).astype(F32) * spacing
-    w_out = w_out_ref[...]
-    rows = iota((atoms, block), 0)
-
-    def one(part, carry):
-        cols = pl.ds(pl.multiple_of(part * block, block), block)
-        total, force = None, None
-        for k in range(count):
-            nbr = nbr_ref[k : k + 1, cols]
-            place = nbr // atoms
-            one_hot = jnp.where(rows == nbr % atoms, 1.0, 0.0).astype(BF16)
-            bond = [bond_ref[c, k : k + 1, cols] for c in range(3)]
-            length = jnp.sqrt(bond[0] * bond[0] + bond[1] * bond[1] + bond[2] * bond[2] + 1e-6)
-            scaled = (length - centers) * (1.0 / spacing)
-            rad_hi, rad_lo = halves(jnp.exp(-scaled * scaled))
-            radial = jnp.concatenate([rad_hi, rad_hi, rad_lo], axis=0)
-            seen = mm(table[...], one_hot)
-            picked = jnp.where(
-                place == 0, seen[:feats], jnp.where(place == 1, seen[feats : 2 * feats], seen[2 * feats :])
-            )
-            half = own_half[:, cols] + picked + mm(rbf, radial)
-            hidden = half + half * jnp.tanh(half)
-            scalar = jnp.sum(hidden * w_out, axis=0, keepdims=True)
-            terms = [scalar * b for b in bond]
-            total = hidden if total is None else total + hidden
-            force = terms if force is None else [f + t for f, t in zip(force, terms)]
-        for c in range(3):
-            force_ref[c : c + 1, cols] = force[c]
-        new_ref[:, cols] = (own_ref[:, cols].astype(F32) + total * (1.0 / count)).astype(BF16)
-        return carry
-
-    lax.fori_loop(0, atoms // block, one, 0)
-
-
-def potential(near, own, far, nbrs, bonds, w_self, w_nbr, w_rbf, w_out):
-    feats, atoms = own.shape
+    rbf_hi, rbf_lo = rbf_hi.astype(F32), rbf_lo.astype(F32)
+    rest = jnp.zeros((feats - 3 * basis, feats), F32)
+    rbf = jnp.concatenate([rbf_hi, rbf_lo, rbf_hi, rest], axis=0).T.astype(BF16)
+    w_out = jnp.broadcast_to(w_out_ref[...], (8, feats)).T[:, 0:1]
+    total, force = message(
+        table_ref,
+        half_ref[:, cols],
+        rbf,
+        w_out,
+        [nbr_ref[k : k + 1, cols] for k in range(count)],
+        [[bond_ref[c, k : k + 1, cols] for c in range(3)] for k in range(count)],
+        RADIAL_REACH / (basis - 1),
+        basis,
+    )
+    for c in range(3):
+        force_ref[c : c + 1, cols] = force[c]
+    new_ref[:, cols] = (own_ref[:, cols].astype(F32) + total * (1.0 / count)).astype(BF16)
+
+
+def potential_second_kernel(
+    near_ref,
+    own_ref,
+    far_ref,
+    nbr_ref,
+    bond_ref,
+    w_self_ref,
+    w_nbr_ref,
+    w_rbf_ref,
+    w_out_ref,
+    first_force_ref,
+    first_new_ref,
+    force_ref,
+    new_ref,
+    table,
+    own_half,
+):
+    half = first_new_ref.shape[1]
+    force_ref[:, :half] = first_force_ref[...]
+    new_ref[:, :half] = first_new_ref[...]
+    potential_table(near_ref, own_ref, far_ref, w_self_ref, w_nbr_ref, table, own_half)
+    potential_block(half, own_ref, nbr_ref, bond_ref, w_rbf_ref, w_out_ref, table, own_half, force_ref, new_ref)
+
+
+def potential(kernel, name, columns, flops, *args):
+    feats, atoms = args[1].shape
     return pl.pallas_call(
-        potential_kernel,
+        kernel,
         out_shape=(
-            jax.ShapeDtypeStruct((3, atoms), F32),
-            jax.ShapeDtypeStruct((feats, atoms), BF16),
+            jax.ShapeDtypeStruct((3, columns), F32),
+            jax.ShapeDtypeStruct((feats, columns), BF16),
         ),
         scratch_shapes=[
             pltpu.VMEM((3 * feats, atoms), BF16),
             pltpu.VMEM((feats, atoms), F32),
         ],
-        name="potential",
+        name=name,
         compiler_params=pltpu.CompilerParams(vmem_limit_bytes=VMEM_LIMIT),
-        cost_estimate=pl.CostEstimate(flops=1_000_000, bytes_accessed=100_000, transcendentals=0),
-    )(near, own, far, nbrs, bonds, w_self, w_nbr, w_rbf, w_out)
+        cost_estimate=pl.CostEstimate(flops=flops, bytes_accessed=100_000, transcendentals=0),
+    )(*args)
 
 
 def body(
@@ -644,32 +697,19 @@
     slab_row = slab.reshape(1, atoms)
     friction_row = friction.reshape(1, atoms)
 
-    mail, rank, vel, axis, calm, near, far, side = begin(
-        relax_rates,
-        populations.reshape(19, planes * width, depth),
-        slab_row,
-        stencil_base.reshape(1, atoms),
-        frac,
-        atom_vel,
-        friction_row,
-        features,
-        slabs,
-    )
+    mail, rank = pack(slab_row, stencil_base.reshape(1, atoms), frac, atom_vel, friction_row, slabs)
+    sent = features
+    near_features = lax.ppermute(sent, "fluid", chip)
+    far_features = lax.ppermute(sent, "fluid", link)
     mail = lax.all_to_all(mail.reshape(slabs, 1, 128), "fluid", split_axis=0, concat_axis=0, tiled=True)
+    rest, axis, vel, near, far = relax(relax_rates, populations.reshape(19, planes * width, depth))
+    calm, side = stream(rest)
     far = lax.ppermute(far, "fluid", link)
     near = lax.ppermute(near, "fluid", chip)
-    pull, new_features = potential(
-        near,
-        features,
-        far,
-        neighbors.T,
-        bonds.transpose(0, 2, 1),
-        w_self,
-        w_nbr,
-        w_rbf,
-        w_out.reshape(-1, 1),
-    )
-    mail, pull = lax.optimization_barrier((mail, pull))
+    nbrs, bonds, w_rbf, w_out = neighbors.T, bonds.transpose(0, 2, 1), w_rbf.T, w_out.reshape(1, -1)
+    around = (near_features, features, far_features, nbrs, bonds, w_self, w_nbr, w_rbf, w_out)
+    first_pull, first_new = potential(potential_first_kernel, "potential_first", atoms // 2, FIRST_FLOPS, *around)
+    mail, first_pull, side = lax.optimization_barrier((mail, first_pull, side))
 
     reply, slot, wy_hi, wy_lo = look(mail.reshape(slabs, 128), vel)
     reply = lax.all_to_all(reply.reshape(slabs, 1, 128), "fluid", split_axis=0, concat_axis=0, tiled=True)
@@ -677,6 +717,10 @@
     side = lax.ppermute(side, "group", across)
     late_far = lax.ppermute(late_far, "fluid", link)
     late_near = lax.ppermute(late_near, "fluid", chip)
+    first_pull, moved = lax.optimization_barrier((first_pull, moved))
+    pull, new_features = potential(
+        potential_second_kernel, "potential_second", atoms, SECOND_FLOPS, *around, first_pull, first_new
+    )
     pops = gather(calm, moved, near, far, side, late_near, late_far)
     atom_force = finish(reply.reshape(slabs, 128), slab_row, rank, atom_vel, friction_row, pull)
     return pops.reshape(populations.shape), atom_force, new_features

time: 55.1 us -> 52.3 us (0.949)
  waiting for transfers between devices: 8.94 us -> 0.02 us
  starting transfers between devices: 29.9 us -> 36.1 us
    ppermute x0 -> x2, starting transfers between devices: none -> 8.3 us  [the longest x1 8.3 us: body(): far_features = lax.ppermute(sent, 'fluid', link)]
    ppermute x1, waiting for transfers between devices: 4.6 us -> 0.01 us  [body(): side = lax.ppermute(side, 'group', across)]
    all_to_all x1, waiting for transfers between devices: 4.33 us -> 0.01 us  [body(): lax.all_to_all(mail.reshape(slabs, 1, 128), 'fluid', split_axis=0, concat...]
    ppermute x1, starting transfers between devices: 8.87 us -> 6.2 us  [body(): far = lax.ppermute(far, 'fluid', link)]
    all_to_all x1, starting transfers between devices: 6.19 us -> 7.17 us  [body(): lax.all_to_all(mail.reshape(slabs, 1, 128), 'fluid', split_axis=0, concat...]
    all_to_all x1, starting transfers between devices: 7.91 us -> 7.08 us  [body(): lax.all_to_all(reply.reshape(slabs, 1, 128), 'fluid', split_axis=0, conca...]
    ppermute x1, starting transfers between devices: 6.2 us -> 6.81 us  [body(): late_far = lax.ppermute(late_far, 'fluid', link)]
    pallas_call x2 -> x5, Pallas kernels: 9.54 us -> 9.75 us  [the longest x2 5.98 us: potential(): pl.pallas_call(kernel, out_shape=(jax.ShapeDtypeStruct((3, columns), F32)...]
  transfers between devices with their start and end apart: 7 -> 9, of which waited for: 2 -> 0; matrix products, arithmetic and copies ran while one was open for 0% -> 0% of each run, Pallas kernels for 14% -> 26%
where the time goes in v3:
time: 52.3 us; the launch traced here: 52.1 us
  starting transfers between devices  36.1 us (69%)
  Pallas kernels  14.4 us (28%)
  between operations  0.83 us (2%)
  local copies, waits for them, and re-layouts  0.78 us (1%)
    ppermute x1, starting transfers between devices, body(): far_features = lax.ppermute(sent, 'fluid', link)  8.3 us
    all_to_all x1, starting transfers between devices, body(): lax.all_to_all(mail.reshape(slabs, 1, 128), 'fluid', split_axis=0, concat...  7.17 us
    all_to_all x1, starting transfers between devices, body(): lax.all_to_all(reply.reshape(slabs, 1, 128), 'fluid', split_axis=0, conca...  7.08 us
    ppermute x1, starting transfers between devices, body(): late_far = lax.ppermute(late_far, 'fluid', link)  6.81 us
    ppermute x1, starting transfers between devices, body(): far = lax.ppermute(far, 'fluid', link)  6.2 us
    pallas_call x2, Pallas kernels, potential(): pl.pallas_call(kernel, out_shape=(jax.ShapeDtypeStruct((3, columns), F32)...  5.98 us
    pallas_call x1, Pallas kernels, pack(): pl.pallas_call(pack_kernel, in_specs=[pl.BlockSpec(memory_space=pltpu.HBM...  1.98 us
    pallas_call x1, Pallas kernels, look(): pl.pallas_call(look_kernel, out_shape=(jax.ShapeDtypeStruct((slabs, 128),...  1.64 us
  transfers between devices with their start and end apart: 9, of which 0 were waited for; matrix products, arithmetic and copies ran while one was open for 0% of the time, Pallas kernels for 26%

profile of v3, /device:TPU:16, one launch (start us, length us, event | category | flops | bytes accessed | tf_op | source)
XLA Modules:
  0.0 52.1 jit_solution(11424206690356870280)
XLA Ops:
  0.7 8.3 %collective-permute-start.1 = (bf16[128,512]{1,0:T(8,128)(2,1)}, bf16[128,512]{1,0:T(8,128)(2,1)S(1)}, u32[]{:S(2)}, u32[]{:S(2)}) collective-permute-start(bf16[128,512]{1,0:T(8,128)(2,1)} %own_ref.3), channel_id=1, source_target_pairs={{0,254},{2,4},{4,2},{6,8},{8,6},{10,12},{12,10},{14,16},{16,14},{1... | collective-permute-start | bytes 393224 | tf_op jit(solution)/shard_map/ppermute | solution.py:703
  8.9 0.0 collective-permute-start
  8.9 2.0 %pack.1 = (f32[128,128]{1,0:T(8,128)}, f32[1,512]{1,0:T(1,128)S(1)}) custom-call(s32[1,512]{1,0:T(1,128)} %bitcast.20, s32[1,512]{1,0:T(1,128)} %bitcast.33, f32[3,512]{1,0:T(4,128)} %frac_hbm.1, f32[3,512]{1,0:T(4,128)} %vel_ref.1, f32[1,512]{1,0:T(1,128)} %bitcast.22), custom_call_target="tpu_custom_call" | custom-call | flops 400000000 | bytes 4000000 | tf_op jit(solution)/shard_map/pack/pallas_call | solution.py:203
  10.9 7.2 %all-to-all-start = ((f32[128,1,128]{2,1,0:T(1,128)}), f32[128,1,128]{2,1,0:T(1,128)S(1)}, u32[]{:S(2)}, u32[]{:S(2)}) async-start(f32[128,1,128]{2,1,0:T(1,128)} %bitcast.5), calls=%async_computation | async-start | bytes 131072 | tf_op jit(solution)/shard_map/all_to_all | solution.py:704
  18.1 1.6 %relax.1 = (f32[13,128,128]{2,1,0:T(8,128)S(1)}, f32[6,128,128]{2,1,0:T(8,128)S(1)}, f32[3,128,128]{2,1,0:T(8,128)S(1)}, bf16[64,512]{1,0:T(8,128)(2,1)S(1)}, bf16[64,512]{1,0:T(8,128)(2,1)S(1)}) custom-call(f32[19]{0:T(128)S(1)} %copy-done.4, f32[19,128,128]{2,1,0:T(8,128)S(1)} %bitcast.17), custom_call_target="tpu_custom_call" | custom-call | flops 10000000 | bytes 6000000 | tf_op jit(solution)/shard_map/relax/pallas_call | solution.py:306
  19.8 0.1 collective-permute-start.2
  19.9 6.2 %collective-permute-start.3 = (bf16[64,512]{1,0:T(8,128)(2,1)S(1)}, bf16[64,512]{1,0:T(8,128)(2,1)S(1)}, u32[]{:S(2)}, u32[]{:S(2)}) collective-permute-start(bf16[64,512]{1,0:T(8,128)(2,1)S(1)} %get-tuple-element.43), channel_id=1, source_target_pairs={{0,254},{2,4},{4,2},{6,8},{8,6},{10,12},{12,10},{14,16},{16,14},{1... | collective-permute-start | bytes 196616 | tf_op jit(solution)/shard_map/ppermute | solution.py:707
  26.1 0.0 copy-start.9
  26.1 0.0 copy-start.10
  26.1 0.0 copy-start.11
  26.1 0.2 stream.1
  26.3 0.0 collective-permute-done.1.far_ref
  26.3 0.0 collective-permute-done.near_ref
  26.3 0.7 %copy-done.5 = bf16[128,512]{1,0:T(8,128)(2,1)S(1)} copy-done((bf16[128,512]{1,0:T(8,128)(2,1)S(1)}, bf16[128,512]{1,0:T(8,128)(2,1)}, u32[]{:S(2)}) %copy-start.5) | copy-done | bytes 131096
  27.0 0.1 copy-done.6
  27.0 2.7 %potential_first.1 = (f32[3,256]{1,0:T(4,128)S(1)}, bf16[128,256]{1,0:T(8,128)(2,1)S(1)}) custom-call(bf16[128,512]{1,0:T(8,128)(2,1)S(1)} %collective-permute-done.near_ref, bf16[128,512]{1,0:T(8,128)(2,1)S(1)} %copy-done.5, bf16[128,512]{1,0:T(8,128)(2,1)S(1)} %collective-permute-done.1.far_ref, s32[16,512]{1,0:T(8,128)S(1)} %bitcast.26, ...), custom_call_target="tpu_custom_call" | custom-call | flops 3500000000 | bytes 100000 | tf_op jit(solution)/shard_map/potential_first/pallas_call | solution.py:659
  29.7 0.0 all-to-all-done
  29.7 1.6 %look.1 = (f32[128,128]{1,0:T(8,128)}, f32[48,128]{1,0:T(8,128)S(1)}, bf16[128,1024]{1,0:T(8,128)(2,1)S(1)}, bf16[128,1024]{1,0:T(8,128)(2,1)S(1)}) custom-call(f32[128,128]{1,0:T(8,128)S(1)} %bitcast.19, f32[3,128,128]{2,1,0:T(8,128)S(1)} %get-tuple-element.37.vel_ref), custom_call_target="tpu_custom_call" | custom-call | flops 500000000 | bytes 1000000 | tf_op jit(solution)/shard_map/look/pallas_call | solution.py:368
  31.4 7.1 %all-to-all-start.1 = ((f32[128,1,128]{2,1,0:T(1,128)}), f32[128,1,128]{2,1,0:T(1,128)S(1)}, u32[]{:S(2)}, u32[]{:S(2)}) async-start(f32[128,1,128]{2,1,0:T(1,128)} %bitcast.13), calls=%async_computation.1 | async-start | bytes 131072 | tf_op jit(solution)/shard_map/all_to_all | solution.py:715
  38.4 0.0 collective-permute-done.2.near_ref
  38.5 0.0 collective-permute-done.3.far_ref
  38.5 1.0 %push.1 = (f32[6,128,128]{2,1,0:T(8,128)S(1)}, f32[64,128]{1,0:T(8,128)S(1)}, f32[64,128]{1,0:T(8,128)S(1)}, f32[24,128]{1,0:T(8,128)S(1)}) custom-call(f32[6,128,128]{2,1,0:T(8,128)S(1)} %get-tuple-element.35.axis_ref, f32[48,128]{1,0:T(8,128)S(1)} %get-tuple-element.38.slot_ref, bf16[128,1024]{1,0:T(8,128)(2,1)S(1)} %get-tuple-element.39.wy_hi, ...), custom_call_target="tpu_custom_call" | custom-call | flops 500000000 | bytes 1500000 | tf_op jit(solution)/shard_map/push/pallas_call | solution.py:463
  39.5 0.4 collective-permute-start.4
  39.9 0.0 collective-permute-start.5
  39.9 6.8 %collective-permute-start.6 = (f32[64,128]{1,0:T(8,128)S(1)}, f32[64,128]{1,0:T(8,128)S(1)}, u32[]{:S(2)}, u32[]{:S(2)}) collective-permute-start(f32[64,128]{1,0:T(8,128)S(1)} %get-tuple-element.48), channel_id=1, source_target_pairs={{0,254},{2,4},{4,2},{6,8},{8,6},{10,12},{12,10},{14,16},{16,14},{1... | collective-permute-start | bytes 98312 | tf_op jit(solution)/shard_map/ppermute | solution.py:718
  46.7 3.3 %potential_second.1 = (f32[3,512]{1,0:T(4,128)S(1)}, bf16[128,512]{1,0:T(8,128)(2,1)}) custom-call(bf16[128,512]{1,0:T(8,128)(2,1)S(1)} %collective-permute-done.near_ref, bf16[128,512]{1,0:T(8,128)(2,1)S(1)} %copy-done.5, bf16[128,512]{1,0:T(8,128)(2,1)S(1)} %collective-permute-done.1.far_ref, s32[16,512]{1,0:T(8,128)S(1)} %bitcast.27, ...), custom_call_target="tpu_custom_call" | custom-call | flops 500000000 | bytes 100000 | tf_op jit(solution)/shard_map/potential_second/pallas_call | solution.py:659
  50.0 0.0 collective-permute-done.6.late_far_ref
  50.1 0.0 copy-start.1
  50.1 0.0 copy-start.2
  50.1 0.0 copy-start.3
  50.1 1.1 %gather.1 = f32[19,128,128]{2,1,0:T(8,128)} custom-call(f32[13,128,128]{2,1,0:T(8,128)S(1)} %get-tuple-element.30.calm_ref, f32[6,128,128]{2,1,0:T(8,128)S(1)} %get-tuple-element.45.moved_ref, bf16[64,512]{1,0:T(8,128)(2,1)S(1)} %collective-permute-done.2.near_ref, bf16[64,512]{1,0:T(8,128)(2,1)S(1)} %collective-permute-done.3.far_ref, ...), custom_call_target="tpu_custom_call" | custom-call | flops 1000 | bytes 3000000 | tf_op jit(solution)/shard_map/gather/pallas_call | solution.py:523
  51.2 0.8 %finish.1 = f32[3,512]{1,0:T(4,128)} custom-call(f32[128,128]{1,0:T(8,128)S(1)} %bitcast.18, s32[1,512]{1,0:T(1,128)S(1)} %bitcast.21, f32[1,512]{1,0:T(1,128)S(1)} %get-tuple-element.50.rank_ref, f32[3,512]{1,0:T(4,128)S(1)} %copy-done.1, f32[1,512]{1,0:T(1,128)S(1)} %bitcast.23, f32[3,512]{1,0:T(4,128)S(1)} %get-tuple-element.53.pull_ref), custom_call_target="tpu_custom_call" | custom-call | flops 20000000 | bytes 100000 | tf_op jit(solution)/shard_map/finish/pallas_call | solution.py:546
  (19 shorter events, 0.0 us)
Async XLA Ops:
  0.6 17.5 %copy-start.4 = (f32[19]{0:T(128)S(1)}, f32[19]{0:T(128)}, u32[]{:S(2)}) copy-start(f32[19]{0:T(128)} %rates_ref.1) | copy-start | bytes 232
  0.6 17.5 %copy-start = (f32[19,2,64,128]{3,2,1,0:T(8,128)S(1)}, f32[19,2,64,128]{3,2,1,0:T(8,128)}, u32[]{:S(2)}) copy-start(f32[19,2,64,128]{3,2,1,0:T(8,128)} %param.14) | copy-start | bytes 3735556
  0.7 25.6 %collective-permute-start.1 = (bf16[128,512]{1,0:T(8,128)(2,1)}, bf16[128,512]{1,0:T(8,128)(2,1)S(1)}, u32[]{:S(2)}, u32[]{:S(2)}) collective-permute-start(bf16[128,512]{1,0:T(8,128)(2,1)} %own_ref.3), channel_id=1, source_target_pairs={{0,254},{2,4},{4,2},{6,8},{8,6},{10,12},{12,10},{14,16},{16,14},{1... | collective-permute-start | bytes 393224 | tf_op jit(solution)/shard_map/ppermute | solution.py:703
  8.9 17.3 %collective-permute-start = (bf16[128,512]{1,0:T(8,128)(2,1)}, bf16[128,512]{1,0:T(8,128)(2,1)S(1)}, u32[]{:S(2)}, u32[]{:S(2)}) collective-permute-start(bf16[128,512]{1,0:T(8,128)(2,1)} %own_ref.3), channel_id=1, source_target_pairs={{0,2},{2,0},{4,6},{6,4},{8,10},{10,8},{12,14},{14,12},{16,18},{18,... | collective-permute-start | bytes 393224 | tf_op jit(solution)/shard_map/ppermute | solution.py:702
  10.9 18.8 %all-to-all-start = ((f32[128,1,128]{2,1,0:T(1,128)}), f32[128,1,128]{2,1,0:T(1,128)S(1)}, u32[]{:S(2)}, u32[]{:S(2)}) async-start(f32[128,1,128]{2,1,0:T(1,128)} %bitcast.5), calls=%async_computation | async-start | bytes 131072 | tf_op jit(solution)/shard_map/all_to_all | solution.py:704
  19.8 18.7 %collective-permute-start.2 = (bf16[64,512]{1,0:T(8,128)(2,1)S(1)}, bf16[64,512]{1,0:T(8,128)(2,1)S(1)}, u32[]{:S(2)}, u32[]{:S(2)}) collective-permute-start(bf16[64,512]{1,0:T(8,128)(2,1)S(1)} %get-tuple-element.42), channel_id=1, source_target_pairs={{0,2},{2,0},{4,6},{6,4},{8,10},{10,8},{12,14},{14,12},{16,18},{18,... | collective-permute-start | bytes 196616 | tf_op jit(solution)/shard_map/ppermute | solution.py:708
  19.9 18.6 %collective-permute-start.3 = (bf16[64,512]{1,0:T(8,128)(2,1)S(1)}, bf16[64,512]{1,0:T(8,128)(2,1)S(1)}, u32[]{:S(2)}, u32[]{:S(2)}) collective-permute-start(bf16[64,512]{1,0:T(8,128)(2,1)S(1)} %get-tuple-element.43), channel_id=1, source_target_pairs={{0,254},{2,4},{4,2},{6,8},{8,6},{10,12},{12,10},{14,16},{16,14},{1... | collective-permute-start | bytes 196616 | tf_op jit(solution)/shard_map/ppermute | solution.py:707
  26.1 0.9 %copy-start.5 = (bf16[128,512]{1,0:T(8,128)(2,1)S(1)}, bf16[128,512]{1,0:T(8,128)(2,1)}, u32[]{:S(2)}) copy-start(bf16[128,512]{1,0:T(8,128)(2,1)} %own_ref.3) | copy-start | bytes 393220
  26.1 1.0 %copy-start.6 = (f32[3,512,16]{1,2,0:T(8,128)S(1)}, f32[3,512,16]{1,2,0:T(8,128)}, u32[]{:S(2)}) copy-start(f32[3,512,16]{1,2,0:T(8,128)} %param.23) | copy-start | bytes 294916
  26.1 1.0 %copy-start.7 = (s32[512,16]{0,1:T(8,128)S(1)}, s32[512,16]{0,1:T(8,128)}, u32[]{:S(2)}) copy-start(s32[512,16]{0,1:T(8,128)} %param.22) | copy-start | bytes 98308
  26.1 1.0 %copy-start.8 = (bf16[128,128]{1,0:T(8,128)(2,1)S(1)}, bf16[128,128]{1,0:T(8,128)(2,1)}, u32[]{:S(2)}) copy-start(bf16[128,128]{1,0:T(8,128)(2,1)} %w_self_ref.3) | copy-start | bytes 98308
  26.1 1.0 %copy-start.9 = (bf16[128,128]{1,0:T(8,128)(2,1)S(1)}, bf16[128,128]{1,0:T(8,128)(2,1)}, u32[]{:S(2)}) copy-start(bf16[128,128]{1,0:T(8,128)(2,1)} %w_nbr_ref.3) | copy-start | bytes 98308
  26.1 0.9 %copy-start.10 = (f32[128,16]{0,1:T(8,128)S(1)}, f32[128,16]{0,1:T(8,128)}, u32[]{:S(2)}) copy-start(f32[128,16]{0,1:T(8,128)} %param.26) | copy-start | bytes 24580
  26.1 0.9 %copy-start.11 = (f32[128]{0:T(128)S(1)}, f32[128]{0:T(128)}, u32[]{:S(2)}) copy-start(f32[128]{0:T(128)} %param.27) | copy-start | bytes 1540
  31.4 19.9 %all-to-all-start.1 = ((f32[128,1,128]{2,1,0:T(1,128)}), f32[128,1,128]{2,1,0:T(1,128)S(1)}, u32[]{:S(2)}, u32[]{:S(2)}) async-start(f32[128,1,128]{2,1,0:T(1,128)} %bitcast.13), calls=%async_computation.1 | async-start | bytes 131072 | tf_op jit(solution)/shard_map/all_to_all | solution.py:715
  39.5 10.6 %collective-permute-start.4 = (f32[24,128]{1,0:T(8,128)S(1)}, f32[24,128]{1,0:T(8,128)S(1)}, u32[]{:S(2)}, u32[]{:S(2)}) collective-permute-start(f32[24,128]{1,0:T(8,128)S(1)} %get-tuple-element.46), channel_id=1, source_target_pairs={{0,1},{1,0},{2,3},{3,2},{4,5},{5,4},{6,7},{7,6},{8,9},{9,8},{10,11... | collective-permute-start | bytes 36872 | tf_op jit(solution)/shard_map/ppermute | solution.py:717
  39.9 10.1 %collective-permute-start.5 = (f32[64,128]{1,0:T(8,128)S(1)}, f32[64,128]{1,0:T(8,128)S(1)}, u32[]{:S(2)}, u32[]{:S(2)}) collective-permute-start(f32[64,128]{1,0:T(8,128)S(1)} %get-tuple-element.47), channel_id=1, source_target_pairs={{0,2},{2,0},{4,6},{6,4},{8,10},{10,8},{12,14},{14,12},{16,18},{18,... | collective-permute-start | bytes 98312 | tf_op jit(solution)/shard_map/ppermute | solution.py:719
  39.9 10.1 %collective-permute-start.6 = (f32[64,128]{1,0:T(8,128)S(1)}, f32[64,128]{1,0:T(8,128)S(1)}, u32[]{:S(2)}, u32[]{:S(2)}) collective-permute-start(f32[64,128]{1,0:T(8,128)S(1)} %get-tuple-element.48), channel_id=1, source_target_pairs={{0,254},{2,4},{4,2},{6,8},{8,6},{10,12},{12,10},{14,16},{16,14},{1... | collective-permute-start | bytes 98312 | tf_op jit(solution)/shard_map/ppermute | solution.py:718
  50.1 1.2 %copy-start.1 = (f32[3,512]{1,0:T(4,128)S(1)}, f32[3,512]{1,0:T(4,128)}, u32[]{:S(2)}) copy-start(f32[3,512]{1,0:T(4,128)} %vel_ref.1) | copy-start | bytes 18436
  50.1 1.2 %copy-start.2 = (s32[512,1]{0,1:T(1,128)S(1)}, s32[512,1]{0,1:T(1,128)}, u32[]{:S(2)}) copy-start(s32[512,1]{0,1:T(1,128)} %param.16) | copy-start | bytes 6148
  50.1 1.2 %copy-start.3 = (f32[512]{0:T(512)S(1)}, f32[512]{0:T(512)}, u32[]{:S(2)}) copy-start(f32[512]{0:T(512)} %param.20) | copy-start | bytes 6148

commit v4 on v3

--- a/solution.py
+++ b/solution.py
@@ -226,7 +226,8 @@
     return lax.axis_index("fluid") % 2 == 0
 
 
-def relax_kernel(rates_ref, pops_ref, rest_ref, axis_ref, vel_ref, near_ref, far_ref):
+def relax_kernel(rates_ref, pops_ref, *refs):
+    rest_ref, axis_ref, vel_ref, near_ref, far_ref = refs[-5:]
     cells = pops_ref.shape[1]
     width = cells // 2
 
@@ -249,7 +250,7 @@
                 axis_ref[i - 1, rows, :] = f[i] - relaxed[i]
         return carry
 
-    lax.fori_loop(0, cells // 8, chunk, 0)
+    lax.fori_loop(0, cells // 8, chunk, 0, unroll=4)
 
     lanes = pops_ref.shape[2]
     even = even_device()
@@ -299,13 +300,13 @@
     )(rest)
 
 
-def relax(rates, pops):
+def relax(rates, pops, *later):
     _, cells, lanes = pops.shape
     width = cells // 2
     vmem = pl.BlockSpec(memory_space=pltpu.VMEM)
     return pl.pallas_call(
         relax_kernel,
-        in_specs=[pl.BlockSpec(memory_space=pltpu.SMEM), vmem],
+        in_specs=[pl.BlockSpec(memory_space=pltpu.SMEM)] + [vmem] * (1 + len(later)),
         out_specs=[vmem] * 5,
         out_shape=(
             jax.ShapeDtypeStruct((13, cells, lanes), F32),
@@ -317,7 +318,7 @@
         name="relax",
         compiler_params=pltpu.CompilerParams(vmem_limit_bytes=VMEM_LIMIT),
         cost_estimate=pl.CostEstimate(flops=10_000_000, bytes_accessed=6_000_000, transcendentals=0),
-    )(rates, pops)
+    )(rates, pops, *later)
 
 
 def look_kernel(mail_ref, vel_ref, reply_ref, slot_ref, wy_hi, wy_lo):
@@ -587,9 +588,9 @@
 
 
 def potential_first_kernel(
+    far_ref,
+    own_ref,
     near_ref,
-    own_ref,
-    far_ref,
     nbr_ref,
     bond_ref,
     w_self_ref,
@@ -631,9 +632,9 @@
 
 
 def potential_second_kernel(
+    far_ref,
+    own_ref,
     near_ref,
-    own_ref,
-    far_ref,
     nbr_ref,
     bond_ref,
     w_self_ref,
@@ -702,12 +703,22 @@
     near_features = lax.ppermute(sent, "fluid", chip)
     far_features = lax.ppermute(sent, "fluid", link)
     mail = lax.all_to_all(mail.reshape(slabs, 1, 128), "fluid", split_axis=0, concat_axis=0, tiled=True)
-    rest, axis, vel, near, far = relax(relax_rates, populations.reshape(19, planes * width, depth))
+    nbrs, bonds, w_rbf, w_out = neighbors.T, bonds.transpose(0, 2, 1), w_rbf.T, w_out.reshape(1, -1)
+    rest, axis, vel, near, far = relax(
+        relax_rates,
+        populations.reshape(19, planes * width, depth),
+        features,
+        nbrs,
+        bonds,
+        w_self,
+        w_nbr,
+        w_rbf,
+        w_out,
+    )
     calm, side = stream(rest)
     far = lax.ppermute(far, "fluid", link)
     near = lax.ppermute(near, "fluid", chip)
-    nbrs, bonds, w_rbf, w_out = neighbors.T, bonds.transpose(0, 2, 1), w_rbf.T, w_out.reshape(1, -1)
-    around = (near_features, features, far_features, nbrs, bonds, w_self, w_nbr, w_rbf, w_out)
+    around = (far_features, features, near_features, nbrs, bonds, w_self, w_nbr, w_rbf, w_out)
     first_pull, first_new = potential(potential_first_kernel, "potential_first", atoms // 2, FIRST_FLOPS, *around)
     mail, first_pull, side = lax.optimization_barrier((mail, first_pull, side))
 

time: 52.3 us -> 51.4 us (0.983)
  local copies, waits for them, and re-layouts: 0.78 us -> 0.06 us
    all_to_all x1, starting transfers between devices: 7.17 us -> 6.2 us  [body(): lax.all_to_all(mail.reshape(slabs, 1, 128), 'fluid', split_axis=0, concat...]
    unnamed x24, local copies, waits for them, and re-layouts: 0.78 us -> 0.06 us
    ppermute x1, starting transfers between devices: 8.3 us -> 8.87 us  [body(): far_features = lax.ppermute(sent, 'fluid', link)]
where the time goes in v4:
time: 51.4 us; the launch traced here: 51.2 us
  starting transfers between devices  36 us (70%)
  Pallas kernels  14.2 us (28%)
  between operations  0.91 us (2%)
    ppermute x1, starting transfers between devices, body(): far_features = lax.ppermute(sent, 'fluid', link)  8.87 us
    all_to_all x1, starting transfers between devices, body(): lax.all_to_all(reply.reshape(slabs, 1, 128), 'fluid', split_axis=0, conca...  7.07 us
    ppermute x1, starting transfers between devices, body(): late_far = lax.ppermute(late_far, 'fluid', link)  6.81 us
    all_to_all x1, starting transfers between devices, body(): lax.all_to_all(mail.reshape(slabs, 1, 128), 'fluid', split_axis=0, concat...  6.2 us
    ppermute x1, starting transfers between devices, body(): far = lax.ppermute(far, 'fluid', link)  6.2 us
    pallas_call x2, Pallas kernels, potential(): pl.pallas_call(kernel, out_shape=(jax.ShapeDtypeStruct((3, columns), F32)...  5.95 us
    pallas_call x1, Pallas kernels, pack(): pl.pallas_call(pack_kernel, in_specs=[pl.BlockSpec(memory_space=pltpu.HBM...  1.98 us
    pallas_call x1, Pallas kernels, look(): pl.pallas_call(look_kernel, out_shape=(jax.ShapeDtypeStruct((slabs, 128),...  1.64 us
  transfers between devices with their start and end apart: 9, of which 0 were waited for; matrix products, arithmetic and copies ran while one was open for 0% of the time, Pallas kernels for 26%

profile of v4, /device:TPU:16, one launch (start us, length us, event | category | flops | bytes accessed | tf_op | source)
XLA Modules:
  0.0 51.2 jit_solution(10310175010314293833)
XLA Ops:
  0.6 0.0 copy-start.1
  0.6 0.0 copy-start.5
  0.7 0.1 collective-permute-start.1
  0.8 8.9 %collective-permute-start = (bf16[128,512]{1,0:T(8,128)(2,1)}, bf16[128,512]{1,0:T(8,128)(2,1)S(1)}, u32[]{:S(2)}, u32[]{:S(2)}) collective-permute-start(bf16[128,512]{1,0:T(8,128)(2,1)} %own_ref.3), channel_id=1, source_target_pairs={{0,254},{2,4},{4,2},{6,8},{8,6},{10,12},{12,10},{14,16},{16,14},{1... | collective-permute-start | bytes 393224 | tf_op jit(solution)/shard_map/ppermute | solution.py:704
  9.7 2.0 %pack.1 = (f32[128,128]{1,0:T(8,128)}, f32[1,512]{1,0:T(1,128)S(1)}) custom-call(s32[1,512]{1,0:T(1,128)} %bitcast.29, s32[1,512]{1,0:T(1,128)} %bitcast.37, f32[3,512]{1,0:T(4,128)} %frac_hbm.1, f32[3,512]{1,0:T(4,128)} %vel_ref.1, f32[1,512]{1,0:T(1,128)} %bitcast.31), custom_call_target="tpu_custom_call" | custom-call | flops 400000000 | bytes 4000000 | tf_op jit(solution)/shard_map/pack/pallas_call | solution.py:203
  11.7 6.2 %all-to-all-start = ((f32[128,1,128]{2,1,0:T(1,128)}), f32[128,1,128]{2,1,0:T(1,128)S(1)}, u32[]{:S(2)}, u32[]{:S(2)}) async-start(f32[128,1,128]{2,1,0:T(1,128)} %bitcast.9), calls=%async_computation | async-start | bytes 131072 | tf_op jit(solution)/shard_map/all_to_all | solution.py:705
  18.0 1.4 %relax.1 = (f32[13,128,128]{2,1,0:T(8,128)S(1)}, f32[6,128,128]{2,1,0:T(8,128)S(1)}, f32[3,128,128]{2,1,0:T(8,128)S(1)}, bf16[64,512]{1,0:T(8,128)(2,1)S(1)}, bf16[64,512]{1,0:T(8,128)(2,1)S(1)}) custom-call(f32[19]{0:T(128)S(1)} %copy-done.10, f32[19,128,128]{2,1,0:T(8,128)S(1)} %bitcast.17, bf16[128,512]{1,0:T(8,128)(2,1)S(1)} %copy-done.1, ...), custom_call_target="tpu_custom_call" | custom-call | flops 10000000 | bytes 6000000 | tf_op jit(solution)/shard_map/relax/pallas_call | solution.py:307
  19.4 0.1 collective-permute-start.2
  19.5 6.2 %collective-permute-start.3 = (bf16[64,512]{1,0:T(8,128)(2,1)S(1)}, bf16[64,512]{1,0:T(8,128)(2,1)S(1)}, u32[]{:S(2)}, u32[]{:S(2)}) collective-permute-start(bf16[64,512]{1,0:T(8,128)(2,1)S(1)} %get-tuple-element.43), channel_id=1, source_target_pairs={{0,254},{2,4},{4,2},{6,8},{8,6},{10,12},{12,10},{14,16},{16,14},{1... | collective-permute-start | bytes 196616 | tf_op jit(solution)/shard_map/ppermute | solution.py:719
  25.7 0.2 stream.1
  25.9 0.0 collective-permute-done.1.near_ref
  25.9 0.0 collective-permute-done.far_ref
  25.9 2.7 %potential_first.1 = (f32[3,256]{1,0:T(4,128)S(1)}, bf16[128,256]{1,0:T(8,128)(2,1)S(1)}) custom-call(bf16[128,512]{1,0:T(8,128)(2,1)S(1)} %collective-permute-done.far_ref, bf16[128,512]{1,0:T(8,128)(2,1)S(1)} %copy-done.1, bf16[128,512]{1,0:T(8,128)(2,1)S(1)} %collective-permute-done.1.near_ref, s32[16,512]{1,0:T(8,128)S(1)} %bitcast.24, ...), custom_call_target="tpu_custom_call" | custom-call | flops 3500000000 | bytes 100000 | tf_op jit(solution)/shard_map/potential_first/pallas_call | solution.py:660
  28.6 0.0 all-to-all-done
  28.6 1.6 %look.1 = (f32[128,128]{1,0:T(8,128)}, f32[48,128]{1,0:T(8,128)S(1)}, bf16[128,1024]{1,0:T(8,128)(2,1)S(1)}, bf16[128,1024]{1,0:T(8,128)(2,1)S(1)}) custom-call(f32[128,128]{1,0:T(8,128)S(1)} %bitcast.22, f32[3,128,128]{2,1,0:T(8,128)S(1)} %get-tuple-element.37.vel_ref), custom_call_target="tpu_custom_call" | custom-call | flops 500000000 | bytes 1000000 | tf_op jit(solution)/shard_map/look/pallas_call | solution.py:369
  30.2 7.1 %all-to-all-start.1 = ((f32[128,1,128]{2,1,0:T(1,128)}), f32[128,1,128]{2,1,0:T(1,128)S(1)}, u32[]{:S(2)}, u32[]{:S(2)}) async-start(f32[128,1,128]{2,1,0:T(1,128)} %bitcast.13), calls=%async_computation.1 | async-start | bytes 131072 | tf_op jit(solution)/shard_map/all_to_all | solution.py:726
  37.3 0.0 collective-permute-done.2.near_ref
  37.3 0.0 collective-permute-done.3.far_ref
  37.3 1.0 %push.1 = (f32[6,128,128]{2,1,0:T(8,128)S(1)}, f32[64,128]{1,0:T(8,128)S(1)}, f32[64,128]{1,0:T(8,128)S(1)}, f32[24,128]{1,0:T(8,128)S(1)}) custom-call(f32[6,128,128]{2,1,0:T(8,128)S(1)} %get-tuple-element.35.axis_ref, f32[48,128]{1,0:T(8,128)S(1)} %get-tuple-element.38.slot_ref, bf16[128,1024]{1,0:T(8,128)(2,1)S(1)} %get-tuple-element.39.wy_hi, ...), custom_call_target="tpu_custom_call" | custom-call | flops 500000000 | bytes 1500000 | tf_op jit(solution)/shard_map/push/pallas_call | solution.py:464
  38.3 0.7 %collective-permute-start.4 = (f32[24,128]{1,0:T(8,128)S(1)}, f32[24,128]{1,0:T(8,128)S(1)}, u32[]{:S(2)}, u32[]{:S(2)}) collective-permute-start(f32[24,128]{1,0:T(8,128)S(1)} %get-tuple-element.46), channel_id=1, source_target_pairs={{0,1},{1,0},{2,3},{3,2},{4,5},{5,4},{6,7},{7,6},{8,9},{9,8},{10,11... | collective-permute-start | bytes 36872 | tf_op jit(solution)/shard_map/ppermute | solution.py:728
  39.0 0.0 collective-permute-start.5
  39.0 6.8 %collective-permute-start.6 = (f32[64,128]{1,0:T(8,128)S(1)}, f32[64,128]{1,0:T(8,128)S(1)}, u32[]{:S(2)}, u32[]{:S(2)}) collective-permute-start(f32[64,128]{1,0:T(8,128)S(1)} %get-tuple-element.48), channel_id=1, source_target_pairs={{0,254},{2,4},{4,2},{6,8},{8,6},{10,12},{12,10},{14,16},{16,14},{1... | collective-permute-start | bytes 98312 | tf_op jit(solution)/shard_map/ppermute | solution.py:729
  45.8 3.3 %potential_second.1 = (f32[3,512]{1,0:T(4,128)S(1)}, bf16[128,512]{1,0:T(8,128)(2,1)}) custom-call(bf16[128,512]{1,0:T(8,128)(2,1)S(1)} %collective-permute-done.far_ref, bf16[128,512]{1,0:T(8,128)(2,1)S(1)} %copy-done.1, bf16[128,512]{1,0:T(8,128)(2,1)S(1)} %collective-permute-done.1.near_ref, s32[16,512]{1,0:T(8,128)S(1)} %bitcast.25, ...), custom_call_target="tpu_custom_call" | custom-call | flops 500000000 | bytes 100000 | tf_op jit(solution)/shard_map/potential_second/pallas_call | solution.py:660
  49.1 0.0 collective-permute-done.4.side_ref
  49.1 0.0 collective-permute-done.5.late_near_ref
  49.1 0.0 collective-permute-done.6.late_far_ref
  49.1 0.0 copy-start.7
  49.1 0.0 copy-start.8
  49.2 0.0 copy-start.9
  49.2 1.1 %gather.1 = f32[19,128,128]{2,1,0:T(8,128)} custom-call(f32[13,128,128]{2,1,0:T(8,128)S(1)} %get-tuple-element.30.calm_ref, f32[6,128,128]{2,1,0:T(8,128)S(1)} %get-tuple-element.45.moved_ref, bf16[64,512]{1,0:T(8,128)(2,1)S(1)} %collective-permute-done.2.near_ref, bf16[64,512]{1,0:T(8,128)(2,1)S(1)} %collective-permute-done.3.far_ref, ...), custom_call_target="tpu_custom_call" | custom-call | flops 1000 | bytes 3000000 | tf_op jit(solution)/shard_map/gather/pallas_call | solution.py:524
  50.3 0.0 all-to-all-done.1
  50.3 0.8 %finish.1 = f32[3,512]{1,0:T(4,128)} custom-call(f32[128,128]{1,0:T(8,128)S(1)} %bitcast.18, s32[1,512]{1,0:T(1,128)S(1)} %bitcast.30, f32[1,512]{1,0:T(1,128)S(1)} %get-tuple-element.50.rank_ref, f32[3,512]{1,0:T(4,128)S(1)} %copy-done.7, f32[1,512]{1,0:T(1,128)S(1)} %bitcast.32, f32[3,512]{1,0:T(4,128)S(1)} %get-tuple-element.53.pull_ref), custom_call_target="tpu_custom_call" | custom-call | flops 20000000 | bytes 100000 | tf_op jit(solution)/shard_map/finish/pallas_call | solution.py:547
  (19 shorter events, 0.0 us)
Async XLA Ops:
  0.6 17.3 %copy-start.1 = (bf16[128,512]{1,0:T(8,128)(2,1)S(1)}, bf16[128,512]{1,0:T(8,128)(2,1)}, u32[]{:S(2)}) copy-start(bf16[128,512]{1,0:T(8,128)(2,1)} %own_ref.3) | copy-start | bytes 393220
  0.6 17.3 %copy-start.5 = (bf16[128,128]{1,0:T(8,128)(2,1)S(1)}, bf16[128,128]{1,0:T(8,128)(2,1)}, u32[]{:S(2)}) copy-start(bf16[128,128]{1,0:T(8,128)(2,1)} %w_nbr_ref.3) | copy-start | bytes 98308
  0.7 17.3 %copy-start.4 = (bf16[128,128]{1,0:T(8,128)(2,1)S(1)}, bf16[128,128]{1,0:T(8,128)(2,1)}, u32[]{:S(2)}) copy-start(bf16[128,128]{1,0:T(8,128)(2,1)} %w_self_ref.3) | copy-start | bytes 98308
  0.7 17.3 %copy-start.11 = (f32[128]{0:T(128)S(1)}, f32[128]{0:T(128)}, u32[]{:S(2)}) copy-start(f32[128]{0:T(128)} %param.27) | copy-start | bytes 1540
  0.7 17.3 %copy-start.6 = (f32[128,16]{0,1:T(8,128)S(1)}, f32[128,16]{0,1:T(8,128)}, u32[]{:S(2)}) copy-start(f32[128,16]{0,1:T(8,128)} %param.26) | copy-start | bytes 24580
  0.7 17.3 %copy-start.2 = (f32[3,512,16]{1,2,0:T(8,128)S(1)}, f32[3,512,16]{1,2,0:T(8,128)}, u32[]{:S(2)}) copy-start(f32[3,512,16]{1,2,0:T(8,128)} %param.23) | copy-start | bytes 294916
  0.7 17.3 %copy-start.3 = (s32[512,16]{0,1:T(8,128)S(1)}, s32[512,16]{0,1:T(8,128)}, u32[]{:S(2)}) copy-start(s32[512,16]{0,1:T(8,128)} %param.22) | copy-start | bytes 98308
  0.7 17.3 %copy-start.10 = (f32[19]{0:T(128)S(1)}, f32[19]{0:T(128)}, u32[]{:S(2)}) copy-start(f32[19]{0:T(128)} %rates_ref.1) | copy-start | bytes 232
  0.7 17.3 %copy-start = (f32[19,2,64,128]{3,2,1,0:T(8,128)S(1)}, f32[19,2,64,128]{3,2,1,0:T(8,128)}, u32[]{:S(2)}) copy-start(f32[19,2,64,128]{3,2,1,0:T(8,128)} %param.14) | copy-start | bytes 3735556
  0.7 25.2 %collective-permute-start.1 = (bf16[128,512]{1,0:T(8,128)(2,1)}, bf16[128,512]{1,0:T(8,128)(2,1)S(1)}, u32[]{:S(2)}, u32[]{:S(2)}) collective-permute-start(bf16[128,512]{1,0:T(8,128)(2,1)} %own_ref.3), channel_id=1, source_target_pairs={{0,2},{2,0},{4,6},{6,4},{8,10},{10,8},{12,14},{14,12},{16,18},{18,... | collective-permute-start | bytes 393224 | tf_op jit(solution)/shard_map/ppermute | solution.py:703
  0.8 25.1 %collective-permute-start = (bf16[128,512]{1,0:T(8,128)(2,1)}, bf16[128,512]{1,0:T(8,128)(2,1)S(1)}, u32[]{:S(2)}, u32[]{:S(2)}) collective-permute-start(bf16[128,512]{1,0:T(8,128)(2,1)} %own_ref.3), channel_id=1, source_target_pairs={{0,254},{2,4},{4,2},{6,8},{8,6},{10,12},{12,10},{14,16},{16,14},{1... | collective-permute-start | bytes 393224 | tf_op jit(solution)/shard_map/ppermute | solution.py:704
  11.7 16.9 %all-to-all-start = ((f32[128,1,128]{2,1,0:T(1,128)}), f32[128,1,128]{2,1,0:T(1,128)S(1)}, u32[]{:S(2)}, u32[]{:S(2)}) async-start(f32[128,1,128]{2,1,0:T(1,128)} %bitcast.9), calls=%async_computation | async-start | bytes 131072 | tf_op jit(solution)/shard_map/all_to_all | solution.py:705
  19.4 17.9 %collective-permute-start.2 = (bf16[64,512]{1,0:T(8,128)(2,1)S(1)}, bf16[64,512]{1,0:T(8,128)(2,1)S(1)}, u32[]{:S(2)}, u32[]{:S(2)}) collective-permute-start(bf16[64,512]{1,0:T(8,128)(2,1)S(1)} %get-tuple-element.42), channel_id=1, source_target_pairs={{0,2},{2,0},{4,6},{6,4},{8,10},{10,8},{12,14},{14,12},{16,18},{18,... | collective-permute-start | bytes 196616 | tf_op jit(solution)/shard_map/ppermute | solution.py:720
  19.5 17.8 %collective-permute-start.3 = (bf16[64,512]{1,0:T(8,128)(2,1)S(1)}, bf16[64,512]{1,0:T(8,128)(2,1)S(1)}, u32[]{:S(2)}, u32[]{:S(2)}) collective-permute-start(bf16[64,512]{1,0:T(8,128)(2,1)S(1)} %get-tuple-element.43), channel_id=1, source_target_pairs={{0,254},{2,4},{4,2},{6,8},{8,6},{10,12},{12,10},{14,16},{16,14},{1... | collective-permute-start | bytes 196616 | tf_op jit(solution)/shard_map/ppermute | solution.py:719
  30.2 20.1 %all-to-all-start.1 = ((f32[128,1,128]{2,1,0:T(1,128)}), f32[128,1,128]{2,1,0:T(1,128)S(1)}, u32[]{:S(2)}, u32[]{:S(2)}) async-start(f32[128,1,128]{2,1,0:T(1,128)} %bitcast.13), calls=%async_computation.1 | async-start | bytes 131072 | tf_op jit(solution)/shard_map/all_to_all | solution.py:726
  38.3 10.8 %collective-permute-start.4 = (f32[24,128]{1,0:T(8,128)S(1)}, f32[24,128]{1,0:T(8,128)S(1)}, u32[]{:S(2)}, u32[]{:S(2)}) collective-permute-start(f32[24,128]{1,0:T(8,128)S(1)} %get-tuple-element.46), channel_id=1, source_target_pairs={{0,1},{1,0},{2,3},{3,2},{4,5},{5,4},{6,7},{7,6},{8,9},{9,8},{10,11... | collective-permute-start | bytes 36872 | tf_op jit(solution)/shard_map/ppermute | solution.py:728
  39.0 10.1 %collective-permute-start.5 = (f32[64,128]{1,0:T(8,128)S(1)}, f32[64,128]{1,0:T(8,128)S(1)}, u32[]{:S(2)}, u32[]{:S(2)}) collective-permute-start(f32[64,128]{1,0:T(8,128)S(1)} %get-tuple-element.47), channel_id=1, source_target_pairs={{0,2},{2,0},{4,6},{6,4},{8,10},{10,8},{12,14},{14,12},{16,18},{18,... | collective-permute-start | bytes 98312 | tf_op jit(solution)/shard_map/ppermute | solution.py:730
  39.0 10.1 %collective-permute-start.6 = (f32[64,128]{1,0:T(8,128)S(1)}, f32[64,128]{1,0:T(8,128)S(1)}, u32[]{:S(2)}, u32[]{:S(2)}) collective-permute-start(f32[64,128]{1,0:T(8,128)S(1)} %get-tuple-element.48), channel_id=1, source_target_pairs={{0,254},{2,4},{4,2},{6,8},{8,6},{10,12},{12,10},{14,16},{16,14},{1... | collective-permute-start | bytes 98312 | tf_op jit(solution)/shard_map/ppermute | solution.py:729
  49.1 1.2 %copy-start.7 = (f32[3,512]{1,0:T(4,128)S(1)}, f32[3,512]{1,0:T(4,128)}, u32[]{:S(2)}) copy-start(f32[3,512]{1,0:T(4,128)} %vel_ref.1) | copy-start | bytes 18436
  49.1 1.2 %copy-start.8 = (s32[512,1]{0,1:T(1,128)S(1)}, s32[512,1]{0,1:T(1,128)}, u32[]{:S(2)}) copy-start(s32[512,1]{0,1:T(1,128)} %param.16) | copy-start | bytes 6148
  49.2 1.2 %copy-start.9 = (f32[512]{0:T(512)S(1)}, f32[512]{0:T(512)}, u32[]{:S(2)}) copy-start(f32[512]{0:T(512)} %param.20) | copy-start | bytes 6148

commit v5 on v4

--- a/solution.py
+++ b/solution.py
@@ -52,14 +52,6 @@
     return high, low
 
 
-def thirds(value):
-    high = value.astype(BF16)
-    rest = value - high.astype(F32)
-    middle = rest.astype(BF16)
-    low = (rest - middle.astype(F32)).astype(BF16)
-    return high, middle, low
-
-
 def mm(a, b):
     return jnp.dot(a, b, preferred_element_type=F32)
 
@@ -77,15 +69,23 @@
     named = iota((slabs, atoms), 0) == slab
     one_hot = jnp.where(named, 1.0, 0.0)
     one_hot_b = one_hot.astype(BF16)
-    before = mm(one_hot_b, earlier)
+    slab_rows, run = one_hot_b.shape[0], earlier.shape[0]
+    runs = [one_hot_b[:, at : at + run] for at in range(0, atoms, run)]
+    counts = mm(jnp.concatenate(runs, axis=0), earlier)
+    before, total = [], 0.0
+    for at in range(len(runs)):
+        part = counts[at * slab_rows : (at + 1) * slab_rows]
+        before.append(part[:, :run] + total)
+        total = total + part[:, run:]
+    before = jnp.concatenate(before, axis=1)
     rank = jnp.sum(one_hot * before, axis=0, keepdims=True)
     mine = iota((SLOTS, atoms), 0).astype(F32) == rank
     rows = [frac_ref[c : c + 1, :] for c in range(3)]
     rows += [vel_ref[c : c + 1, :] for c in range(3)]
     rows += [fric, base.astype(F32)]
     spread = [jnp.where(mine, row, 0.0) for row in rows]
-    high, middle, low = thirds(jnp.concatenate(spread, axis=0))
-    return mm_nt(one_hot_b, high) + (mm_nt(one_hot_b, middle) + mm_nt(one_hot_b, low)), rank
+    both = mm_nt(one_hot_b, jnp.concatenate(halves(jnp.concatenate(spread, axis=0)), axis=0))
+    return both + pltpu.roll(both, both.shape[1] // 2, 1), rank
 
 
 def moments_of(d):
@@ -183,16 +183,13 @@
     copies = [pltpu.make_async_copy(src, dst, sems.at[at]) for at, (src, dst) in enumerate(pairs)]
     for copy in copies:
         copy.start()
-    atoms = slab_ref.shape[1]
-    earlier = jnp.where(iota((atoms, atoms), 0) < iota((atoms, atoms), 1), 1.0, 0.0).astype(BF16)
+    earlier = jnp.where(iota((128, 256), 0) < iota((128, 256), 1), 1.0, 0.0).astype(BF16)
     for copy in copies:
         copy.wait()
     mail, rank = packed(
         slab_ref[...], base_ref[...], frac_ref, vel_ref, fric_ref[...], mail_ref.shape[0], earlier
     )
-    filled = mail.shape[1]
-    mail_ref[:, :filled] = mail
-    mail_ref[:, filled:] = jnp.zeros((mail.shape[0], mail_ref.shape[1] - filled), F32)
+    mail_ref[...] = mail
     rank_ref[...] = rank
 
 
@@ -339,20 +336,29 @@
     row_x = iota((width, slots), 0)
 
     v_hi, v_lo = halves(vel_ref[...].reshape(comps * cells, depth))
+    v_parts = jnp.concatenate([v_hi, v_lo, v_hi], axis=1)
     values = [[], [], []]
-    for r in range(SLOTS):
-        one = slice(r, r + 1)
-        cols = slice(r * slots, (r + 1) * slots)
-        wy = jnp.where(row_y == y0[one], gy[one], 0.0) + jnp.where(row_y == y1[one], fy[one], 0.0)
-        wx = jnp.where(row_x == x0[one], gx[one], 0.0) + jnp.where(row_x == x0[one] + 1, fx[one], 0.0)
-        hi, lo = halves(wy)
+    for first in range(0, SLOTS, 2):
+        wx, weights = [], []
+        for r in (first, first + 1):
+            one = slice(r, r + 1)
+            weights.append(
+                jnp.where(row_y == y0[one], gy[one], 0.0) + jnp.where(row_y == y1[one], fy[one], 0.0)
+            )
+            wx.append(jnp.where(row_x == x0[one], gx[one], 0.0) + jnp.where(row_x == x0[one] + 1, fx[one], 0.0))
+        hi, lo = halves(jnp.concatenate(weights, axis=1))
+        cols = slice(first * slots, (first + 2) * slots)
         wy_hi[:, cols] = hi
         wy_lo[:, cols] = lo
-        seen = mm(v_hi, hi) + (mm(v_lo, hi) + mm(v_hi, lo))
-        for c in range(3):
-            close = seen[c * cells : c * cells + width]
-            beyond = seen[c * cells + width : (c + 1) * cells]
-            values[c].append(jnp.sum(wx * (close * gz[one] + beyond * fz[one]), axis=0, keepdims=True))
+        pair = mm(v_parts, jnp.concatenate([hi, hi, lo], axis=0))
+        for r in (first, first + 1):
+            one = slice(r, r + 1)
+            seen = pair[:, (r - first) * slots : (r - first + 1) * slots]
+            for c in range(3):
+                close = seen[c * cells : c * cells + width]
+                beyond = seen[c * cells + width : (c + 1) * cells]
+                value = wx[r - first] * (close * gz[one] + beyond * fz[one])
+                values[c].append(jnp.sum(value, axis=0, keepdims=True))
     rows = jnp.concatenate([row for c in range(3) for row in values[c]], axis=0)
     reply_ref[...] = jnp.concatenate([rows, jnp.zeros((128 - 3 * SLOTS, slots), F32)], axis=0).T
     slot_ref[0:SLOTS, :] = x0.astype(F32)
@@ -533,8 +539,8 @@
 def finish_kernel(reply_ref, slab_ref, rank_ref, vel_ref, fric_ref, pull_ref, force_ref):
     slabs, atoms = reply_ref.shape[0], slab_ref.shape[1]
     one_hot = jnp.where(iota((slabs, atoms), 0) == slab_ref[...], 1.0, 0.0).astype(BF16)
-    high, low = halves(reply_ref[...].T[: 3 * SLOTS])
-    picked = mm(high, one_hot) + mm(low, one_hot)
+    picked = mm(jnp.concatenate(halves(reply_ref[...].T[: 3 * SLOTS]), axis=0), one_hot)
+    picked = picked[: 3 * SLOTS] + picked[3 * SLOTS :]
     mine = iota((SLOTS, atoms), 0).astype(F32) == rank_ref[...]
     for c in range(3):
         seen = jnp.sum(jnp.where(mine, picked[c * SLOTS : (c + 1) * SLOTS], 0.0), axis=0, keepdims=True)

time: 51.4 us -> 51.2 us (level)
  no operation moved by 1% of the time
where the time goes in v5:
time: 51.2 us; the launch traced here: 50.9 us
  starting transfers between devices  36 us (70%)
  Pallas kernels  13.9 us (27%)
  between operations  0.91 us (2%)
    ppermute x1, starting transfers between devices, body(): far_features = lax.ppermute(sent, 'fluid', link)  8.87 us
    all_to_all x1, starting transfers between devices, body(): lax.all_to_all(reply.reshape(slabs, 1, 128), 'fluid', split_axis=0, conca...  7.07 us
    ppermute x1, starting transfers between devices, body(): late_far = lax.ppermute(late_far, 'fluid', link)  6.81 us
    all_to_all x1, starting transfers between devices, body(): lax.all_to_all(mail.reshape(slabs, 1, 128), 'fluid', split_axis=0, concat...  6.2 us
    ppermute x1, starting transfers between devices, body(): far = lax.ppermute(far, 'fluid', link)  6.2 us
    pallas_call x2, Pallas kernels, potential(): pl.pallas_call(kernel, out_shape=(jax.ShapeDtypeStruct((3, columns), F32)...  5.95 us
    pallas_call x1, Pallas kernels, pack(): pl.pallas_call(pack_kernel, in_specs=[pl.BlockSpec(memory_space=pltpu.HBM...  1.92 us
    pallas_call x1, Pallas kernels, look(): pl.pallas_call(look_kernel, out_shape=(jax.ShapeDtypeStruct((slabs, 128),...  1.5 us
  transfers between devices with their start and end apart: 9, of which 0 were waited for; matrix products, arithmetic and copies ran while one was open for 0% of the time, Pallas kernels for 26%

profile of v5, /device:TPU:16, one launch (start us, length us, event | category | flops | bytes accessed | tf_op | source)
XLA Modules:
  0.0 50.9 jit_solution(9533256143647914524)
XLA Ops:
  0.6 0.0 copy-start.1
  0.6 0.0 copy-start.5
  0.7 0.1 collective-permute-start.1
  0.8 8.9 %collective-permute-start = (bf16[128,512]{1,0:T(8,128)(2,1)}, bf16[128,512]{1,0:T(8,128)(2,1)S(1)}, u32[]{:S(2)}, u32[]{:S(2)}) collective-permute-start(bf16[128,512]{1,0:T(8,128)(2,1)} %own_ref.3), channel_id=1, source_target_pairs={{0,254},{2,4},{4,2},{6,8},{8,6},{10,12},{12,10},{14,16},{16,14},{1... | collective-permute-start | bytes 393224 | tf_op jit(solution)/shard_map/ppermute | solution.py:710
  9.7 1.9 %pack.1 = (f32[128,128]{1,0:T(8,128)}, f32[1,512]{1,0:T(1,128)S(1)}) custom-call(s32[1,512]{1,0:T(1,128)} %bitcast.29, s32[1,512]{1,0:T(1,128)} %bitcast.37, f32[3,512]{1,0:T(4,128)} %frac_hbm.1, f32[3,512]{1,0:T(4,128)} %vel_ref.1, f32[1,512]{1,0:T(1,128)} %bitcast.31), custom_call_target="tpu_custom_call" | custom-call | flops 400000000 | bytes 4000000 | tf_op jit(solution)/shard_map/pack/pallas_call | solution.py:200
  11.6 6.2 %all-to-all-start = ((f32[128,1,128]{2,1,0:T(1,128)}), f32[128,1,128]{2,1,0:T(1,128)S(1)}, u32[]{:S(2)}, u32[]{:S(2)}) async-start(f32[128,1,128]{2,1,0:T(1,128)} %bitcast.9), calls=%async_computation | async-start | bytes 131072 | tf_op jit(solution)/shard_map/all_to_all | solution.py:711
  17.9 1.4 %relax.1 = (f32[13,128,128]{2,1,0:T(8,128)S(1)}, f32[6,128,128]{2,1,0:T(8,128)S(1)}, f32[3,128,128]{2,1,0:T(8,128)S(1)}, bf16[64,512]{1,0:T(8,128)(2,1)S(1)}, bf16[64,512]{1,0:T(8,128)(2,1)S(1)}) custom-call(f32[19]{0:T(128)S(1)} %copy-done.10, f32[19,128,128]{2,1,0:T(8,128)S(1)} %bitcast.17, bf16[128,512]{1,0:T(8,128)(2,1)S(1)} %copy-done.1, ...), custom_call_target="tpu_custom_call" | custom-call | flops 10000000 | bytes 6000000 | tf_op jit(solution)/shard_map/relax/pallas_call | solution.py:304
  19.4 0.1 collective-permute-start.2
  19.5 6.2 %collective-permute-start.3 = (bf16[64,512]{1,0:T(8,128)(2,1)S(1)}, bf16[64,512]{1,0:T(8,128)(2,1)S(1)}, u32[]{:S(2)}, u32[]{:S(2)}) collective-permute-start(bf16[64,512]{1,0:T(8,128)(2,1)S(1)} %get-tuple-element.43), channel_id=1, source_target_pairs={{0,254},{2,4},{4,2},{6,8},{8,6},{10,12},{12,10},{14,16},{16,14},{1... | collective-permute-start | bytes 196616 | tf_op jit(solution)/shard_map/ppermute | solution.py:725
  25.7 0.2 stream.1
  25.8 0.0 collective-permute-done.1.near_ref
  25.8 0.0 collective-permute-done.far_ref
  25.8 2.7 %potential_first.1 = (f32[3,256]{1,0:T(4,128)S(1)}, bf16[128,256]{1,0:T(8,128)(2,1)S(1)}) custom-call(bf16[128,512]{1,0:T(8,128)(2,1)S(1)} %collective-permute-done.far_ref, bf16[128,512]{1,0:T(8,128)(2,1)S(1)} %copy-done.1, bf16[128,512]{1,0:T(8,128)(2,1)S(1)} %collective-permute-done.1.near_ref, s32[16,512]{1,0:T(8,128)S(1)} %bitcast.24, ...), custom_call_target="tpu_custom_call" | custom-call | flops 3500000000 | bytes 100000 | tf_op jit(solution)/shard_map/potential_first/pallas_call | solution.py:666
  28.5 0.0 all-to-all-done
  28.5 1.5 %look.1 = (f32[128,128]{1,0:T(8,128)}, f32[48,128]{1,0:T(8,128)S(1)}, bf16[128,1024]{1,0:T(8,128)(2,1)S(1)}, bf16[128,1024]{1,0:T(8,128)(2,1)S(1)}) custom-call(f32[128,128]{1,0:T(8,128)S(1)} %bitcast.22, f32[3,128,128]{2,1,0:T(8,128)S(1)} %get-tuple-element.37.vel_ref), custom_call_target="tpu_custom_call" | custom-call | flops 500000000 | bytes 1000000 | tf_op jit(solution)/shard_map/look/pallas_call | solution.py:375
  30.0 7.1 %all-to-all-start.1 = ((f32[128,1,128]{2,1,0:T(1,128)}), f32[128,1,128]{2,1,0:T(1,128)S(1)}, u32[]{:S(2)}, u32[]{:S(2)}) async-start(f32[128,1,128]{2,1,0:T(1,128)} %bitcast.13), calls=%async_computation.1 | async-start | bytes 131072 | tf_op jit(solution)/shard_map/all_to_all | solution.py:732
  37.1 0.0 collective-permute-done.2.near_ref
  37.1 0.0 collective-permute-done.3.far_ref
  37.1 1.0 %push.1 = (f32[6,128,128]{2,1,0:T(8,128)S(1)}, f32[64,128]{1,0:T(8,128)S(1)}, f32[64,128]{1,0:T(8,128)S(1)}, f32[24,128]{1,0:T(8,128)S(1)}) custom-call(f32[6,128,128]{2,1,0:T(8,128)S(1)} %get-tuple-element.35.axis_ref, f32[48,128]{1,0:T(8,128)S(1)} %get-tuple-element.38.slot_ref, bf16[128,1024]{1,0:T(8,128)(2,1)S(1)} %get-tuple-element.39.wy_hi, ...), custom_call_target="tpu_custom_call" | custom-call | flops 500000000 | bytes 1500000 | tf_op jit(solution)/shard_map/push/pallas_call | solution.py:470
  38.1 0.7 %collective-permute-start.4 = (f32[24,128]{1,0:T(8,128)S(1)}, f32[24,128]{1,0:T(8,128)S(1)}, u32[]{:S(2)}, u32[]{:S(2)}) collective-permute-start(f32[24,128]{1,0:T(8,128)S(1)} %get-tuple-element.46), channel_id=1, source_target_pairs={{0,1},{1,0},{2,3},{3,2},{4,5},{5,4},{6,7},{7,6},{8,9},{9,8},{10,11... | collective-permute-start | bytes 36872 | tf_op jit(solution)/shard_map/ppermute | solution.py:734
  38.8 0.0 collective-permute-start.5
  38.8 6.8 %collective-permute-start.6 = (f32[64,128]{1,0:T(8,128)S(1)}, f32[64,128]{1,0:T(8,128)S(1)}, u32[]{:S(2)}, u32[]{:S(2)}) collective-permute-start(f32[64,128]{1,0:T(8,128)S(1)} %get-tuple-element.48), channel_id=1, source_target_pairs={{0,254},{2,4},{4,2},{6,8},{8,6},{10,12},{12,10},{14,16},{16,14},{1... | collective-permute-start | bytes 98312 | tf_op jit(solution)/shard_map/ppermute | solution.py:735
  45.6 3.3 %potential_second.1 = (f32[3,512]{1,0:T(4,128)S(1)}, bf16[128,512]{1,0:T(8,128)(2,1)}) custom-call(bf16[128,512]{1,0:T(8,128)(2,1)S(1)} %collective-permute-done.far_ref, bf16[128,512]{1,0:T(8,128)(2,1)S(1)} %copy-done.1, bf16[128,512]{1,0:T(8,128)(2,1)S(1)} %collective-permute-done.1.near_ref, s32[16,512]{1,0:T(8,128)S(1)} %bitcast.25, ...), custom_call_target="tpu_custom_call" | custom-call | flops 500000000 | bytes 100000 | tf_op jit(solution)/shard_map/potential_second/pallas_call | solution.py:666
  48.9 0.0 collective-permute-done.4.side_ref
  48.9 0.0 collective-permute-done.5.late_near_ref
  48.9 0.0 collective-permute-done.6.late_far_ref
  48.9 0.0 copy-start.7
  48.9 0.0 copy-start.8
  49.0 0.0 copy-start.9
  49.0 1.1 %gather.1 = f32[19,128,128]{2,1,0:T(8,128)} custom-call(f32[13,128,128]{2,1,0:T(8,128)S(1)} %get-tuple-element.30.calm_ref, f32[6,128,128]{2,1,0:T(8,128)S(1)} %get-tuple-element.45.moved_ref, bf16[64,512]{1,0:T(8,128)(2,1)S(1)} %collective-permute-done.2.near_ref, bf16[64,512]{1,0:T(8,128)(2,1)S(1)} %collective-permute-done.3.far_ref, ...), custom_call_target="tpu_custom_call" | custom-call | flops 1000 | bytes 3000000 | tf_op jit(solution)/shard_map/gather/pallas_call | solution.py:530
  50.1 0.0 all-to-all-done.1
  50.1 0.8 %finish.1 = f32[3,512]{1,0:T(4,128)} custom-call(f32[128,128]{1,0:T(8,128)S(1)} %bitcast.18, s32[1,512]{1,0:T(1,128)S(1)} %bitcast.30, f32[1,512]{1,0:T(1,128)S(1)} %get-tuple-element.50.rank_ref, f32[3,512]{1,0:T(4,128)S(1)} %copy-done.7, f32[1,512]{1,0:T(1,128)S(1)} %bitcast.32, f32[3,512]{1,0:T(4,128)S(1)} %get-tuple-element.53.pull_ref), custom_call_target="tpu_custom_call" | custom-call | flops 20000000 | bytes 100000 | tf_op jit(solution)/shard_map/finish/pallas_call | solution.py:553
  (19 shorter events, 0.0 us)
Async XLA Ops:
  0.6 17.2 %copy-start.1 = (bf16[128,512]{1,0:T(8,128)(2,1)S(1)}, bf16[128,512]{1,0:T(8,128)(2,1)}, u32[]{:S(2)}) copy-start(bf16[128,512]{1,0:T(8,128)(2,1)} %own_ref.3) | copy-start | bytes 393220
  0.6 17.2 %copy-start.5 = (bf16[128,128]{1,0:T(8,128)(2,1)S(1)}, bf16[128,128]{1,0:T(8,128)(2,1)}, u32[]{:S(2)}) copy-start(bf16[128,128]{1,0:T(8,128)(2,1)} %w_nbr_ref.3) | copy-start | bytes 98308
  0.7 17.2 %copy-start.4 = (bf16[128,128]{1,0:T(8,128)(2,1)S(1)}, bf16[128,128]{1,0:T(8,128)(2,1)}, u32[]{:S(2)}) copy-start(bf16[128,128]{1,0:T(8,128)(2,1)} %w_self_ref.3) | copy-start | bytes 98308
  0.7 17.2 %copy-start.11 = (f32[128]{0:T(128)S(1)}, f32[128]{0:T(128)}, u32[]{:S(2)}) copy-start(f32[128]{0:T(128)} %param.27) | copy-start | bytes 1540
  0.7 17.2 %copy-start.6 = (f32[128,16]{0,1:T(8,128)S(1)}, f32[128,16]{0,1:T(8,128)}, u32[]{:S(2)}) copy-start(f32[128,16]{0,1:T(8,128)} %param.26) | copy-start | bytes 24580
  0.7 17.2 %copy-start.2 = (f32[3,512,16]{1,2,0:T(8,128)S(1)}, f32[3,512,16]{1,2,0:T(8,128)}, u32[]{:S(2)}) copy-start(f32[3,512,16]{1,2,0:T(8,128)} %param.23) | copy-start | bytes 294916
  0.7 17.2 %copy-start.3 = (s32[512,16]{0,1:T(8,128)S(1)}, s32[512,16]{0,1:T(8,128)}, u32[]{:S(2)}) copy-start(s32[512,16]{0,1:T(8,128)} %param.22) | copy-start | bytes 98308
  0.7 17.2 %copy-start.10 = (f32[19]{0:T(128)S(1)}, f32[19]{0:T(128)}, u32[]{:S(2)}) copy-start(f32[19]{0:T(128)} %rates_ref.1) | copy-start | bytes 232
  0.7 17.2 %copy-start = (f32[19,2,64,128]{3,2,1,0:T(8,128)S(1)}, f32[19,2,64,128]{3,2,1,0:T(8,128)}, u32[]{:S(2)}) copy-start(f32[19,2,64,128]{3,2,1,0:T(8,128)} %param.14) | copy-start | bytes 3735556
  0.7 25.1 %collective-permute-start.1 = (bf16[128,512]{1,0:T(8,128)(2,1)}, bf16[128,512]{1,0:T(8,128)(2,1)S(1)}, u32[]{:S(2)}, u32[]{:S(2)}) collective-permute-start(bf16[128,512]{1,0:T(8,128)(2,1)} %own_ref.3), channel_id=1, source_target_pairs={{0,2},{2,0},{4,6},{6,4},{8,10},{10,8},{12,14},{14,12},{16,18},{18,... | collective-permute-start | bytes 393224 | tf_op jit(solution)/shard_map/ppermute | solution.py:709
  0.8 25.0 %collective-permute-start = (bf16[128,512]{1,0:T(8,128)(2,1)}, bf16[128,512]{1,0:T(8,128)(2,1)S(1)}, u32[]{:S(2)}, u32[]{:S(2)}) collective-permute-start(bf16[128,512]{1,0:T(8,128)(2,1)} %own_ref.3), channel_id=1, source_target_pairs={{0,254},{2,4},{4,2},{6,8},{8,6},{10,12},{12,10},{14,16},{16,14},{1... | collective-permute-start | bytes 393224 | tf_op jit(solution)/shard_map/ppermute | solution.py:710
  11.6 16.9 %all-to-all-start = ((f32[128,1,128]{2,1,0:T(1,128)}), f32[128,1,128]{2,1,0:T(1,128)S(1)}, u32[]{:S(2)}, u32[]{:S(2)}) async-start(f32[128,1,128]{2,1,0:T(1,128)} %bitcast.9), calls=%async_computation | async-start | bytes 131072 | tf_op jit(solution)/shard_map/all_to_all | solution.py:711
  19.4 17.7 %collective-permute-start.2 = (bf16[64,512]{1,0:T(8,128)(2,1)S(1)}, bf16[64,512]{1,0:T(8,128)(2,1)S(1)}, u32[]{:S(2)}, u32[]{:S(2)}) collective-permute-start(bf16[64,512]{1,0:T(8,128)(2,1)S(1)} %get-tuple-element.42), channel_id=1, source_target_pairs={{0,2},{2,0},{4,6},{6,4},{8,10},{10,8},{12,14},{14,12},{16,18},{18,... | collective-permute-start | bytes 196616 | tf_op jit(solution)/shard_map/ppermute | solution.py:726
  19.5 17.6 %collective-permute-start.3 = (bf16[64,512]{1,0:T(8,128)(2,1)S(1)}, bf16[64,512]{1,0:T(8,128)(2,1)S(1)}, u32[]{:S(2)}, u32[]{:S(2)}) collective-permute-start(bf16[64,512]{1,0:T(8,128)(2,1)S(1)} %get-tuple-element.43), channel_id=1, source_target_pairs={{0,254},{2,4},{4,2},{6,8},{8,6},{10,12},{12,10},{14,16},{16,14},{1... | collective-permute-start | bytes 196616 | tf_op jit(solution)/shard_map/ppermute | solution.py:725
  30.0 20.1 %all-to-all-start.1 = ((f32[128,1,128]{2,1,0:T(1,128)}), f32[128,1,128]{2,1,0:T(1,128)S(1)}, u32[]{:S(2)}, u32[]{:S(2)}) async-start(f32[128,1,128]{2,1,0:T(1,128)} %bitcast.13), calls=%async_computation.1 | async-start | bytes 131072 | tf_op jit(solution)/shard_map/all_to_all | solution.py:732
  38.1 10.8 %collective-permute-start.4 = (f32[24,128]{1,0:T(8,128)S(1)}, f32[24,128]{1,0:T(8,128)S(1)}, u32[]{:S(2)}, u32[]{:S(2)}) collective-permute-start(f32[24,128]{1,0:T(8,128)S(1)} %get-tuple-element.46), channel_id=1, source_target_pairs={{0,1},{1,0},{2,3},{3,2},{4,5},{5,4},{6,7},{7,6},{8,9},{9,8},{10,11... | collective-permute-start | bytes 36872 | tf_op jit(solution)/shard_map/ppermute | solution.py:734
  38.8 10.1 %collective-permute-start.5 = (f32[64,128]{1,0:T(8,128)S(1)}, f32[64,128]{1,0:T(8,128)S(1)}, u32[]{:S(2)}, u32[]{:S(2)}) collective-permute-start(f32[64,128]{1,0:T(8,128)S(1)} %get-tuple-element.47), channel_id=1, source_target_pairs={{0,2},{2,0},{4,6},{6,4},{8,10},{10,8},{12,14},{14,12},{16,18},{18,... | collective-permute-start | bytes 98312 | tf_op jit(solution)/shard_map/ppermute | solution.py:736
  38.8 10.1 %collective-permute-start.6 = (f32[64,128]{1,0:T(8,128)S(1)}, f32[64,128]{1,0:T(8,128)S(1)}, u32[]{:S(2)}, u32[]{:S(2)}) collective-permute-start(f32[64,128]{1,0:T(8,128)S(1)} %get-tuple-element.48), channel_id=1, source_target_pairs={{0,254},{2,4},{4,2},{6,8},{8,6},{10,12},{12,10},{14,16},{16,14},{1... | collective-permute-start | bytes 98312 | tf_op jit(solution)/shard_map/ppermute | solution.py:735
  48.9 1.2 %copy-start.7 = (f32[3,512]{1,0:T(4,128)S(1)}, f32[3,512]{1,0:T(4,128)}, u32[]{:S(2)}) copy-start(f32[3,512]{1,0:T(4,128)} %vel_ref.1) | copy-start | bytes 18436
  48.9 1.2 %copy-start.8 = (s32[512,1]{0,1:T(1,128)S(1)}, s32[512,1]{0,1:T(1,128)}, u32[]{:S(2)}) copy-start(s32[512,1]{0,1:T(1,128)} %param.16) | copy-start | bytes 6148
  49.0 1.2 %copy-start.9 = (f32[512]{0:T(512)S(1)}, f32[512]{0:T(512)}, u32[]{:S(2)}) copy-start(f32[512]{0:T(512)} %param.20) | copy-start | bytes 6148

commit v6 on v5

--- a/solution.py
+++ b/solution.py
@@ -40,6 +40,7 @@
 FLAT = (0, 7, 8, 9, 10)
 CALM = (0, 7, 8, 9, 10, 11, 12, 13, 14, 15, 16, 17, 18)
 
+EARLY = 5
 VMEM_LIMIT = 48 * 1024 * 1024
 STREAM_FLOPS = 4_000_000_000
 FIRST_FLOPS = 3_500_000_000
@@ -593,10 +594,30 @@
     own_half[...] = 0.5 * mm(w_self_ref[...], own_ref[...])
 
 
+def potential_sums(cols, ks, own_ref, nbr_ref, bond_ref, w_rbf_ref, w_out_ref, table, own_half):
+    basis = w_rbf_ref.shape[0]
+    feats = own_ref.shape[0]
+    rbf_hi, rbf_lo = halves(0.5 * w_rbf_ref[...])
+    rbf_hi, rbf_lo = rbf_hi.astype(F32), rbf_lo.astype(F32)
+    rest = jnp.zeros((feats - 3 * basis, feats), F32)
+    rbf = jnp.concatenate([rbf_hi, rbf_lo, rbf_hi, rest], axis=0).T.astype(BF16)
+    w_out = jnp.broadcast_to(w_out_ref[...], (8, feats)).T[:, 0:1]
+    return message(
+        table,
+        own_half[:, cols],
+        rbf,
+        w_out,
+        [nbr_ref[k : k + 1, cols] for k in ks],
+        [[bond_ref[c, k : k + 1, cols] for c in range(3)] for k in ks],
+        RADIAL_REACH / (basis - 1),
+        basis,
+    )
+
+
 def potential_first_kernel(
+    near_ref,
+    own_ref,
     far_ref,
-    own_ref,
-    near_ref,
     nbr_ref,
     bond_ref,
     w_self_ref,
@@ -605,42 +626,29 @@
     w_out_ref,
     force_ref,
     new_ref,
+    part_force_ref,
+    part_ref,
     table,
     own_half,
 ):
     potential_table(near_ref, own_ref, far_ref, w_self_ref, w_nbr_ref, table, own_half)
-    potential_block(0, own_ref, nbr_ref, bond_ref, w_rbf_ref, w_out_ref, table, own_half, force_ref, new_ref)
-
-
-def potential_block(start, own_ref, nbr_ref, bond_ref, w_rbf_ref, w_out_ref, table_ref, half_ref, force_ref, new_ref):
-    block = force_ref.shape[1] - start
-    count, basis = nbr_ref.shape[0], w_rbf_ref.shape[0]
-    cols = slice(start, start + block)
-    feats = own_ref.shape[0]
-    rbf_hi, rbf_lo = halves(0.5 * w_rbf_ref[...])
-    rbf_hi, rbf_lo = rbf_hi.astype(F32), rbf_lo.astype(F32)
-    rest = jnp.zeros((feats - 3 * basis, feats), F32)
-    rbf = jnp.concatenate([rbf_hi, rbf_lo, rbf_hi, rest], axis=0).T.astype(BF16)
-    w_out = jnp.broadcast_to(w_out_ref[...], (8, feats)).T[:, 0:1]
-    total, force = message(
-        table_ref,
-        half_ref[:, cols],
-        rbf,
-        w_out,
-        [nbr_ref[k : k + 1, cols] for k in range(count)],
-        [[bond_ref[c, k : k + 1, cols] for c in range(3)] for k in range(count)],
-        RADIAL_REACH / (basis - 1),
-        basis,
-    )
+    atoms, count = own_ref.shape[1], nbr_ref.shape[0]
+    args = (own_ref, nbr_ref, bond_ref, w_rbf_ref, w_out_ref, table, own_half)
+    cols = slice(0, atoms // 2)
+    total, force = potential_sums(cols, range(count), *args)
     for c in range(3):
-        force_ref[c : c + 1, cols] = force[c]
-    new_ref[:, cols] = (own_ref[:, cols].astype(F32) + total * (1.0 / count)).astype(BF16)
+        force_ref[c : c + 1, :] = force[c]
+    new_ref[...] = (own_ref[:, cols].astype(F32) + total * (1.0 / count)).astype(BF16)
+    total, force = potential_sums(slice(atoms // 2, atoms), range(EARLY), *args)
+    for c in range(3):
+        part_force_ref[c : c + 1, :] = force[c]
+    part_ref[...] = total
 
 
 def potential_second_kernel(
+    near_ref,
+    own_ref,
     far_ref,
-    own_ref,
-    near_ref,
     nbr_ref,
     bond_ref,
     w_self_ref,
@@ -649,26 +657,31 @@
     w_out_ref,
     first_force_ref,
     first_new_ref,
+    part_force_ref,
+    part_ref,
     force_ref,
     new_ref,
     table,
     own_half,
 ):
-    half = first_new_ref.shape[1]
-    force_ref[:, :half] = first_force_ref[...]
-    new_ref[:, :half] = first_new_ref[...]
+    atoms, count = own_ref.shape[1], nbr_ref.shape[0]
+    cols = slice(atoms // 2, atoms)
+    force_ref[:, : atoms // 2] = first_force_ref[...]
+    new_ref[:, : atoms // 2] = first_new_ref[...]
     potential_table(near_ref, own_ref, far_ref, w_self_ref, w_nbr_ref, table, own_half)
-    potential_block(half, own_ref, nbr_ref, bond_ref, w_rbf_ref, w_out_ref, table, own_half, force_ref, new_ref)
-
-
-def potential(kernel, name, columns, flops, *args):
+    total, force = potential_sums(
+        cols, range(EARLY, count), own_ref, nbr_ref, bond_ref, w_rbf_ref, w_out_ref, table, own_half
+    )
+    for c in range(3):
+        force_ref[c : c + 1, cols] = part_force_ref[c : c + 1, :] + force[c]
+    new_ref[:, cols] = (own_ref[:, cols].astype(F32) + (part_ref[...] + total) * (1.0 / count)).astype(BF16)
+
+
+def potential(kernel, name, shapes, flops, *args):
     feats, atoms = args[1].shape
     return pl.pallas_call(
         kernel,
-        out_shape=(
-            jax.ShapeDtypeStruct((3, columns), F32),
-            jax.ShapeDtypeStruct((feats, columns), BF16),
-        ),
+        out_shape=tuple(jax.ShapeDtypeStruct(*shape) for shape in shapes),
         scratch_shapes=[
             pltpu.VMEM((3 * feats, atoms), BF16),
             pltpu.VMEM((feats, atoms), F32),
@@ -724,8 +737,12 @@
     calm, side = stream(rest)
     far = lax.ppermute(far, "fluid", link)
     near = lax.ppermute(near, "fluid", chip)
-    around = (far_features, features, near_features, nbrs, bonds, w_self, w_nbr, w_rbf, w_out)
-    first_pull, first_new = potential(potential_first_kernel, "potential_first", atoms // 2, FIRST_FLOPS, *around)
+    around = (near_features, features, far_features, nbrs, bonds, w_self, w_nbr, w_rbf, w_out)
+    feats, half = features.shape[0], atoms // 2
+    shapes = (((3, half), F32), ((feats, half), BF16), ((3, half), F32), ((feats, half), F32))
+    first_pull, first_new, part_pull, part = potential(
+        potential_first_kernel, "potential_first", shapes, FIRST_FLOPS, *around
+    )
     mail, first_pull, side = lax.optimization_barrier((mail, first_pull, side))
 
     reply, slot, wy_hi, wy_lo = look(mail.reshape(slabs, 128), vel)
@@ -735,8 +752,10 @@
     late_far = lax.ppermute(late_far, "fluid", link)
     late_near = lax.ppermute(late_near, "fluid", chip)
     first_pull, moved = lax.optimization_barrier((first_pull, moved))
+    shapes = (((3, atoms), F32), ((feats, atoms), BF16))
+    first = (first_pull, first_new, part_pull, part)
     pull, new_features = potential(
-        potential_second_kernel, "potential_second", atoms, SECOND_FLOPS, *around, first_pull, first_new
+        potential_second_kernel, "potential_second", shapes, SECOND_FLOPS, *around, *first
     )
     pops = gather(calm, moved, near, far, side, late_near, late_far)
     atom_force = finish(reply.reshape(slabs, 128), slab_row, rank, atom_vel, friction_row, pull)

time: 51.2 us -> 52.7 us (1.029)
  waiting for transfers between devices: 0.02 us -> 1.97 us
    ppermute x1, waiting for transfers between devices: 0.01 us -> 1.95 us  [body(): side = lax.ppermute(side, 'group', across)]
    ppermute x1, starting transfers between devices: 6.81 us -> 6.2 us  [body(): late_far = lax.ppermute(late_far, 'fluid', link)]
  transfers between devices with their start and end apart: 9 -> 9, of which waited for: 0 -> 1; matrix products, arithmetic and copies ran while one was open for 0% -> 0% of each run, Pallas kernels for 26% -> 25%
where the time goes in v6:
time: 52.7 us; the launch traced here: 52.5 us
  starting transfers between devices  35.6 us (68%)
  Pallas kernels  14 us (27%)
  waiting for transfers between devices  1.97 us (4%)
  between operations  0.91 us (2%)
    ppermute x1, starting transfers between devices, body(): far_features = lax.ppermute(sent, 'fluid', link)  8.87 us
    all_to_all x1, starting transfers between devices, body(): lax.all_to_all(reply.reshape(slabs, 1, 128), 'fluid', split_axis=0, conca...  7.05 us
    all_to_all x1, starting transfers between devices, body(): lax.all_to_all(mail.reshape(slabs, 1, 128), 'fluid', split_axis=0, concat...  6.2 us
    ppermute x1, starting transfers between devices, body(): late_far = lax.ppermute(late_far, 'fluid', link)  6.2 us
    ppermute x1, starting transfers between devices, body(): far = lax.ppermute(far, 'fluid', link)  6.2 us
    pallas_call x2, Pallas kernels, potential(): pl.pallas_call(kernel, out_shape=tuple((jax.ShapeDtypeStruct(*shape) for...  6 us
    ppermute x1, waiting for transfers between devices, body(): side = lax.ppermute(side, 'group', across)  1.95 us
    pallas_call x1, Pallas kernels, pack(): pl.pallas_call(pack_kernel, in_specs=[pl.BlockSpec(memory_space=pltpu.HBM...  1.92 us
  transfers between devices with their start and end apart: 9, of which 1 were waited for; matrix products, arithmetic and copies ran while one was open for 0% of the time, Pallas kernels for 25%

profile of v6, /device:TPU:16, one launch (start us, length us, event | category | flops | bytes accessed | tf_op | source)
XLA Modules:
  0.0 52.5 jit_solution(13222480695716201285)
XLA Ops:
  0.6 0.0 copy-start.1
  0.6 0.0 copy-start.3
  0.7 0.0 copy-start.2
  0.7 0.1 collective-permute-start
  0.8 8.9 %collective-permute-start.1 = (bf16[128,512]{1,0:T(8,128)(2,1)}, bf16[128,512]{1,0:T(8,128)(2,1)S(1)}, u32[]{:S(2)}, u32[]{:S(2)}) collective-permute-start(bf16[128,512]{1,0:T(8,128)(2,1)} %own_ref.3), channel_id=1, source_target_pairs={{0,254},{2,4},{4,2},{6,8},{8,6},{10,12},{12,10},{14,16},{16,14},{1... | collective-permute-start | bytes 393224 | tf_op jit(solution)/shard_map/ppermute | solution.py:723
  9.7 1.9 %pack.1 = (f32[128,128]{1,0:T(8,128)}, f32[1,512]{1,0:T(1,128)S(1)}) custom-call(s32[1,512]{1,0:T(1,128)} %bitcast.29, s32[1,512]{1,0:T(1,128)} %bitcast.37, f32[3,512]{1,0:T(4,128)} %frac_hbm.1, f32[3,512]{1,0:T(4,128)} %vel_ref.1, f32[1,512]{1,0:T(1,128)} %bitcast.31), custom_call_target="tpu_custom_call" | custom-call | flops 400000000 | bytes 4000000 | tf_op jit(solution)/shard_map/pack/pallas_call | solution.py:201
  11.6 6.2 %all-to-all-start = ((f32[128,1,128]{2,1,0:T(1,128)}), f32[128,1,128]{2,1,0:T(1,128)S(1)}, u32[]{:S(2)}, u32[]{:S(2)}) async-start(f32[128,1,128]{2,1,0:T(1,128)} %bitcast.9), calls=%async_computation | async-start | bytes 131072 | tf_op jit(solution)/shard_map/all_to_all | solution.py:724
  17.9 1.4 %relax.1 = (f32[13,128,128]{2,1,0:T(8,128)S(1)}, f32[6,128,128]{2,1,0:T(8,128)S(1)}, f32[3,128,128]{2,1,0:T(8,128)S(1)}, bf16[64,512]{1,0:T(8,128)(2,1)S(1)}, bf16[64,512]{1,0:T(8,128)(2,1)S(1)}) custom-call(f32[19]{0:T(128)S(1)} %copy-done.10, f32[19,128,128]{2,1,0:T(8,128)S(1)} %bitcast.17, bf16[128,512]{1,0:T(8,128)(2,1)S(1)} %copy-done.1, ...), custom_call_target="tpu_custom_call" | custom-call | flops 10000000 | bytes 6000000 | tf_op jit(solution)/shard_map/relax/pallas_call | solution.py:305
  19.4 0.1 collective-permute-start.2
  19.5 6.2 %collective-permute-start.3 = (bf16[64,512]{1,0:T(8,128)(2,1)S(1)}, bf16[64,512]{1,0:T(8,128)(2,1)S(1)}, u32[]{:S(2)}, u32[]{:S(2)}) collective-permute-start(bf16[64,512]{1,0:T(8,128)(2,1)S(1)} %get-tuple-element.45), channel_id=1, source_target_pairs={{0,254},{2,4},{4,2},{6,8},{8,6},{10,12},{12,10},{14,16},{16,14},{1... | collective-permute-start | bytes 196616 | tf_op jit(solution)/shard_map/ppermute | solution.py:738
  25.7 0.2 stream.1
  25.8 0.0 collective-permute-done.near_ref
  25.8 0.0 collective-permute-done.1.far_ref
  25.8 3.4 %potential_first.1 = (f32[3,256]{1,0:T(4,128)S(1)}, bf16[128,256]{1,0:T(8,128)(2,1)S(1)}, f32[3,256]{1,0:T(4,128)S(1)}, f32[128,256]{1,0:T(8,128)S(1)}) custom-call(bf16[128,512]{1,0:T(8,128)(2,1)S(1)} %collective-permute-done.near_ref, bf16[128,512]{1,0:T(8,128)(2,1)S(1)} %copy-done.1, bf16[128,512]{1,0:T(8,128)(2,1)S(1)} %collective-permute-done.1.far_ref, ...), custom_call_target="tpu_custom_call" | custom-call | flops 3500000000 | bytes 100000 | tf_op jit(solution)/shard_map/potential_first/pallas_call | solution.py:682
  29.2 0.0 all-to-all-done
  29.2 1.5 %look.1 = (f32[128,128]{1,0:T(8,128)}, f32[48,128]{1,0:T(8,128)S(1)}, bf16[128,1024]{1,0:T(8,128)(2,1)S(1)}, bf16[128,1024]{1,0:T(8,128)(2,1)S(1)}) custom-call(f32[128,128]{1,0:T(8,128)S(1)} %bitcast.22, f32[3,128,128]{2,1,0:T(8,128)S(1)} %get-tuple-element.39.vel_ref), custom_call_target="tpu_custom_call" | custom-call | flops 500000000 | bytes 1000000 | tf_op jit(solution)/shard_map/look/pallas_call | solution.py:376
  30.7 7.1 %all-to-all-start.1 = ((f32[128,1,128]{2,1,0:T(1,128)}), f32[128,1,128]{2,1,0:T(1,128)S(1)}, u32[]{:S(2)}, u32[]{:S(2)}) async-start(f32[128,1,128]{2,1,0:T(1,128)} %bitcast.13), calls=%async_computation.1 | async-start | bytes 131072 | tf_op jit(solution)/shard_map/all_to_all | solution.py:749
  37.8 0.0 collective-permute-done.2.near_ref
  37.8 0.0 collective-permute-done.3.far_ref
  37.8 1.0 %push.1 = (f32[6,128,128]{2,1,0:T(8,128)S(1)}, f32[64,128]{1,0:T(8,128)S(1)}, f32[64,128]{1,0:T(8,128)S(1)}, f32[24,128]{1,0:T(8,128)S(1)}) custom-call(f32[6,128,128]{2,1,0:T(8,128)S(1)} %get-tuple-element.37.axis_ref, f32[48,128]{1,0:T(8,128)S(1)} %get-tuple-element.40.slot_ref, bf16[128,1024]{1,0:T(8,128)(2,1)S(1)} %get-tuple-element.41.wy_hi, ...), custom_call_target="tpu_custom_call" | custom-call | flops 500000000 | bytes 1500000 | tf_op jit(solution)/shard_map/push/pallas_call | solution.py:471
  38.8 0.3 collective-permute-start.5
  39.1 6.2 %collective-permute-start.6 = (f32[64,128]{1,0:T(8,128)S(1)}, f32[64,128]{1,0:T(8,128)S(1)}, u32[]{:S(2)}, u32[]{:S(2)}) collective-permute-start(f32[64,128]{1,0:T(8,128)S(1)} %get-tuple-element.50), channel_id=1, source_target_pairs={{0,254},{2,4},{4,2},{6,8},{8,6},{10,12},{12,10},{14,16},{16,14},{1... | collective-permute-start | bytes 98312 | tf_op jit(solution)/shard_map/ppermute | solution.py:752
  45.3 0.6 %collective-permute-start.4 = (f32[24,128]{1,0:T(8,128)S(1)}, f32[24,128]{1,0:T(8,128)S(1)}, u32[]{:S(2)}, u32[]{:S(2)}) collective-permute-start(f32[24,128]{1,0:T(8,128)S(1)} %get-tuple-element.48), channel_id=1, source_target_pairs={{0,1},{1,0},{2,3},{3,2},{4,5},{5,4},{6,7},{7,6},{8,9},{9,8},{10,11... | collective-permute-start | bytes 36872 | tf_op jit(solution)/shard_map/ppermute | solution.py:751
  45.9 2.6 %potential_second.1 = (f32[3,512]{1,0:T(4,128)S(1)}, bf16[128,512]{1,0:T(8,128)(2,1)}) custom-call(bf16[128,512]{1,0:T(8,128)(2,1)S(1)} %collective-permute-done.near_ref, bf16[128,512]{1,0:T(8,128)(2,1)S(1)} %copy-done.1, bf16[128,512]{1,0:T(8,128)(2,1)S(1)} %collective-permute-done.1.far_ref, s32[16,512]{1,0:T(8,128)S(1)} %bitcast.25, ...), custom_call_target="tpu_custom_call" | custom-call | flops 500000000 | bytes 100000 | tf_op jit(solution)/shard_map/potential_second/pallas_call | solution.py:682
  48.5 2.0 %collective-permute-done.4.side_ref = f32[24,128]{1,0:T(8,128)S(1)} collective-permute-done((f32[24,128]{1,0:T(8,128)S(1)}, f32[24,128]{1,0:T(8,128)S(1)}, u32[]{:S(2)}, u32[]{:S(2)}) %collective-permute-start.4) | collective-permute-done | bytes 12320 | tf_op jit(solution)/shard_map/ppermute | solution.py:751
  50.5 0.0 collective-permute-done.5.late_near_ref
  50.5 0.0 collective-permute-done.6.late_far_ref
  50.5 0.0 copy-start.8
  50.5 0.0 copy-start.9
  50.5 1.1 %gather.1 = f32[19,128,128]{2,1,0:T(8,128)} custom-call(f32[13,128,128]{2,1,0:T(8,128)S(1)} %get-tuple-element.32.calm_ref, f32[6,128,128]{2,1,0:T(8,128)S(1)} %get-tuple-element.47.moved_ref, bf16[64,512]{1,0:T(8,128)(2,1)S(1)} %collective-permute-done.2.near_ref, bf16[64,512]{1,0:T(8,128)(2,1)S(1)} %collective-permute-done.3.far_ref, ...), custom_call_target="tpu_custom_call" | custom-call | flops 1000 | bytes 3000000 | tf_op jit(solution)/shard_map/gather/pallas_call | solution.py:531
  51.7 0.0 all-to-all-done.1
  51.7 0.8 %finish.1 = f32[3,512]{1,0:T(4,128)} custom-call(f32[128,128]{1,0:T(8,128)S(1)} %bitcast.18, s32[1,512]{1,0:T(1,128)S(1)} %bitcast.30, f32[1,512]{1,0:T(1,128)S(1)} %get-tuple-element.52.rank_ref, f32[3,512]{1,0:T(4,128)S(1)} %copy-done.7, f32[1,512]{1,0:T(1,128)S(1)} %bitcast.32, f32[3,512]{1,0:T(4,128)S(1)} %get-tuple-element.57.pull_ref), custom_call_target="tpu_custom_call" | custom-call | flops 20000000 | bytes 100000 | tf_op jit(solution)/shard_map/finish/pallas_call | solution.py:554
  (19 shorter events, 0.0 us)
Async XLA Ops:
  0.6 17.2 %copy-start.1 = (bf16[128,512]{1,0:T(8,128)(2,1)S(1)}, bf16[128,512]{1,0:T(8,128)(2,1)}, u32[]{:S(2)}) copy-start(bf16[128,512]{1,0:T(8,128)(2,1)} %own_ref.3) | copy-start | bytes 393220
  0.6 17.2 %copy-start.3 = (s32[512,16]{0,1:T(8,128)S(1)}, s32[512,16]{0,1:T(8,128)}, u32[]{:S(2)}) copy-start(s32[512,16]{0,1:T(8,128)} %param.22) | copy-start | bytes 98308
  0.7 17.2 %copy-start.2 = (f32[3,512,16]{1,2,0:T(8,128)S(1)}, f32[3,512,16]{1,2,0:T(8,128)}, u32[]{:S(2)}) copy-start(f32[3,512,16]{1,2,0:T(8,128)} %param.23) | copy-start | bytes 294916
  0.7 17.2 %copy-start.6 = (f32[128,16]{0,1:T(8,128)S(1)}, f32[128,16]{0,1:T(8,128)}, u32[]{:S(2)}) copy-start(f32[128,16]{0,1:T(8,128)} %param.26) | copy-start | bytes 24580
  0.7 17.2 %copy-start.11 = (f32[128]{0:T(128)S(1)}, f32[128]{0:T(128)}, u32[]{:S(2)}) copy-start(f32[128]{0:T(128)} %param.27) | copy-start | bytes 1540
  0.7 17.2 %copy-start = (f32[19,2,64,128]{3,2,1,0:T(8,128)S(1)}, f32[19,2,64,128]{3,2,1,0:T(8,128)}, u32[]{:S(2)}) copy-start(f32[19,2,64,128]{3,2,1,0:T(8,128)} %param.14) | copy-start | bytes 3735556
  0.7 17.2 %copy-start.10 = (f32[19]{0:T(128)S(1)}, f32[19]{0:T(128)}, u32[]{:S(2)}) copy-start(f32[19]{0:T(128)} %rates_ref.1) | copy-start | bytes 232
  0.7 17.2 %copy-start.4 = (bf16[128,128]{1,0:T(8,128)(2,1)S(1)}, bf16[128,128]{1,0:T(8,128)(2,1)}, u32[]{:S(2)}) copy-start(bf16[128,128]{1,0:T(8,128)(2,1)} %w_self_ref.3) | copy-start | bytes 98308
  0.7 17.2 %copy-start.5 = (bf16[128,128]{1,0:T(8,128)(2,1)S(1)}, bf16[128,128]{1,0:T(8,128)(2,1)}, u32[]{:S(2)}) copy-start(bf16[128,128]{1,0:T(8,128)(2,1)} %w_nbr_ref.3) | copy-start | bytes 98308
  0.7 25.1 %collective-permute-start = (bf16[128,512]{1,0:T(8,128)(2,1)}, bf16[128,512]{1,0:T(8,128)(2,1)S(1)}, u32[]{:S(2)}, u32[]{:S(2)}) collective-permute-start(bf16[128,512]{1,0:T(8,128)(2,1)} %own_ref.3), channel_id=1, source_target_pairs={{0,2},{2,0},{4,6},{6,4},{8,10},{10,8},{12,14},{14,12},{16,18},{18,... | collective-permute-start | bytes 393224 | tf_op jit(solution)/shard_map/ppermute | solution.py:722
  0.8 25.0 %collective-permute-start.1 = (bf16[128,512]{1,0:T(8,128)(2,1)}, bf16[128,512]{1,0:T(8,128)(2,1)S(1)}, u32[]{:S(2)}, u32[]{:S(2)}) collective-permute-start(bf16[128,512]{1,0:T(8,128)(2,1)} %own_ref.3), channel_id=1, source_target_pairs={{0,254},{2,4},{4,2},{6,8},{8,6},{10,12},{12,10},{14,16},{16,14},{1... | collective-permute-start | bytes 393224 | tf_op jit(solution)/shard_map/ppermute | solution.py:723
  11.6 17.6 %all-to-all-start = ((f32[128,1,128]{2,1,0:T(1,128)}), f32[128,1,128]{2,1,0:T(1,128)S(1)}, u32[]{:S(2)}, u32[]{:S(2)}) async-start(f32[128,1,128]{2,1,0:T(1,128)} %bitcast.9), calls=%async_computation | async-start | bytes 131072 | tf_op jit(solution)/shard_map/all_to_all | solution.py:724
  19.4 18.4 %collective-permute-start.2 = (bf16[64,512]{1,0:T(8,128)(2,1)S(1)}, bf16[64,512]{1,0:T(8,128)(2,1)S(1)}, u32[]{:S(2)}, u32[]{:S(2)}) collective-permute-start(bf16[64,512]{1,0:T(8,128)(2,1)S(1)} %get-tuple-element.44), channel_id=1, source_target_pairs={{0,2},{2,0},{4,6},{6,4},{8,10},{10,8},{12,14},{14,12},{16,18},{18,... | collective-permute-start | bytes 196616 | tf_op jit(solution)/shard_map/ppermute | solution.py:739
  19.5 18.3 %collective-permute-start.3 = (bf16[64,512]{1,0:T(8,128)(2,1)S(1)}, bf16[64,512]{1,0:T(8,128)(2,1)S(1)}, u32[]{:S(2)}, u32[]{:S(2)}) collective-permute-start(bf16[64,512]{1,0:T(8,128)(2,1)S(1)} %get-tuple-element.45), channel_id=1, source_target_pairs={{0,254},{2,4},{4,2},{6,8},{8,6},{10,12},{12,10},{14,16},{16,14},{1... | collective-permute-start | bytes 196616 | tf_op jit(solution)/shard_map/ppermute | solution.py:738
  30.7 20.9 %all-to-all-start.1 = ((f32[128,1,128]{2,1,0:T(1,128)}), f32[128,1,128]{2,1,0:T(1,128)S(1)}, u32[]{:S(2)}, u32[]{:S(2)}) async-start(f32[128,1,128]{2,1,0:T(1,128)} %bitcast.13), calls=%async_computation.1 | async-start | bytes 131072 | tf_op jit(solution)/shard_map/all_to_all | solution.py:749
  38.8 11.7 %collective-permute-start.5 = (f32[64,128]{1,0:T(8,128)S(1)}, f32[64,128]{1,0:T(8,128)S(1)}, u32[]{:S(2)}, u32[]{:S(2)}) collective-permute-start(f32[64,128]{1,0:T(8,128)S(1)} %get-tuple-element.49), channel_id=1, source_target_pairs={{0,2},{2,0},{4,6},{6,4},{8,10},{10,8},{12,14},{14,12},{16,18},{18,... | collective-permute-start | bytes 98312 | tf_op jit(solution)/shard_map/ppermute | solution.py:753
  39.1 11.4 %collective-permute-start.6 = (f32[64,128]{1,0:T(8,128)S(1)}, f32[64,128]{1,0:T(8,128)S(1)}, u32[]{:S(2)}, u32[]{:S(2)}) collective-permute-start(f32[64,128]{1,0:T(8,128)S(1)} %get-tuple-element.50), channel_id=1, source_target_pairs={{0,254},{2,4},{4,2},{6,8},{8,6},{10,12},{12,10},{14,16},{16,14},{1... | collective-permute-start | bytes 98312 | tf_op jit(solution)/shard_map/ppermute | solution.py:752
  45.3 5.2 %collective-permute-start.4 = (f32[24,128]{1,0:T(8,128)S(1)}, f32[24,128]{1,0:T(8,128)S(1)}, u32[]{:S(2)}, u32[]{:S(2)}) collective-permute-start(f32[24,128]{1,0:T(8,128)S(1)} %get-tuple-element.48), channel_id=1, source_target_pairs={{0,1},{1,0},{2,3},{3,2},{4,5},{5,4},{6,7},{7,6},{8,9},{9,8},{10,11... | collective-permute-start | bytes 36872 | tf_op jit(solution)/shard_map/ppermute | solution.py:751
  50.5 1.2 %copy-start.7 = (f32[3,512]{1,0:T(4,128)S(1)}, f32[3,512]{1,0:T(4,128)}, u32[]{:S(2)}) copy-start(f32[3,512]{1,0:T(4,128)} %vel_ref.1) | copy-start | bytes 18436
  50.5 1.2 %copy-start.8 = (s32[512,1]{0,1:T(1,128)S(1)}, s32[512,1]{0,1:T(1,128)}, u32[]{:S(2)}) copy-start(s32[512,1]{0,1:T(1,128)} %param.16) | copy-start | bytes 6148
  50.5 1.2 %copy-start.9 = (f32[512]{0:T(512)S(1)}, f32[512]{0:T(512)}, u32[]{:S(2)}) copy-start(f32[512]{0:T(512)} %param.20) | copy-start | bytes 6148
